TPU v7x, 256 devices: a whole 4x4x8 slice. The times are simulated.
256 devices in a mesh: lon: 32 (over z, y_hi, core), lat: 8 (over x, y_lo).
Axes of the slice: x: 4, y: 4 (y_hi: 2, y_lo: 2; y = y_hi * 2 + y_lo), z: 8, core: 2. Of those that a mesh axis runs over, the one named last changes fastest.
Arguments:
- heat_anomaly: float32 [8, 1536, 4096], P(None, 'lat', 'lon'), may hold values from -6 to 6
- saltiness_anomaly: float32 [8, 1536, 4096], P(None, 'lat', 'lon'), may hold values from -6 to 6
- zonal_current: float32 [8, 1536, 4096], P(None, 'lat', 'lon'), may hold values from -3 to 3
- meridional_current: float32 [8, 1536, 4096], P(None, 'lat', 'lon'), may hold values from -3 to 3
- free_elevation: float32 [1536, 4096], P('lat', 'lon'), may hold values from -3 to 3
- ocean_indicator: int32 [8, 1536, 4096], P(None, 'lat', 'lon'), may hold values from 0 to 1, as said below
- floor_layer_index: int32 [1536, 4096], P('lat', 'lon'), may hold values from 0 to 7, as said below
Outputs:
- temperature_next: float32 [8, 1536, 4096], P(None, 'lat', 'lon')
- salinity_next: float32 [8, 1536, 4096], P(None, 'lat', 'lon')
- zonal_next: float32 [8, 1536, 4096], P(None, 'lat', 'lon')
- meridional_next: float32 [8, 1536, 4096], P(None, 'lat', 'lon')
- height_next: float32 [1536, 4096], P('lat', 'lon')
Inputs may be any that keep to these rules, and one draw needn't show every extreme that they name: In each column with water the cells with ocean_indicator 1 are one run of levels, starting at level 0, 1 or 2 and ending at floor_layer_index; columns without water have ocean_indicator 0 at every level. `floor_layer_index`: the deepest wet level where the column holds water, 0 where it is dry.
All inputs are finite; a program needn't handle non-finite values.
Results may differ from a plain program's by a relative error of at most 0.00002.
Values sent between devices are 32-bit elements; how exact they have to be, the bound alone decides.
No kernel may reach another device: no remote copies, remote signals or barrier semaphores. Data moves between devices by JAX's collectives and lax.ppermute only.
A program may use at most 128 MiB of HBM per device.

v0:
```python
import jax
import jax.numpy as jnp
from jax import lax
from jax.sharding import PartitionSpec as P

time_step = 0.2
viscosity = 0.5
diffusivity = 0.3
press_scale = 0.25
gravity = 1.0
drag_coef = 1.0
coriolis_max = 0.5


def swapped(array, axis, distance):
    return lax.ppermute(array, axis, [(i, i ^ 1 << distance) for i in range(lax.axis_size(axis))])


def with_halo(array, sides, width, wrap):
    for axis, dim in sides:
        devices, length = (lax.axis_size(axis), array.shape[dim])
        up = [(i, (i + 1) % devices) for i in range(devices if wrap else devices - 1)]
        down = [(j, i) for i, j in up]
        last = lax.slice_in_dim(array, length - width, length, axis=dim)
        leading = lax.slice_in_dim(array, 0, width, axis=dim)
        before = lax.ppermute(last, axis, up)
        after = lax.ppermute(leading, axis, down)
        array = jnp.concatenate([before, array, after], axis=dim)
    return array


def offset_view(field, shift_row, shift_col):
    elevation_grid = field.shape[1] - 4
    breadth = field.shape[2] - 4
    return field[
        :, 2 + shift_row : 2 + shift_row + elevation_grid, 2 + shift_col : 2 + shift_col + breadth
    ]


def laplace(field, wet_ext):
    centre = offset_view(field, 0, 0)
    wet_centre = offset_view(wet_ext, 0, 0)
    total = jnp.zeros_like(centre)
    for shift_row, shift_col in ((0, 1), (0, -1), (1, 0), (-1, 0)):
        total = total + wet_centre * offset_view(wet_ext, shift_row, shift_col) * (
            offset_view(field, shift_row, shift_col) - centre
        )
    return total


def coriolis_rows(first_row, count, total):
    row_index = first_row + jnp.arange(count, dtype=jnp.int32)
    return coriolis_max * (2.0 * (row_index.astype(jnp.float32) + 0.5) / total - 1.0)


def momentum(extended, coriolis, bottom):
    layer_pile = (extended.shape[0] - 1) // 5
    thermal = extended[:layer_pile]
    saline = extended[layer_pile : 2 * layer_pile]
    eastward = extended[2 * layer_pile : 3 * layer_pile]
    northward = extended[3 * layer_pile : 4 * layer_pile]
    wet_ext = extended[4 * layer_pile : 5 * layer_pile]
    surface = extended[5 * layer_pile : 5 * layer_pile + 1]
    density = -0.2 * thermal + 0.8 * saline - 0.05 * thermal * thermal + 0.02 * thermal * saline
    pressure = press_scale * (jnp.cumsum(density, axis=0) - 0.5 * density) + gravity * surface
    slope_x = 0.5 * (offset_view(pressure, 0, 1) - offset_view(pressure, 0, -1))
    slope_y = 0.5 * (offset_view(pressure, 1, 0) - offset_view(pressure, -1, 0))
    wet_centre = offset_view(wet_ext, 0, 0)
    east_now = offset_view(eastward, 0, 0)
    north_now = offset_view(northward, 0, 0)
    spin = coriolis[None, :, None]
    east_trial = east_now + time_step * (
        spin * north_now - slope_x + viscosity * laplace(eastward, wet_ext)
    )
    north_trial = north_now + time_step * (
        -spin * east_now - slope_y + viscosity * laplace(northward, wet_ext)
    )
    level_index = lax.broadcasted_iota(jnp.int32, east_trial.shape, 0)
    speed = jnp.sqrt(east_trial * east_trial + north_trial * north_trial)
    damping = jnp.where(level_index == bottom[None], 1.0 / (1.0 + drag_coef * speed), 1.0)
    return (wet_centre * east_trial * damping, wet_centre * north_trial * damping)


def faces_x(field):
    elevation_grid = field.shape[1] - 4
    breadth = field.shape[2] - 4
    band = field[:, 2 : 2 + elevation_grid, :]
    return (
        7.0 * (band[:, :, 1 : breadth + 2] + band[:, :, 2 : breadth + 3])
        - (band[:, :, 0 : breadth + 1] + band[:, :, 3 : breadth + 4])
    ) / 12.0


def faces_y(field):
    elevation_grid = field.shape[1] - 4
    breadth = field.shape[2] - 4
    band = field[:, :, 2 : 2 + breadth]
    return (
        7.0 * (band[:, 1 : elevation_grid + 2, :] + band[:, 2 : elevation_grid + 3, :])
        - (band[:, 0 : elevation_grid + 1, :] + band[:, 3 : elevation_grid + 4, :])
    ) / 12.0


def normal_x(velocity, wet_ext):
    elevation_grid = velocity.shape[1] - 4
    breadth = velocity.shape[2] - 4
    band = velocity[:, 2 : 2 + elevation_grid, :]
    wetband = wet_ext[:, 2 : 2 + elevation_grid, :]
    return (
        0.5
        * (band[:, :, 1 : breadth + 2] + band[:, :, 2 : breadth + 3])
        * wetband[:, :, 1 : breadth + 2]
        * wetband[:, :, 2 : breadth + 3]
    )


def normal_y(velocity, wet_ext):
    elevation_grid = velocity.shape[1] - 4
    breadth = velocity.shape[2] - 4
    band = velocity[:, :, 2 : 2 + breadth]
    wetband = wet_ext[:, :, 2 : 2 + breadth]
    return (
        0.5
        * (band[:, 1 : elevation_grid + 2, :] + band[:, 2 : elevation_grid + 3, :])
        * wetband[:, 1 : elevation_grid + 2, :]
        * wetband[:, 2 : elevation_grid + 3, :]
    )


def tracers(extended, moved):
    layer_pile = (extended.shape[0] - 1) // 5
    wet_ext = extended[4 * layer_pile : 5 * layer_pile]
    trans_x = normal_x(moved[:layer_pile], wet_ext)
    trans_y = normal_y(moved[layer_pile:], wet_ext)
    wet_centre = offset_view(wet_ext, 0, 0)

    def advance(field):
        flux_x = trans_x * faces_x(field)
        flux_y = trans_y * faces_y(field)
        spread = flux_x[:, :, 1:] - flux_x[:, :, :-1] + (flux_y[:, 1:, :] - flux_y[:, :-1, :])
        return wet_centre * (
            offset_view(field, 0, 0)
            - time_step * spread
            + time_step * diffusivity * laplace(field, wet_ext)
        )

    thermal_next = advance(extended[:layer_pile])
    saline_next = advance(extended[layer_pile : 2 * layer_pile])
    inflow = jnp.sum(
        trans_x[:, :, 1:] - trans_x[:, :, :-1] + (trans_y[:, 1:, :] - trans_y[:, :-1, :]), axis=0
    )
    height_next = (
        offset_view(extended[5 * layer_pile : 5 * layer_pile + 1], 0, 0)[0]
        - time_step / layer_pile * inflow
    )
    return (thermal_next, saline_next, height_next)


def mirror(fold_edge):
    for bit_number in range(lax.axis_size("lon").bit_length() - 1):
        fold_edge = swapped(fold_edge, "lon", bit_number)
    return fold_edge


def refold(padded, signs):
    elevation_grid = padded.shape[1]
    fold_edge = (
        padded[:, elevation_grid - 4 : elevation_grid - 2, :][:, ::-1, ::-1] * signs[:, None, None]
    )
    received = mirror(fold_edge)
    northmost = lax.axis_index("lat") == lax.axis_size("lat") - 1
    ghost_rows = jnp.where(northmost, received, padded[:, elevation_grid - 2 :, :])
    return jnp.concatenate([padded[:, : elevation_grid - 2, :], ghost_rows], axis=1)


def extend(joined_tracer_grids, signs):
    padded = with_halo(joined_tracer_grids, (("lat", 1),), 2, False)
    padded = refold(padded, signs)
    return with_halo(padded, (("lon", 2),), 2, True)


def on_device(
    heat_anomaly,
    saltiness_anomaly,
    zonal_current,
    meridional_current,
    free_elevation,
    ocean_indicator,
    floor_layer_index,
):
    layer_pile = heat_anomaly.shape[0]
    elevation_grid = heat_anomaly.shape[1]
    holds_water = ocean_indicator.astype(jnp.float32)
    joined_tracer_grids = jnp.concatenate(
        [
            heat_anomaly,
            saltiness_anomaly,
            zonal_current,
            meridional_current,
            holds_water,
            free_elevation[None],
        ],
        axis=0,
    )
    signs = jnp.concatenate(
        [
            jnp.ones(2 * layer_pile, jnp.float32),
            -jnp.ones(2 * layer_pile, jnp.float32),
            jnp.ones(layer_pile + 1, jnp.float32),
        ]
    )
    extended = extend(joined_tracer_grids, signs)
    first_row = lax.axis_index("lat") * elevation_grid
    coriolis = coriolis_rows(first_row, elevation_grid, elevation_grid * lax.axis_size("lat"))
    east_next, north_next = momentum(extended, coriolis, floor_layer_index)
    moved = extend(
        jnp.concatenate([east_next, north_next], axis=0), -jnp.ones(2 * layer_pile, jnp.float32)
    )
    thermal_next, saline_next, height_next = tracers(extended, moved)
    return (thermal_next, saline_next, east_next, north_next, height_next)


def solution(mesh):
    return jax.shard_map(
        on_device,
        mesh=mesh,
        in_specs=(
            P(None, "lat", "lon"),
            P(None, "lat", "lon"),
            P(None, "lat", "lon"),
            P(None, "lat", "lon"),
            P("lat", "lon"),
            P(None, "lat", "lon"),
            P("lat", "lon"),
        ),
        out_specs=(
            P(None, "lat", "lon"),
            P(None, "lat", "lon"),
            P(None, "lat", "lon"),
            P(None, "lat", "lon"),
            P("lat", "lon"),
        ),
        check_vma=False,
    )
```

profile of v0, /device:TPU:14, one launch (start us, length us, event | category | flops | bytes accessed | tf_op | source)
XLA Modules:
  0.0 156.7 jit_solution(2005157237059822716)
XLA Ops:
  0.7 1.3 constant_dynamic-update-slice_fusion.3
  4.2 2.0 %copy-done = f32[41,192,128]{2,1,0:T(8,128)} copy-done((f32[41,192,128]{2,1,0:T(8,128)}, f32[41,192,128]{2,1,0:T(8,128)S(1)}, u32[]{:S(2)}) %copy-start) | copy-done | bytes 4030488
  6.6 1.2 collective-permute-done.1
  7.8 2.3 %collective-permute-start.2 = (f32[41,2,128]{2,1,0:T(2,128)S(1)}, f32[41,2,128]{2,1,0:T(2,128)S(1)}, u32[]{:S(2)}, u32[]{:S(2)}) collective-permute-start(f32[41,2,128]{2,1,0:T(2,128)S(1)} %collective-permute-done.1), channel_id=1, source_target_pairs={{0,16},{8,24},{16,0},{24,8},{32,48},{40,56},{48,32},{56,40},{64,80... | collective-permute-start | bytes 125960 | tf_op jit(solution)/shard_map/ppermute | solution.py:16
  10.1 3.2 %collective-permute-done.2 = f32[41,2,128]{2,1,0:T(2,128)S(1)} collective-permute-done((f32[41,2,128]{2,1,0:T(2,128)S(1)}, f32[41,2,128]{2,1,0:T(2,128)S(1)}, u32[]{:S(2)}, u32[]{:S(2)}) %collective-permute-start.2) | collective-permute-done | bytes 42016 | tf_op jit(solution)/shard_map/ppermute | solution.py:16
  13.3 1.9 %collective-permute-start.3 = (f32[41,2,128]{2,1,0:T(2,128)S(1)}, f32[41,2,128]{2,1,0:T(2,128)S(1)}, u32[]{:S(2)}, u32[]{:S(2)}) collective-permute-start(f32[41,2,128]{2,1,0:T(2,128)S(1)} %collective-permute-done.2), channel_id=1, source_target_pairs={{0,32},{8,40},{16,48},{24,56},{32,0},{40,8},{48,16},{56,24},{64,96... | collective-permute-start | bytes 125960 | tf_op jit(solution)/shard_map/ppermute | solution.py:16
  15.3 2.1 %collective-permute-done.3 = f32[41,2,128]{2,1,0:T(2,128)S(1)} collective-permute-done((f32[41,2,128]{2,1,0:T(2,128)S(1)}, f32[41,2,128]{2,1,0:T(2,128)S(1)}, u32[]{:S(2)}, u32[]{:S(2)}) %collective-permute-start.3) | collective-permute-done | bytes 42016 | tf_op jit(solution)/shard_map/ppermute | solution.py:16
  17.3 3.3 %collective-permute-start.4 = (f32[41,2,128]{2,1,0:T(2,128)S(1)}, f32[41,2,128]{2,1,0:T(2,128)S(1)}, u32[]{:S(2)}, u32[]{:S(2)}) collective-permute-start(f32[41,2,128]{2,1,0:T(2,128)S(1)} %collective-permute-done.3), channel_id=1, source_target_pairs={{0,64},{8,72},{16,80},{24,88},{32,96},{40,104},{48,112},{56,120},{... | collective-permute-start | bytes 125960 | tf_op jit(solution)/shard_map/ppermute | solution.py:16
  20.6 2.3 %collective-permute-start.6 = (f32[41,2,128]{2,1,0:T(2,128)S(1)}, f32[41,2,128]{2,1,0:T(2,128)S(1)}, u32[]{:S(2)}, u32[]{:S(2)}) collective-permute-start(f32[41,2,128]{2,1,0:T(2,128)S(1)} %get-tuple-element.36), channel_id=1, source_target_pairs={{1,0},{2,1},{3,2},{4,3},{5,4},{6,5},{7,6},{9,8},{10,9},{11,10},{12... | collective-permute-start | bytes 125960 | tf_op jit(solution)/shard_map/ppermute | solution.py:27
  23.0 6.6 %collective-permute-start.5 = (f32[41,2,128]{2,1,0:T(2,128)S(1)}, f32[41,2,128]{2,1,0:T(2,128)S(1)}, u32[]{:S(2)}, u32[]{:S(2)}) collective-permute-start(f32[41,2,128]{2,1,0:T(2,128)S(1)} %collective-permute-done.4), channel_id=1, source_target_pairs={{0,128},{8,136},{16,144},{24,152},{32,160},{40,168},{48,176},{56,1... | collective-permute-start | bytes 125960 | tf_op jit(solution)/shard_map/ppermute | solution.py:16
  29.6 1.3 collective-permute-start
  30.9 1.1 collective-permute-done.5
  32.0 3.4 %collective-permute-done = f32[41,2,128]{2,1,0:T(2,128)S(1)} collective-permute-done((f32[41,2,128]{2,1,0:T(2,128)S(1)}, f32[41,2,128]{2,1,0:T(2,128)S(1)}, u32[]{:S(2)}, u32[]{:S(2)}) %collective-permute-start) | collective-permute-done | bytes 42016 | tf_op jit(solution)/shard_map/ppermute | solution.py:26
  35.4 2.5 %pad_maximum_fusion.1 = f32[41,196,128]{2,1,0:T(8,128)S(1)} fusion(f32[41,2,128]{2,1,0:T(2,128)S(1)} %broadcast_select_fusion, f32[41,192,128]{2,1,0:T(8,128)} %copy-done, f32[41,2,128]{2,1,0:T(2,128)S(1)} %collective-permute-done), kind=kLoop, calls=%fused_computation.20 | loop fusion | flops 2057216 | bytes 8228864 | tf_op jit(solution)/shard_map/concatenate | solution.py:173
  37.9 4.7 %fusion.115 = (f32[41,196,2]{2,1,0:T(8,128)}, f32[41,196,2]{2,1,0:T(8,128)}) fusion(f32[41,196,128]{2,1,0:T(8,128)S(1)} %pad_maximum_fusion.1), kind=kLoop, calls=%fused_computation.218 | loop fusion | bytes 257152 | tf_op jit(solution)/shard_map/slice | solution.py:25
  42.6 3.5 %copy.147 = f32[41,196,2]{1,0,2:T(8,128)S(1)} copy(f32[41,196,2]{2,1,0:T(8,128)} %get-tuple-element.33) | data formatting | bytes 128576 | tf_op jit(solution)/shard_map/slice | solution.py:24
  46.2 3.5 %copy.148 = f32[41,196,2]{1,0,2:T(8,128)S(1)} copy(f32[41,196,2]{2,1,0:T(8,128)} %get-tuple-element.32) | data formatting | bytes 128576 | tf_op jit(solution)/shard_map/slice | solution.py:25
  49.7 5.6 %collective-permute-start.8 = (f32[41,196,2]{1,0,2:T(8,128)S(1)}, f32[41,196,2]{1,0,2:T(8,128)S(1)}, u32[]{:S(2)}, u32[]{:S(2)}) collective-permute-start(f32[41,196,2]{1,0,2:T(8,128)S(1)} %copy.148), channel_id=1, source_target_pairs={{8,0},{16,8},{24,16},{32,24},{40,32},{48,40},{56,48},{64,56},{72,6... | collective-permute-start | bytes 192872 | tf_op jit(solution)/shard_map/ppermute | solution.py:27
  55.3 2.9 %copy.149 = f32[41,196,2]{2,1,0:T(8,128)} copy(f32[41,196,2]{1,0,2:T(8,128)S(1)} %collective-permute-done.7) | data formatting | bytes 128576 | tf_op jit(solution)/shard_map/ppermute | solution.py:26
  58.2 2.8 %copy.150 = f32[41,196,2]{2,1,0:T(8,128)} copy(f32[41,196,2]{1,0,2:T(8,128)S(1)} %collective-permute-done.8) | data formatting | bytes 128576 | tf_op jit(solution)/shard_map/ppermute | solution.py:27
  61.0 1.3 fusion.110
  63.3 1.3 slice-done.1
  64.6 1.2 copy-done.4
  65.8 2.7 %multiply_add_fusion = f32[8,196,132]{2,1,0:T(8,128)S(1)} fusion(f32[196,132]{1,0:T(8,128)S(1)} %fusion.110, f32[41,196,2]{2,1,0:T(8,128)S(1)} %copy-done.4, f32[41,2,128]{2,1,0:T(2,128)S(1)} %broadcast_select_fusion, f32[41,192,128]{2,1,0:T(8,128)S(1)} %copy-done.1, f32[41,2,128]{2,1,0:T(2,128)S(1)} %collective-permute-done, f32[41,196,2]{2,1,0:T(8,128)S(1)} %bitcast.5), kind=kOutput, calls=%fused_computation.45 | output fusion | flops 9313920 | bytes 5174400 | tf_op jit(solution)/shard_map/jit(cumsum)/reduce_window_sum | solution.py:65
  68.5 5.3 %multiply_multiply_fusion.2 = (f32[8,192,128]{2,1,0:T(8,128)S(1)}, f32[8,192,128]{2,1,0:T(8,128)S(1)}, f32[8,192,128]{2,1,0:T(8,128)S(1)}) fusion(s32[8,192,128]{2,1,0:T(8,128)S(1)} %copy-done.5, s32[192,128]{1,0:T(8,128)S(1)} %copy-done.14, f32[8,192,128]{2,1,0:T(8,128)S(1)} %copy-done.10, f32[41,192,128]{2,1,0:T(8,128)S(1)} %copy-done.1, ...), kind=kLoop, calls=%fused_computation.197 | loop fusion | flops 15728640 | bytes 12207168 | tf_op jit(solution)/shard_map/mul | solution.py:81
  74.6 1.2 collective-permute-done.10
  75.7 1.8 %collective-permute-start.11 = (f32[16,2,128]{2,0,1:T(8,128)S(1)}, f32[16,2,128]{2,0,1:T(8,128)S(1)}, u32[]{:S(2)}, u32[]{:S(2)}) collective-permute-start(f32[16,2,128]{2,0,1:T(8,128)S(1)} %collective-permute-done.10), channel_id=1, source_target_pairs={{0,16},{8,24},{16,0},{24,8},{32,48},{40,56},{48,32},{56,40},{64,80... | collective-permute-start | bytes 49160 | tf_op jit(solution)/shard_map/ppermute | solution.py:16
  77.5 3.4 %collective-permute-done.11 = f32[16,2,128]{2,0,1:T(8,128)S(1)} collective-permute-done((f32[16,2,128]{2,0,1:T(8,128)S(1)}, f32[16,2,128]{2,0,1:T(8,128)S(1)}, u32[]{:S(2)}, u32[]{:S(2)}) %collective-permute-start.11) | collective-permute-done | bytes 16416 | tf_op jit(solution)/shard_map/ppermute | solution.py:16
  81.2 3.5 %collective-permute-done.12 = f32[16,2,128]{2,0,1:T(8,128)S(1)} collective-permute-done((f32[16,2,128]{2,0,1:T(8,128)S(1)}, f32[16,2,128]{2,0,1:T(8,128)S(1)}, u32[]{:S(2)}, u32[]{:S(2)}) %collective-permute-start.12) | collective-permute-done | bytes 16416 | tf_op jit(solution)/shard_map/ppermute | solution.py:16
  84.7 1.0 collective-permute-start.13
  85.9 3.9 %collective-permute-start.15 = (f32[16,2,128]{2,0,1:T(8,128)S(1)}, f32[16,2,128]{2,0,1:T(8,128)S(1)}, u32[]{:S(2)}, u32[]{:S(2)}) collective-permute-start(f32[16,2,128]{2,0,1:T(8,128)S(1)} %copy.158), channel_id=1, source_target_pairs={{1,0},{2,1},{3,2},{4,3},{5,4},{6,5},{7,6},{9,8},{10,9},{11,10},{12... | collective-permute-start | bytes 49160 | tf_op jit(solution)/shard_map/ppermute | solution.py:27
  89.8 1.3 collective-permute-start.9
  91.1 2.3 %collective-permute-start.14 = (f32[16,2,128]{2,0,1:T(8,128)S(1)}, f32[16,2,128]{2,0,1:T(8,128)S(1)}, u32[]{:S(2)}, u32[]{:S(2)}) collective-permute-start(f32[16,2,128]{2,0,1:T(8,128)S(1)} %collective-permute-done.13), channel_id=1, source_target_pairs={{0,128},{8,136},{16,144},{24,152},{32,160},{40,168},{48,176},{56,1... | collective-permute-start | bytes 49160 | tf_op jit(solution)/shard_map/ppermute | solution.py:16
  93.4 13.1 %maximum_maximum_fusion = (f32[41,196,130]{2,1,0:T(8,128)}, f32[41,196,130]{2,1,0:T(8,128)}) fusion(f32[41,2,128]{2,1,0:T(2,128)S(1)} %broadcast_select_fusion, f32[41,192,128]{2,1,0:T(8,128)} %copy-done, f32[41,2,128]{2,1,0:T(2,128)S(1)} %collective-permute-done, f32[41,196,2]{2,1,0:T(8,128)} %copy.149, f32[41,196,2]{2,1,0:T(8,128)} %copy.150), kind=kLoop, calls=%fused_computation.19 | loop fusion | flops 6268080 | bytes 12600448 | tf_op jit(solution)/shard_map/concatenate | solution.py:28
  106.7 2.2 %fusion.117 = (f32[16,196,2]{2,1,0:T(8,128)}, f32[16,196,2]{2,1,0:T(8,128)}) fusion(f32[16,196,128]{2,1,0:T(8,128)S(1)} %pad_maximum_fusion.4), kind=kLoop, calls=%fused_computation.220 | loop fusion | bytes 100352 | tf_op jit(solution)/shard_map/slice | solution.py:24
  108.9 2.0 %copy.162 = f32[16,196,2]{1,0,2:T(8,128)S(1)} copy(f32[16,196,2]{2,1,0:T(8,128)} %get-tuple-element.38) | data formatting | bytes 50176 | tf_op jit(solution)/shard_map/slice | solution.py:24
  111.2 2.0 %copy.164 = f32[16,196,2]{1,0,2:T(8,128)S(1)} copy(f32[16,196,2]{2,1,0:T(8,128)} %get-tuple-element.39) | data formatting | bytes 50176 | tf_op jit(solution)/shard_map/slice | solution.py:25
  113.3 5.4 %collective-permute-start.17 = (f32[16,196,2]{1,0,2:T(8,128)S(1)}, f32[16,196,2]{1,0,2:T(8,128)}, u32[]{:S(2)}, u32[]{:S(2)}) collective-permute-start(f32[16,196,2]{1,0,2:T(8,128)S(1)} %copy.164), channel_id=1, source_target_pairs={{8,0},{16,8},{24,16},{32,24},{40,32},{48,40},{56,48},{64,56},{72,6... | collective-permute-start | bytes 75272 | tf_op jit(solution)/shard_map/ppermute | solution.py:27
  118.7 4.0 %fusion.16 = (f32[8,193,128]{2,1,0:T(8,128)}, f32[8,193,128]{2,1,0:T(8,128)S(1)}) fusion(f32[41,192,128]{2,1,0:T(8,128)} %copy-done, f32[41,2,128]{2,1,0:T(2,128)S(1)} %collective-permute-done, f32[41,2,128]{2,1,0:T(2,128)S(1)} %broadcast_select_fusion, f32[16,2,128]{2,1,0:T(2,128)S(1)} %copy_select_fusion, f32[8,192,128]{2,1,0:T(8,128)S(1)} %multiply_multiply_fusion.1, ...), kind=kLoop, calls=%fused_computation.74 | loop fusion | flops 3952640 | bytes 7301120 | tf_op jit(solution)/shard_map/mul | solution.py:139
  122.7 1.3 fusion.25
  124.0 1.7 %copy.163 = f32[16,196,2]{2,1,0:T(8,128)} copy(f32[16,196,2]{1,0,2:T(8,128)S(1)} %collective-permute-done.16) | data formatting | bytes 50176 | tf_op jit(solution)/shard_map/ppermute | solution.py:26
  125.7 2.5 %copy.165 = f32[16,196,2]{2,1,0:T(8,128)} copy(f32[16,196,2]{1,0,2:T(8,128)} %collective-permute-done.17) | data formatting | bytes 50176 | tf_op jit(solution)/shard_map/ppermute | solution.py:27
  128.2 7.6 %fusion.4 = (f32[8,192,129]{2,1,0:T(8,128)}, f32[8,192,129]{2,1,0:T(8,128)S(1)}) fusion(f32[41,196,130]{2,1,0:T(8,128)} %get-tuple-element.35, f32[41,196,130]{2,1,0:T(8,128)} %get-tuple-element.34, f32[16,196,2]{2,1,0:T(8,128)} %copy.165, f32[16,2,128]{2,1,0:T(2,128)S(1)} %copy_select_fusion, f32[8,192,128]{2,1,0:T(8,128)S(1)} %multiply_multiply_fusion.1, ...), kind=kLoop, calls=%fused_computation.49 | loop fusion | flops 3566592 | bytes 7996416 | tf_op jit(solution)/shard_map/mul | solution.py:138
  136.7 4.0 %fusion.8 = f32[8,192,129]{2,1,0:T(8,128)S(1)} fusion(f32[8,192,129]{2,1,0:T(8,128)S(1)} %get-tuple-element.26, f32[41,196,130]{2,1,0:T(8,128)} %get-tuple-element.35, f32[41,196,130]{2,1,0:T(8,128)} %get-tuple-element.34), kind=kLoop, calls=%fused_computation.55 | loop fusion | flops 1188864 | bytes 4755456 | tf_op jit(solution)/shard_map/mul | solution.py:138
  140.7 1.1 copy.171
  142.5 1.6 %copy.169 = f32[192,128]{1,0:T(8,128)} copy(f32[192,128]{0,1:T(8,128)} %multiply_subtract_fusion) | data formatting | bytes 196608
  144.1 7.3 %fusion.84 = f32[8,192,128]{2,1,0:T(8,128)} fusion(f32[8,192,128]{2,1,0:T(8,128)} %param.8, f32[41,192,128]{2,1,0:T(8,128)} %copy-done, f32[41,2,128]{2,1,0:T(2,128)S(1)} %collective-permute-done, f32[41,2,128]{2,1,0:T(2,128)S(1)} %broadcast_select_fusion, f32[41,196,2]{2,1,0:T(8,128)} %copy.149, f32[41,196,2]{2,1,0:T(8,128)} %copy.150, ...), kind=kLoop, calls=%fused_computation.149 | loop fusion | flops 7864320 | bytes 9748032 | tf_op jit(solution)/shard_map/mul | solution.py:141
  151.9 4.8 %fusion.62 = f32[8,192,128]{2,1,0:T(8,128)} fusion(f32[8,192,128]{2,1,0:T(8,128)S(1)} %copy-done.13, f32[41,192,128]{2,1,0:T(8,128)S(1)} %copy-done.3, f32[41,2,128]{2,1,0:T(2,128)S(1)} %collective-permute-done, f32[41,2,128]{2,1,0:T(2,128)S(1)} %broadcast_select_fusion, f32[41,196,2]{2,1,0:T(8,128)S(1)} %bitcast.7, f32[41,196,2]{2,1,0:T(8,128)} %copy.150, ...), kind=kLoop, calls=%fused_computation.124 | loop fusion | flops 7864320 | bytes 9748032 | tf_op jit(solution)/shard_map/mul | solution.py:141
  (79 shorter events, 7.2 us)
Async XLA Ops:
  0.6 1.4 copy-start.12
  0.6 1.6 %copy-start.10 = (f32[8,192,128]{2,1,0:T(8,128)S(1)}, f32[8,192,128]{2,1,0:T(8,128)}, u32[]{:S(2)}) copy-start(f32[8,192,128]{2,1,0:T(8,128)} %param.9) | copy-start | bytes 2359300
  2.0 1.2 copy-start.11
  2.2 1.2 copy-start.5
  3.2 0.9 copy-start.15
  3.2 3.2 %copy-start.16 = (f32[41]{0:T(128)S(1)}, f32[41]{0:T(128)}, u32[]{:S(2)}) copy-start(f32[41]{0:T(128)} %constant.25.clone.1) | copy-start | bytes 496
  4.2 2.0 %copy-start = (f32[41,192,128]{2,1,0:T(8,128)}, f32[41,192,128]{2,1,0:T(8,128)S(1)}, u32[]{:S(2)}) copy-start(f32[41,192,128]{2,1,0:T(8,128)S(1)} %bitcast_dynamic-update-slice_fusion) | copy-start | bytes 12091396
  6.5 1.3 collective-permute-start.1
  7.8 5.5 %collective-permute-start.2 = (f32[41,2,128]{2,1,0:T(2,128)S(1)}, f32[41,2,128]{2,1,0:T(2,128)S(1)}, u32[]{:S(2)}, u32[]{:S(2)}) collective-permute-start(f32[41,2,128]{2,1,0:T(2,128)S(1)} %collective-permute-done.1), channel_id=1, source_target_pairs={{0,16},{8,24},{16,0},{24,8},{32,48},{40,56},{48,32},{56,40},{64,80... | collective-permute-start | bytes 125960 | tf_op jit(solution)/shard_map/ppermute | solution.py:16
  13.3 4.0 %collective-permute-start.3 = (f32[41,2,128]{2,1,0:T(2,128)S(1)}, f32[41,2,128]{2,1,0:T(2,128)S(1)}, u32[]{:S(2)}, u32[]{:S(2)}) collective-permute-start(f32[41,2,128]{2,1,0:T(2,128)S(1)} %collective-permute-done.2), channel_id=1, source_target_pairs={{0,32},{8,40},{16,48},{24,56},{32,0},{40,8},{48,16},{56,24},{64,96... | collective-permute-start | bytes 125960 | tf_op jit(solution)/shard_map/ppermute | solution.py:16
  17.3 5.6 %collective-permute-start.4 = (f32[41,2,128]{2,1,0:T(2,128)S(1)}, f32[41,2,128]{2,1,0:T(2,128)S(1)}, u32[]{:S(2)}, u32[]{:S(2)}) collective-permute-start(f32[41,2,128]{2,1,0:T(2,128)S(1)} %collective-permute-done.3), channel_id=1, source_target_pairs={{0,64},{8,72},{16,80},{24,88},{32,96},{40,104},{48,112},{56,120},{... | collective-permute-start | bytes 125960 | tf_op jit(solution)/shard_map/ppermute | solution.py:16
  20.6 10.2 %collective-permute-start.6 = (f32[41,2,128]{2,1,0:T(2,128)S(1)}, f32[41,2,128]{2,1,0:T(2,128)S(1)}, u32[]{:S(2)}, u32[]{:S(2)}) collective-permute-start(f32[41,2,128]{2,1,0:T(2,128)S(1)} %get-tuple-element.36), channel_id=1, source_target_pairs={{1,0},{2,1},{3,2},{4,3},{5,4},{6,5},{7,6},{9,8},{10,9},{11,10},{12... | collective-permute-start | bytes 125960 | tf_op jit(solution)/shard_map/ppermute | solution.py:27
  23.0 9.0 %collective-permute-start.5 = (f32[41,2,128]{2,1,0:T(2,128)S(1)}, f32[41,2,128]{2,1,0:T(2,128)S(1)}, u32[]{:S(2)}, u32[]{:S(2)}) collective-permute-start(f32[41,2,128]{2,1,0:T(2,128)S(1)} %collective-permute-done.4), channel_id=1, source_target_pairs={{0,128},{8,136},{16,144},{24,152},{32,160},{40,168},{48,176},{56,1... | collective-permute-start | bytes 125960 | tf_op jit(solution)/shard_map/ppermute | solution.py:16
  29.6 5.9 %collective-permute-start = (f32[41,2,128]{2,1,0:T(2,128)S(1)}, f32[41,2,128]{2,1,0:T(2,128)S(1)}, u32[]{:S(2)}, u32[]{:S(2)}) collective-permute-start(f32[41,2,128]{2,1,0:T(2,128)S(1)} %get-tuple-element.37), channel_id=1, source_target_pairs={{0,1},{1,2},{2,3},{3,4},{4,5},{5,6},{6,7},{8,9},{9,10},{10,11},{11... | collective-permute-start | bytes 125960 | tf_op jit(solution)/shard_map/ppermute | solution.py:26
  46.1 9.2 %collective-permute-start.7 = (f32[41,196,2]{1,0,2:T(8,128)S(1)}, f32[41,196,2]{1,0,2:T(8,128)S(1)}, u32[]{:S(2)}, u32[]{:S(2)}) collective-permute-start(f32[41,196,2]{1,0,2:T(8,128)S(1)} %copy.147), channel_id=1, source_target_pairs={{0,8},{8,16},{16,24},{24,32},{32,40},{40,48},{48,56},{56,64},{64,7... | collective-permute-start | bytes 192872 | tf_op jit(solution)/shard_map/ppermute | solution.py:26
  49.7 8.5 %collective-permute-start.8 = (f32[41,196,2]{1,0,2:T(8,128)S(1)}, f32[41,196,2]{1,0,2:T(8,128)S(1)}, u32[]{:S(2)}, u32[]{:S(2)}) collective-permute-start(f32[41,196,2]{1,0,2:T(8,128)S(1)} %copy.148), channel_id=1, source_target_pairs={{8,0},{16,8},{24,16},{32,24},{40,32},{48,40},{56,48},{64,56},{72,6... | collective-permute-start | bytes 192872 | tf_op jit(solution)/shard_map/ppermute | solution.py:27
  58.2 4.1 %slice-start = ((s8[4198400]{0:T(1024)(128)(4,1)}), s8[4096]{0:T(1024)(128)(4,1)S(1)}, s32[]{:S(2)}) async-start(s8[4198400]{0:T(1024)(128)(4,1)} %bitcast.4), calls=%async_computation | async-start | bytes 8192
  61.0 2.3 %copy-start.1 = (f32[41,192,128]{2,1,0:T(8,128)S(1)}, f32[41,192,128]{2,1,0:T(8,128)}, u32[]{:S(2)}) copy-start(f32[41,192,128]{2,1,0:T(8,128)} %copy-done) | copy-start | bytes 12091396
  61.0 3.6 %slice-start.1 = ((s8[4198400]{0:T(1024)(128)(4,1)}), s8[4194304]{0:T(1024)(128)(4,1)S(1)}, s32[]{:S(2)}) async-start(s8[4198400]{0:T(1024)(128)(4,1)} %bitcast.4), calls=%async_computation.1 | async-start | bytes 8388608
  61.0 4.8 %copy-start.4 = (f32[41,196,2]{2,1,0:T(8,128)S(1)}, f32[41,196,2]{2,1,0:T(8,128)}, u32[]{:S(2)}) copy-start(f32[41,196,2]{2,1,0:T(8,128)} %copy.150) | copy-start | bytes 192868
  65.8 2.7 %copy-start.14 = (s32[192,128]{1,0:T(8,128)S(1)}, s32[192,128]{1,0:T(8,128)}, u32[]{:S(2)}) copy-start(s32[192,128]{1,0:T(8,128)} %param.13) | copy-start | bytes 294916
  73.8 54.4 %copy-start.6 = (f32[8,192,128]{2,1,0:T(8,128)}, f32[8,192,128]{2,1,0:T(8,128)S(1)}, u32[]{:S(2)}) copy-start(f32[8,192,128]{2,1,0:T(8,128)S(1)} %get-tuple-element.29) | copy-start | bytes 2359300
  74.3 53.9 %copy-start.7 = (f32[8,192,128]{2,1,0:T(8,128)}, f32[8,192,128]{2,1,0:T(8,128)S(1)}, u32[]{:S(2)}) copy-start(f32[8,192,128]{2,1,0:T(8,128)S(1)} %multiply_multiply_fusion.1) | copy-start | bytes 2359300
  74.5 1.3 collective-permute-start.10
  75.7 5.2 %collective-permute-start.11 = (f32[16,2,128]{2,0,1:T(8,128)S(1)}, f32[16,2,128]{2,0,1:T(8,128)S(1)}, u32[]{:S(2)}, u32[]{:S(2)}) collective-permute-start(f32[16,2,128]{2,0,1:T(8,128)S(1)} %collective-permute-done.10), channel_id=1, source_target_pairs={{0,16},{8,24},{16,0},{24,8},{32,48},{40,56},{48,32},{56,40},{64,80... | collective-permute-start | bytes 49160 | tf_op jit(solution)/shard_map/ppermute | solution.py:16
  81.0 3.7 %collective-permute-start.12 = (f32[16,2,128]{2,0,1:T(8,128)S(1)}, f32[16,2,128]{2,0,1:T(8,128)S(1)}, u32[]{:S(2)}, u32[]{:S(2)}) collective-permute-start(f32[16,2,128]{2,0,1:T(8,128)S(1)} %collective-permute-done.11), channel_id=1, source_target_pairs={{0,32},{8,40},{16,48},{24,56},{32,0},{40,8},{48,16},{56,24},{64,96... | collective-permute-start | bytes 49160 | tf_op jit(solution)/shard_map/ppermute | solution.py:16
  84.7 6.4 %collective-permute-start.13 = (f32[16,2,128]{2,0,1:T(8,128)S(1)}, f32[16,2,128]{2,0,1:T(8,128)S(1)}, u32[]{:S(2)}, u32[]{:S(2)}) collective-permute-start(f32[16,2,128]{2,0,1:T(8,128)S(1)} %collective-permute-done.12), channel_id=1, source_target_pairs={{0,64},{8,72},{16,80},{24,88},{32,96},{40,104},{48,112},{56,120},{... | collective-permute-start | bytes 49160 | tf_op jit(solution)/shard_map/ppermute | solution.py:16
  85.9 20.7 %collective-permute-start.15 = (f32[16,2,128]{2,0,1:T(8,128)S(1)}, f32[16,2,128]{2,0,1:T(8,128)S(1)}, u32[]{:S(2)}, u32[]{:S(2)}) collective-permute-start(f32[16,2,128]{2,0,1:T(8,128)S(1)} %copy.158), channel_id=1, source_target_pairs={{1,0},{2,1},{3,2},{4,3},{5,4},{6,5},{7,6},{9,8},{10,9},{11,10},{12... | collective-permute-start | bytes 49160 | tf_op jit(solution)/shard_map/ppermute | solution.py:27
  89.8 16.8 %collective-permute-start.9 = (f32[16,2,128]{2,0,1:T(8,128)S(1)}, f32[16,2,128]{2,0,1:T(8,128)S(1)}, u32[]{:S(2)}, u32[]{:S(2)}) collective-permute-start(f32[16,2,128]{2,0,1:T(8,128)S(1)} %copy.155), channel_id=1, source_target_pairs={{0,1},{1,2},{2,3},{3,4},{4,5},{5,6},{6,7},{8,9},{9,10},{10,11},{11... | collective-permute-start | bytes 49160 | tf_op jit(solution)/shard_map/ppermute | solution.py:26
  91.1 15.5 %collective-permute-start.14 = (f32[16,2,128]{2,0,1:T(8,128)S(1)}, f32[16,2,128]{2,0,1:T(8,128)S(1)}, u32[]{:S(2)}, u32[]{:S(2)}) collective-permute-start(f32[16,2,128]{2,0,1:T(8,128)S(1)} %collective-permute-done.13), channel_id=1, source_target_pairs={{0,128},{8,136},{16,144},{24,152},{32,160},{40,168},{48,176},{56,1... | collective-permute-start | bytes 49160 | tf_op jit(solution)/shard_map/ppermute | solution.py:16
  111.0 13.0 %collective-permute-start.16 = (f32[16,196,2]{1,0,2:T(8,128)S(1)}, f32[16,196,2]{1,0,2:T(8,128)S(1)}, u32[]{:S(2)}, u32[]{:S(2)}) collective-permute-start(f32[16,196,2]{1,0,2:T(8,128)S(1)} %copy.162), channel_id=1, source_target_pairs={{0,8},{8,16},{16,24},{24,32},{32,40},{40,48},{48,56},{56,64},{64,7... | collective-permute-start | bytes 75272 | tf_op jit(solution)/shard_map/ppermute | solution.py:26
  113.3 12.4 %collective-permute-start.17 = (f32[16,196,2]{1,0,2:T(8,128)S(1)}, f32[16,196,2]{1,0,2:T(8,128)}, u32[]{:S(2)}, u32[]{:S(2)}) collective-permute-start(f32[16,196,2]{1,0,2:T(8,128)S(1)} %copy.164), channel_id=1, source_target_pairs={{8,0},{16,8},{24,16},{32,24},{40,32},{48,40},{56,48},{64,56},{72,6... | collective-permute-start | bytes 75272 | tf_op jit(solution)/shard_map/ppermute | solution.py:27
  118.7 4.0 %copy-start.2 = (f32[41,192,128]{2,1,0:T(8,128)S(1)}, f32[41,192,128]{2,1,0:T(8,128)}, u32[]{:S(2)}) copy-start(f32[41,192,128]{2,1,0:T(8,128)} %copy-done) | copy-start | bytes 12091396
  136.7 14.7 %slice-start.2 = ((s8[4198400]{0:T(1024)(128)(4,1)}), s8[4096]{0:T(1024)(128)(4,1)S(1)}, s32[]{:S(2)}) async-start(s8[4198400]{0:T(1024)(128)(4,1)} %bitcast.6), calls=%async_computation.2 | async-start | bytes 8192
  140.7 3.4 %copy-start.9 = (f32[8,193,128]{2,1,0:T(8,128)S(1)}, f32[8,193,128]{2,1,0:T(8,128)}, u32[]{:S(2)}) copy-start(f32[8,193,128]{2,1,0:T(8,128)} %get-tuple-element.27) | copy-start | bytes 2371588
  144.1 7.4 %copy-start.3 = (f32[41,192,128]{2,1,0:T(8,128)S(1)}, f32[41,192,128]{2,1,0:T(8,128)}, u32[]{:S(2)}) copy-start(f32[41,192,128]{2,1,0:T(8,128)} %copy-done) | copy-start | bytes 12091396
  144.1 7.4 %slice-start.3 = ((s8[4198400]{0:T(1024)(128)(4,1)}), s8[4194304]{0:T(1024)(128)(4,1)S(1)}, s32[]{:S(2)}) async-start(s8[4198400]{0:T(1024)(128)(4,1)} %bitcast.6), calls=%async_computation.3 | async-start | bytes 8388608
  144.1 7.4 %copy-start.8 = (f32[8,193,128]{2,1,0:T(8,128)S(1)}, f32[8,193,128]{2,1,0:T(8,128)}, u32[]{:S(2)}) copy-start(f32[8,193,128]{2,1,0:T(8,128)} %fusion.25) | copy-start | bytes 2371588
  144.1 7.7 %copy-start.13 = (f32[8,192,128]{2,1,0:T(8,128)S(1)}, f32[8,192,128]{2,1,0:T(8,128)}, u32[]{:S(2)}) copy-start(f32[8,192,128]{2,1,0:T(8,128)} %param.7) | copy-start | bytes 2359300
where the time goes:
time: 159 us; the launch traced here: 157 us
  other arithmetic  56.3 us (35%)
  local copies, waits for them, and re-layouts  40.3 us (25%)
  starting transfers between devices  39.8 us (25%)
  waiting for transfers between devices  19.2 us (12%)
    ppermute x10, starting transfers between devices, swapped(): lax.ppermute(array, axis, [(i, i ^ 1 << distance) for i in range(lax.axis...  19.7 us
    ppermute x4, starting transfers between devices, with_halo(): after = lax.ppermute(leading, axis, down)  17.2 us
    ppermute x10, waiting for transfers between devices, swapped(): lax.ppermute(array, axis, [(i, i ^ 1 << distance) for i in range(lax.axis...  15.8 us
    concatenate x1, other arithmetic, with_halo(): array = jnp.concatenate([before, array, after], axis=dim)  13.1 us
    mul x2, other arithmetic, advance(): wet_centre * (offset_view(field, 0, 0) - time_step * spread + time_step *...  12.2 us
    unnamed x49, local copies, waits for them, and re-layouts  12 us
    mul x2, other arithmetic, advance(): flux_x = trans_x * faces_x(field)  11.6 us
    slice x5, local copies, waits for them, and re-layouts, with_halo(): leading = lax.slice_in_dim(array, 0, width, axis=dim)  10.3 us
  transfers between devices with their start and end apart: 18, of which 8 were waited for; matrix products, arithmetic and copies ran while one was open for 18% of the time, Pallas kernels for 0%

commit v1 on v0

v1 whole, which is shorter than its diff:
```python
import functools

import jax
import jax.numpy as jnp
from jax import lax
from jax.experimental import pallas as pl
from jax.experimental.pallas import tpu as pltpu
from jax.sharding import PartitionSpec as P

F32 = jnp.float32
LEVELS = 8
LANES = 128
FIELDS = 5
PLANES = FIELDS * LEVELS + 1
ROW_MSG = 2 * FIELDS * LEVELS + 8
BASE = 16
CHUNKS = 4
PACK_ROWS = 48
MAIN_ROWS = 96
EDGE_CHUNKS = 1

time_step = 0.2
viscosity = 0.5
diffusivity = 0.3
press_scale = 0.25
gravity = 1.0
drag_coef = 1.0
coriolis_max = 0.5

HBM = pl.BlockSpec(memory_space=pltpu.HBM)
VMEM = pl.BlockSpec(memory_space=pltpu.VMEM)


def params(mib):
    return pltpu.CompilerParams(vmem_limit_bytes=int(mib * 1024 * 1024))


def lanes(rows=8):
    return lax.broadcasted_iota(jnp.int32, (rows, LANES), 1)


def east(x):
    return pltpu.roll(x, LANES - 1, 1)


def west(x):
    return pltpu.roll(x, 1, 1)


def gather(x, index):
    return jnp.take_along_axis(x, index, axis=1)


def is_even(axis):
    return lax.rem(lax.axis_index(axis), 2) == 0


def row_pack_kernel(*refs):
    ins, (a_ref, b_ref), tiles, sems = refs[:6], refs[6:8], refs[8:20], refs[20]
    rows = ins[5].shape[0]
    copies = []
    for n, x in enumerate(ins):
        for side, start in enumerate((0, rows - 8)):
            src = x.at[:, pl.ds(start, 8), :] if n < FIELDS else x.at[pl.ds(start, 8), :]
            copies.append(pltpu.make_async_copy(src, tiles[2 * n + side], sems.at[2 * n + side]))
            copies[-1].start()
    for x in copies:
        x.wait()
    even = is_even("lat")
    for r in range(2):
        for f in range(FIELDS):
            low, high = tiles[2 * f : 2 * f + 2]
            bottom = low.reshape(LEVELS * 8, LANES)[pl.ds(r, LEVELS, stride=8), :].astype(F32)
            top = high.reshape(LEVELS * 8, LANES)[pl.ds(6 + r, LEVELS, stride=8), :].astype(F32)
            place = pl.ds((r * FIELDS + f) * LEVELS, LEVELS)
            a_ref[place, :] = jnp.where(even, top, bottom)
            b_ref[place, :] = jnp.where(even, bottom, top)
    place = pl.ds(2 * FIELDS * LEVELS, 8)
    low, high = tiles[10][...], tiles[11][...]
    a_ref[place, :] = jnp.where(even, high, low)
    b_ref[place, :] = jnp.where(even, low, high)


def row_pack(fields, surface):
    scratch = [pltpu.VMEM((LEVELS, 8, LANES), x.dtype) for x in fields for _ in range(2)]
    scratch += [pltpu.VMEM((8, LANES), F32)] * 2 + [pltpu.SemaphoreType.DMA((12,))]
    return pl.pallas_call(
        row_pack_kernel,
        in_specs=[HBM] * 6,
        out_specs=[VMEM] * 2,
        out_shape=[pltpu.VMEM((ROW_MSG, LANES), F32)] * 2,
        scratch_shapes=scratch,
        compiler_params=params(60),
        name="row_pack",
    )(*fields, surface)


def pack_columns(plane, rows):
    lane = lanes(rows)
    packed = []
    for first in range(0, PLANES, 16):
        group = None
        for p in range(first, min(first + 16, PLANES)):
            q = p - first
            moved = pltpu.roll(plane(p), (8 * q + 4) % LANES, 1)
            group = moved if group is None else jnp.where(lane >= 8 * q, moved, group)
        packed.append(group)
    return packed


def column_messages(packed, even, rows):
    lane = lanes(rows)
    base = 8 * ((lane // 2) % 16) + lane % 2
    messages = []
    for first in (True, False):
        eastern = even if first else jnp.logical_not(even)
        index = base + jnp.where(eastern, 2, 4)
        c0, c1, c2 = [gather(c, index) for c in packed]
        messages.append(jnp.where(lane < 32, c0, jnp.where(lane < 64, c1, c2)))
    return messages


def column_pack_kernel(t_in, s_in, u_in, v_in, w_in, e_in, t, s, u, v, w, e, p, c_ref, m0_ref, m1_ref, wi, sems):
    rows = e_in.shape[0]
    block = rows // CHUNKS
    even = is_even("lon")
    fields = (t, s, u, v, w)
    copies = []
    for c in range(CHUNKS):
        src, dst = pl.ds(c * block, block), pl.ds(BASE + c * block, block)
        pairs = [(x.at[:, src, :], y.at[:, dst, :]) for x, y in ((t_in, t), (s_in, s), (u_in, u), (v_in, v))]
        pairs += [(w_in.at[:, src, :], wi.at[:, src, :]), (e_in.at[src, :], e.at[dst, :])]
        copies.append([pltpu.make_async_copy(x, y, sems.at[6 * c + n]) for n, (x, y) in enumerate(pairs)])
        for x in copies[-1]:
            x.start()
    for c in range(CHUNKS):
        for x in copies[c]:
            x.wait()

        def step(i, _):
            out = pl.ds(pl.multiple_of(c * block + i * PACK_ROWS, 8), PACK_ROWS)
            here = pl.ds(pl.multiple_of(BASE + c * block + i * PACK_ROWS, 8), PACK_ROWS)
            for k in range(LEVELS):
                w[k, here, :] = wi[k, out, :].astype(F32)

            def plane(q):
                if q == PLANES - 1:
                    return e[here, :]
                return fields[q // LEVELS][q % LEVELS, here, :]

            packed = pack_columns(plane, PACK_ROWS)
            for n, x in enumerate(packed):
                c_ref[out, n * LANES : (n + 1) * LANES] = x
            m0_ref[out, :], m1_ref[out, :] = column_messages(packed, even, PACK_ROWS)
            pressure(here, t, s, e, p)
            return 0

        lax.fori_loop(0, block // PACK_ROWS, step, 0)


def column_pack(fields, surface):
    rows = surface.shape[0]
    tall = rows + BASE + 16
    big = pltpu.VMEM((LEVELS, tall, LANES), F32)
    return pl.pallas_call(
        column_pack_kernel,
        in_specs=[HBM] * 6,
        out_specs=[VMEM] * 10,
        out_shape=[big] * 5
        + [pltpu.VMEM((tall, LANES), F32), big]
        + [pltpu.VMEM((rows + 8, 3 * LANES), F32)]
        + [pltpu.VMEM((rows + 8, LANES), F32)] * 2,
        scratch_shapes=[pltpu.VMEM((LEVELS, rows, LANES), jnp.int32), pltpu.SemaphoreType.DMA((6 * CHUNKS,))],
        compiler_params=params(57.5),
        cost_estimate=pl.CostEstimate(flops=10_000_000, bytes_accessed=6_000_000, transcendentals=0),
        name="column_pack",
    )(*fields, surface)


def ghost_kernel(a_ref, b_ref, *refs):
    t, s, u, v, w, e, p, c_ref, m0_ref, m1_ref, g_ref = refs[10:]
    rows = m0_ref.shape[0] - 8
    even = is_even("lat")
    fold = lax.axis_index("lat") == lax.axis_size("lat") - 1
    mirror = LANES - 1 - lanes()
    flat = g_ref.reshape(PLANES * 8, LANES)
    g_ref[...] = jnp.zeros_like(g_ref)

    def both(start):
        a, b = a_ref[pl.ds(start, 8), :], b_ref[pl.ds(start, 8), :]
        return jnp.where(even, a, b), jnp.where(even, b, a)

    for f in range(FIELDS):
        sign = -1.0 if f in (2, 3) else 1.0
        north0, south0 = both(f * LEVELS)
        north1, south1 = both((FIELDS + f) * LEVELS)
        first = jnp.where(fold, sign * gather(north1, mirror), north0)
        second = jnp.where(fold, sign * gather(north0, mirror), north1)
        for row, value in ((0, first), (1, second), (6, south0), (7, south1)):
            flat[pl.ds(f * LEVELS * 8 + row, LEVELS, stride=8), :] = value
    north, south = both(2 * FIELDS * LEVELS)
    turned = gather(north, mirror)
    row = lax.broadcasted_iota(jnp.int32, (8, LANES), 0)
    folded = jnp.where(row == 0, pltpu.roll(turned, 1, 0), pltpu.roll(turned, 3, 0))
    g_ref[PLANES - 1] = jnp.where(row < 2, jnp.where(fold, folded, north), jnp.where(row >= 6, south, 0.0))
    packed = pack_columns(lambda q: g_ref[q], 8)
    last = pl.ds(rows, 8)
    for n, c in enumerate(packed):
        c_ref[last, n * LANES : (n + 1) * LANES] = c
    m0_ref[last, :], m1_ref[last, :] = column_messages(packed, is_even("lon"), 8)
    for side in (pl.ds(BASE - 8, 8), pl.ds(BASE + rows, 8)):
        for f, x in enumerate((t, s, u, v, w)):
            for k in range(LEVELS):
                x[k, side, :] = g_ref[f * LEVELS + k]
        e[side, :] = g_ref[PLANES - 1]
        pressure(side, t, s, e, p)


def ghosts(a, b, arrays):
    return pl.pallas_call(
        ghost_kernel,
        in_specs=[VMEM] * 12,
        out_specs=[VMEM] * 10,
        out_shape=[pltpu.VMEM(x.shape, F32) for x in arrays],
        scratch_shapes=[pltpu.VMEM((PLANES, 8, LANES), F32)],
        input_output_aliases={n + 2: n for n in range(10)},
        compiler_params=params(8),
        name="ghosts",
    )(a, b, *arrays)


def density_half(t, s):
    k = 0.5 * press_scale * 0.5 * time_step
    return t * (-0.2 * k + (-0.05 * k) * t + (0.02 * k) * s) + (0.8 * k) * s


def pressure(here, t, s, e, p):
    total = (gravity * 0.5 * time_step) * e[here, :]
    for k in range(LEVELS):
        h = density_half(t[k, here, :], s[k, here, :])
        at = total + h
        p[k, here, :] = at
        total = at + h


def coriolis_rows(start, count, rows):
    total = rows * lax.axis_size("lat")
    row = lax.broadcasted_iota(jnp.int32, (count, LANES), 0) + (start - BASE + lax.axis_index("lat") * rows)
    row = jnp.minimum(row, total - 1).astype(F32)
    return (time_step * coriolis_max) * (2.0 * (row + 0.5) / total - 1.0)


def velocity_trial(k, r, n, spin, u, v, w, p, m_east, m_north):
    here, up, down = pl.ds(r, n), pl.ds(r + 1, n), pl.ds(r - 1, n)
    wet = w[k, here, :]
    me = wet * east(wet)
    mw = wet * west(wet)
    mn = wet * w[k, up, :]
    ms = wet * w[k, down, :]
    m_east[k, here, :] = me
    m_north[k, here, :] = mn

    def lap(q_ref, q):
        return me * (east(q) - q) + mw * (west(q) - q) + (mn * (q_ref[k, up, :] - q) + ms * (q_ref[k, down, :] - q))

    un, vn = u[k, here, :], v[k, here, :]
    pc = p[k, here, :]
    u_trial = un + (spin * vn - (east(pc) - west(pc)) + (time_step * viscosity) * lap(u, un))
    v_trial = vn + ((time_step * viscosity) * lap(v, vn) - spin * un - (p[k, up, :] - p[k, down, :]))
    return wet, u_trial, v_trial


def damping(u, v):
    return 1.0 / (1.0 + drag_coef * jnp.sqrt(u * u + v * v))


FLUX = time_step * 0.5 / 12.0
HEIGHT = time_step / LEVELS * 0.5 / FLUX


def flux(q0, q1, qm, qp, tr, md):
    return tr * (7.0 * (q0 + q1) - (qm + qp)) - md * (q1 - q0)


def north_flux(k, r, n, vel, m_north, tracers, g_refs):
    here, up = pl.ds(r, n), pl.ds(r + 1, n)
    mn = m_north[k, here, :]
    tr = (FLUX * mn) * (vel[k, here, :] + vel[k, up, :])
    md = (time_step * diffusivity) * mn
    out = []
    for q, g in zip(tracers, g_refs):
        gy = flux(q[k, here, :], q[k, up, :], q[k, pl.ds(r - 1, n), :], q[k, pl.ds(r + 2, n), :], tr, md)
        g[k, here, :] = gy
        out.append(gy)
    return tr, out


def east_flux(k, r, n, u_next, m_east, tracers):
    here = pl.ds(r, n)
    me = m_east[k, here, :]
    tr = (FLUX * me) * (u_next + east(u_next))
    md = (time_step * diffusivity) * me
    out = []
    for q_ref in tracers:
        q = q_ref[k, here, :]
        out.append((q, flux(q, east(q), west(q), pltpu.roll(q, LANES - 2, 1), tr, md)))
    return tr, out


def main_kernel(t, s, u, v, w, e, p, t_out, s_out, u_out, v_out, h_out, me, mn, vel, gt, gs, hy):
    rows = h_out.shape[0]

    def loop(start, count, body):
        if count == 1:
            body(start)
            return

        def step(i, _):
            body(pl.multiple_of(start + i * MAIN_ROWS, 8))
            return 0

        lax.fori_loop(0, count, step, 0)

    def velocities(n, store):
        def body(r):
            here = pl.ds(r, n)
            spin = coriolis_rows(r, n, rows)
            trial = [velocity_trial(k, r, n, spin, u, v, w, p, me, mn) for k in range(LEVELS)]
            at_floor = [trial[k][0] > (trial[k + 1][0] if k + 1 < LEVELS else 0.0) for k in range(LEVELS)]
            u_floor, v_floor = trial[0][1], trial[0][2]
            for k in range(1, LEVELS):
                u_floor = jnp.where(at_floor[k], trial[k][1], u_floor)
                v_floor = jnp.where(at_floor[k], trial[k][2], v_floor)
            damp = damping(u_floor, v_floor)
            for k in range(LEVELS):
                factor = jnp.where(at_floor[k], damp, trial[k][0])
                v_next = factor * trial[k][2]
                vel[k, here, :] = v_next
                if store:
                    out = pl.ds(pl.multiple_of(r - BASE, 8), n)
                    u_out[k, out, :] = factor * trial[k][1]
                    v_out[k, out, :] = v_next

        return body

    def south_edge(r):
        total = 0.0
        for k in range(LEVELS):
            total = total + north_flux(k, r, 8, vel, mn, (t, s), (gt, gs))[0]
        hy[pl.ds(r, 8), :] = total

    def tracer(r):
        n = MAIN_ROWS
        here, down = pl.ds(r, n), pl.ds(r - 1, n)
        out = pl.ds(pl.multiple_of(r - BASE, 8), n)
        total_x = total_y = 0.0
        for k in range(LEVELS):
            tr_y, (gy_t, gy_s) = north_flux(k, r, n, vel, mn, (t, s), (gt, gs))
            tr_x, ((tc, gx_t), (sc, gx_s)) = east_flux(k, r, n, u_out[k, out, :], me, (t, s))
            total_x, total_y = total_x + tr_x, total_y + tr_y
            wet = w[k, here, :]
            t_out[k, out, :] = wet * (tc - (gx_t - west(gx_t) + (gy_t - gt[k, down, :])))
            s_out[k, out, :] = wet * (sc - (gx_s - west(gx_s) + (gy_s - gs[k, down, :])))
        hy[here, :] = total_y
        h_out[out, :] = e[here, :] - HEIGHT * (total_x - west(total_x) + (total_y - hy[down, :]))

    count = rows // MAIN_ROWS
    loop(BASE - 8, 1, velocities(8, False))
    loop(BASE + rows, 1, velocities(8, False))
    loop(BASE, count, velocities(MAIN_ROWS, True))
    south_edge(BASE - 8)
    loop(BASE, count, tracer)


def main(arrays, rows):
    big = pltpu.VMEM(arrays[0].shape, F32)
    out3 = pltpu.VMEM((LEVELS, rows, LANES), F32)
    return pl.pallas_call(
        main_kernel,
        in_specs=[VMEM] * 7,
        out_specs=[VMEM] * 5,
        out_shape=[out3] * 4 + [pltpu.VMEM((rows, LANES), F32)],
        scratch_shapes=[big] * 5 + [pltpu.VMEM(arrays[5].shape, F32)],
        compiler_params=params(16),
        cost_estimate=pl.CostEstimate(flops=40_000_000, bytes_accessed=8_000_000, transcendentals=100_000),
        name="main",
    )(*arrays)


def edge_kernel(c_ref, m0_ref, m1_ref, t_in, s_in, u_in, v_in, h_in, t_hbm, s_hbm, u_hbm, v_hbm, h_hbm,
                t, s, u, v, w, e, p, me, mn, un, vel, gt, gs, hy, ot, os, ou, ov, oh, sems):
    rows = h_in.shape[0]
    even = is_even("lon")

    def layout(n):
        lane = lanes(n)
        return lane, lane // 16, lane % 16

    def spread(source, place, n):
        lane, level, slot = layout(n)
        own = jnp.where(slot < 4, slot, jnp.where((slot >= 8) & (slot < 12), slot - 4, 0))
        other = jnp.where((slot == 5) | (slot == 7), 1, 0)
        from_east = (slot == 4) | (slot == 5)
        from_west = (slot == 6) | (slot == 7)
        src, here = pl.ds(source, n), pl.ds(place, n)
        m0, m1 = m0_ref[src, :], m1_ref[src, :]
        m_east, m_west = jnp.where(even, m0, m1), jnp.where(even, m1, m0)

        def strip(packed, own_lane, ghost_lane):
            return jnp.where(
                from_east,
                gather(m_east, ghost_lane),
                jnp.where(from_west, gather(m_west, ghost_lane), gather(packed, own_lane)),
            )

        for f, x in enumerate((t, s, u, v, w)):
            packed = c_ref[src, (f // 2) * LANES : (f // 2 + 1) * LANES]
            x[0, here, :] = strip(packed, 8 * level + own + 64 * (f % 2), 2 * level + other + 2 * LEVELS * f)
        e[here, :] = strip(c_ref[src, 2 * LANES : 3 * LANES], own + 64, other + 2 * (PLANES - 1))

    def strip_pressure(r, n):
        here = pl.ds(r, n)
        lane = lanes(n)
        h = density_half(t[0, here, :], s[0, here, :])
        total = h
        for step in (16, 32, 64):
            total = total + jnp.where(lane >= step, pltpu.roll(total, step, 1), 0.0)
        p[0, here, :] = (gravity * 0.5 * time_step) * e[here, :] + (2.0 * total - h)

    def velocities(r, n):
        here = pl.ds(r, n)
        lane = lanes(n)
        wet, u_trial, v_trial = velocity_trial(0, r, n, coriolis_rows(r, n, rows), u, v, w, p, me, mn)
        below = jnp.where(lane < LANES - 16, pltpu.roll(wet, LANES - 16, 1), 0.0)
        factor = jnp.where(wet > below, damping(u_trial, v_trial), wet)
        un[0, here, :] = factor * u_trial
        vel[0, here, :] = factor * v_trial

    def joined(strip, slot):
        return jnp.where(slot < 4, strip, pltpu.roll(strip, LANES - 4, 1))

    def tracer(r, n):
        lane, level, slot = layout(n)
        edge = (lane < 2) | (lane >= LANES - 2)
        here, down = pl.ds(r, n), pl.ds(r - 1, n)
        out = pl.ds(r - BASE, n)
        u_next = un[0, here, :]
        tr_y, (gy_t, gy_s) = north_flux(0, r, n, vel, mn, (t, s), (gt, gs))
        tr_x, ((tc, gx_t), (sc, gx_s)) = east_flux(0, r, n, u_next, me, (t, s))
        wet = w[0, here, :]
        hy[here, :] = tr_y
        strips = (
            wet * (tc - (gx_t - west(gx_t) + (gy_t - gt[0, down, :]))),
            wet * (sc - (gx_s - west(gx_s) + (gy_s - gs[0, down, :]))),
            u_next,
            vel[0, here, :],
        )
        for strip, main_in, out_ref in zip(strips, (t_in, s_in, u_in, v_in), (ot, os, ou, ov)):
            wide = joined(strip, slot)
            for k in range(LEVELS):
                placed = pltpu.roll(wide, (-(16 * k + 4)) % LANES, 1)
                out_ref[k, out, :] = jnp.where(edge, placed, main_in[k, out, :])
        inflow = tr_x - west(tr_x) + (tr_y - hy[down, :])
        for step in (16, 32, 64):
            inflow = inflow + pltpu.roll(inflow, step, 1)
        wide = joined(e[here, :] - HEIGHT * inflow, slot)
        oh[out, :] = jnp.where(edge, pltpu.roll(wide, LANES - 4, 1), h_in[out, :])

    spread(0, BASE, rows + 8)
    strip_pressure(BASE, rows + 8)
    for x in (t, s, u, v, w, p):
        x[0, pl.ds(BASE - 8, 8), :] = x[0, pl.ds(BASE + rows, 8), :]
    e[pl.ds(BASE - 8, 8), :] = e[pl.ds(BASE + rows, 8), :]
    velocities(BASE - 8, rows + 16)
    hy[pl.ds(BASE - 8, 8), :] = north_flux(0, BASE - 8, 8, vel, mn, (t, s), (gt, gs))[0]
    copies = []
    block = rows // EDGE_CHUNKS
    for c in range(EDGE_CHUNKS):
        tracer(BASE + c * block, block)
        at = pl.ds(c * block, block)
        for n, (x, y) in enumerate(((ot, t_hbm), (os, s_hbm), (ou, u_hbm), (ov, v_hbm))):
            copies.append(pltpu.make_async_copy(x.at[:, at, :], y.at[:, at, :], sems.at[c * 5 + n]))
        copies.append(pltpu.make_async_copy(oh.at[at, :], h_hbm.at[at, :], sems.at[c * 5 + 4]))
        for x in copies[-5:]:
            x.start()
    for x in copies:
        x.wait()


def edges(c, m0, m1, outs):
    rows = outs[4].shape[0]
    tall = rows + BASE + 16
    big = pltpu.VMEM((1, tall, LANES), F32)
    flat = pltpu.VMEM((tall, LANES), F32)
    out3 = jax.ShapeDtypeStruct((LEVELS, rows, LANES), F32)
    wide = pltpu.VMEM((LEVELS, rows, LANES), F32)
    return pl.pallas_call(
        edge_kernel,
        in_specs=[VMEM] * 8,
        out_specs=[HBM] * 5,
        out_shape=[out3] * 4 + [jax.ShapeDtypeStruct((rows, LANES), F32)],
        scratch_shapes=[big] * 5
        + [flat]
        + [big] * 7
        + [flat]
        + [wide] * 4
        + [pltpu.VMEM((rows, LANES), F32), pltpu.SemaphoreType.DMA((5 * EDGE_CHUNKS,))],
        compiler_params=params(16),
        name="edges",
    )(c, m0, m1, *outs)


def swaps():
    lon, lat = lax.axis_size("lon"), lax.axis_size("lat")

    def device(o, a):
        return o % lon * lat + a

    lat_first, lat_second, lon_first, lon_second = [], [], [], []
    for o in range(lon):
        for a in range(lat):
            lat_first.append((device(o, a), device(o, a ^ 1)))
            if a == lat - 1:
                lat_second.append((device(o, a), device(lon - 1 - o, a)))
            elif a > 0:
                lat_second.append((device(o, a), device(o, a + 1 if a % 2 else a - 1)))
            lon_first.append((device(o, a), device(o ^ 1, a)))
            lon_second.append((device(o, a), device(o + 1 if o % 2 else o - 1, a)))
    return lat_first, lat_second, lon_first, lon_second


def on_device(
    heat_anomaly,
    saltiness_anomaly,
    zonal_current,
    meridional_current,
    free_elevation,
    ocean_indicator,
    floor_layer_index,
):
    lat_first, lat_second, lon_first, lon_second = swaps()
    send = functools.partial(lax.ppermute, axis_name=("lon", "lat"))
    fields = (heat_anomaly, saltiness_anomaly, zonal_current, meridional_current, ocean_indicator)
    a, b = row_pack(fields, free_elevation)
    a = send(a, perm=lat_first)
    b = send(b, perm=lat_second)
    arrays = column_pack(fields, free_elevation)
    *arrays, c, m0, m1 = ghosts(a, b, arrays)
    m0 = send(m0, perm=lon_first)
    m1 = send(m1, perm=lon_second)
    outs = main(arrays, free_elevation.shape[0])
    return tuple(edges(c, m0, m1, outs))


def solution(mesh):
    return jax.shard_map(
        on_device,
        mesh=mesh,
        in_specs=(
            P(None, "lat", "lon"),
            P(None, "lat", "lon"),
            P(None, "lat", "lon"),
            P(None, "lat", "lon"),
            P("lat", "lon"),
            P(None, "lat", "lon"),
            P("lat", "lon"),
        ),
        out_specs=(
            P(None, "lat", "lon"),
            P(None, "lat", "lon"),
            P(None, "lat", "lon"),
            P(None, "lat", "lon"),
            P("lat", "lon"),
        ),
        check_vma=False,
    )
```

time: 159 us -> 29.8 us (0.19); the launches traced: 157 us -> 29.7 us
  other arithmetic: 56.3 us -> 0 us
  local copies, waits for them, and re-layouts: 40.3 us -> 0 us
  starting transfers between devices: 39.8 us -> 14.4 us
  waiting for transfers between devices: 19.2 us -> 0.01 us
  Pallas kernels: 0 us -> 14.6 us
    mul x11 -> x0, other arithmetic: 34.9 us -> none  [the longest x2 12.2 us: advance(): wet_centre * (offset_view(field, 0, 0) - time_step * spread + time_step *...]
    ppermute x18 -> x4, starting transfers between devices: 39.8 us -> 14.4 us  [the longest x1 8.94 us: on_device(): b = send(b, perm=lat_second)]
    ppermute x18 -> x4, waiting for transfers between devices: 19.2 us -> 0.01 us  [the longest x1 0.01 us: on_device(): a = send(a, perm=lat_first)]
    slice x9 -> x0, local copies, waits for them, and re-layouts: 18 us -> none  [the longest x5 10.3 us: with_halo(): leading = lax.slice_in_dim(array, 0, width, axis=dim)]
    concatenate x3 -> x0, other arithmetic: 15.7 us -> none  [the longest x1 13.1 us: with_halo(): array = jnp.concatenate([before, array, after], axis=dim)]
    pallas_call x0 -> x5, Pallas kernels: none -> 14.6 us  [the longest x1 5.69 us: main(): pl.pallas_call(main_kernel, in_specs=[VMEM] * 7, out_specs=[VMEM] * 5, ou...]
    unnamed x49 -> x0, local copies, waits for them, and re-layouts: 12 us -> none
    ppermute x5 -> x0, local copies, waits for them, and re-layouts: 9.9 us -> none  [the longest x2 5.28 us: with_halo(): after = lax.ppermute(leading, axis, down)]
  transfers between devices with their start and end apart: 18 -> 4, of which waited for: 8 -> 0; matrix products, arithmetic and copies ran while one was open for 18% -> 0% of each run, Pallas kernels for 0% -> 30%
where the time goes in v1:
time: 29.8 us; the launch traced here: 29.7 us
  Pallas kernels  14.6 us (49%)
  starting transfers between devices  14.4 us (48%)
  between operations  0.69 us (2%)
    ppermute x1, starting transfers between devices, on_device(): b = send(b, perm=lat_second)  8.94 us
    pallas_call x1, Pallas kernels, main(): pl.pallas_call(main_kernel, in_specs=[VMEM] * 7, out_specs=[VMEM] * 5, ou...  5.69 us
    pallas_call x1, Pallas kernels, edges(): pl.pallas_call(edge_kernel, in_specs=[VMEM] * 8, out_specs=[HBM] * 5, out...  4.24 us
    ppermute x1, starting transfers between devices, on_device(): m1 = send(m1, perm=lon_second)  3.93 us
    pallas_call x1, Pallas kernels, column_pack(): pl.pallas_call(column_pack_kernel, in_specs=[HBM] * 6, out_specs=[VMEM] *...  3.32 us
    pallas_call x1, Pallas kernels, row_pack(): pl.pallas_call(row_pack_kernel, in_specs=[HBM] * 6, out_specs=[VMEM] * 2,...  1.04 us
    ppermute x1, starting transfers between devices, on_device(): m0 = send(m0, perm=lon_first)  0.99 us
  transfers between devices with their start and end apart: 4, of which 0 were waited for; matrix products, arithmetic and copies ran while one was open for 0% of the time, Pallas kernels for 30%

profile of v1, /device:TPU:14, one launch (start us, length us, event | category | flops | bytes accessed | tf_op | source)
XLA Modules:
  0.0 29.7 jit_solution(4391152690750587858)
XLA Ops:
  0.6 1.0 %row_pack.1 = (f32[88,128]{1,0:T(8,128)S(1)}, f32[88,128]{1,0:T(8,128)S(1)}) custom-call(f32[8,192,128]{2,1,0:T(8,128)} %t_in.1, f32[8,192,128]{2,1,0:T(8,128)} %s_in.1, f32[8,192,128]{2,1,0:T(8,128)} %u_in.1, f32[8,192,128]{2,1,0:T(8,128)} %v_in.1, s32[8,192,128]{2,1,0:T(8,128)} %w_in.1, f32[192,128]{1,0:T(8,128)} %e_in.1), custom_call_target="tpu_custom_call" | custom-call | tf_op jit(solution)/shard_map/row_pack/pallas_call | solution.py:87
  1.7 0.5 %collective-permute-start = (f32[88,128]{1,0:T(8,128)S(1)}, f32[88,128]{1,0:T(8,128)S(1)}, u32[]{:S(2)}, u32[]{:S(2)}) collective-permute-start(f32[88,128]{1,0:T(8,128)S(1)} %get-tuple-element.32), channel_id=1, source_target_pairs={{0,1},{1,0},{2,3},{3,2},{4,5},{5,4},{6,7},{7,6},{8,9},{9,8},{10,11... | collective-permute-start | bytes 135176 | tf_op jit(solution)/shard_map/ppermute | solution.py:545
  2.2 8.9 %collective-permute-start.1 = (f32[88,128]{1,0:T(8,128)S(1)}, f32[88,128]{1,0:T(8,128)S(1)}, u32[]{:S(2)}, u32[]{:S(2)}) collective-permute-start(f32[88,128]{1,0:T(8,128)S(1)} %get-tuple-element.33), channel_id=1, source_target_pairs={{1,2},{2,1},{3,4},{4,3},{5,6},{6,5},{7,255},{9,10},{10,9},{11,12},... | collective-permute-start | bytes 135176 | tf_op jit(solution)/shard_map/ppermute | solution.py:546
  11.2 3.3 %column_pack.1 = (f32[8,224,128]{2,1,0:T(8,128)S(1)}, f32[8,224,128]{2,1,0:T(8,128)S(1)}, f32[8,224,128]{2,1,0:T(8,128)S(1)}, f32[8,224,128]{2,1,0:T(8,128)S(1)}...) custom-call(f32[8,192,128]{2,1,0:T(8,128)} %t_in.1, ...), custom_call_target="tpu_custom_call" | custom-call | flops 10000000 | bytes 6000000 | tf_op jit(solution)/shard_map/column_pack/pallas_call | solution.py:165
  14.5 0.0 collective-permute-done.a_ref
  14.5 0.0 collective-permute-done.1.b_ref
  14.5 0.3 ghosts.1
  14.8 1.0 %collective-permute-start.2 = (f32[200,128]{1,0:T(8,128)S(1)}, f32[200,128]{1,0:T(8,128)S(1)}, u32[]{:S(2)}, u32[]{:S(2)}) collective-permute-start(f32[200,128]{1,0:T(8,128)S(1)} %get-tuple-element.45), channel_id=1, source_target_pairs={{0,8},{1,9},{2,10},{3,11},{4,12},{5,13},{6,14},{7,15},{8,0},{9,1},... | collective-permute-start | bytes 307208 | tf_op jit(solution)/shard_map/ppermute | solution.py:549
  15.8 3.9 %collective-permute-start.3 = (f32[200,128]{1,0:T(8,128)S(1)}, f32[200,128]{1,0:T(8,128)S(1)}, u32[]{:S(2)}, u32[]{:S(2)}) collective-permute-start(f32[200,128]{1,0:T(8,128)S(1)} %get-tuple-element.46), channel_id=1, source_target_pairs={{0,248},{1,249},{2,250},{3,251},{4,252},{5,253},{6,254},{7,255},{8... | collective-permute-start | bytes 307208 | tf_op jit(solution)/shard_map/ppermute | solution.py:550
  19.7 5.7 %main.1 = (f32[8,192,128]{2,1,0:T(8,128)S(1)}, f32[8,192,128]{2,1,0:T(8,128)S(1)}, f32[8,192,128]{2,1,0:T(8,128)S(1)}, f32[8,192,128]{2,1,0:T(8,128)S(1)}, f32[192,128]{1,0:T(8,128)S(1)}) custom-call(f32[8,224,128]{2,1,0:T(8,128)S(1)} %get-tuple-element.47.t, f32[8,224,128]{2,1,0:T(8,128)S(1)} %get-tuple-element.48.s, ...), custom_call_target="tpu_custom_call" | custom-call | flops 40000000 | bytes 8000000 | tf_op jit(solution)/shard_map/main/pallas_call | solution.py:378
  25.4 0.0 collective-permute-done.2.m0_ref
  25.4 0.0 collective-permute-done.3.m1_ref
  25.4 4.2 %edges.1 = (f32[8,192,128]{2,1,0:T(8,128)}, f32[8,192,128]{2,1,0:T(8,128)}, f32[8,192,128]{2,1,0:T(8,128)}, f32[8,192,128]{2,1,0:T(8,128)}, f32[192,128]{1,0:T(8,128)}) custom-call(f32[200,384]{1,0:T(8,128)S(1)} %get-tuple-element.44.c_ref, f32[200,128]{1,0:T(8,128)S(1)} %collective-permute-done.2.m0_ref, f32[200,128]{1,0:T(8,128)S(1)} %collective-permute-done.3.m1_ref, ...), custom_call_target="tpu_custom_call" | custom-call | tf_op jit(solution)/shard_map/edges/pallas_call | solution.py:497
Async XLA Ops:
  1.7 12.8 %collective-permute-start = (f32[88,128]{1,0:T(8,128)S(1)}, f32[88,128]{1,0:T(8,128)S(1)}, u32[]{:S(2)}, u32[]{:S(2)}) collective-permute-start(f32[88,128]{1,0:T(8,128)S(1)} %get-tuple-element.32), channel_id=1, source_target_pairs={{0,1},{1,0},{2,3},{3,2},{4,5},{5,4},{6,7},{7,6},{8,9},{9,8},{10,11... | collective-permute-start | bytes 135176 | tf_op jit(solution)/shard_map/ppermute | solution.py:545
  2.2 12.3 %collective-permute-start.1 = (f32[88,128]{1,0:T(8,128)S(1)}, f32[88,128]{1,0:T(8,128)S(1)}, u32[]{:S(2)}, u32[]{:S(2)}) collective-permute-start(f32[88,128]{1,0:T(8,128)S(1)} %get-tuple-element.33), channel_id=1, source_target_pairs={{1,2},{2,1},{3,4},{4,3},{5,6},{6,5},{7,255},{9,10},{10,9},{11,12},... | collective-permute-start | bytes 135176 | tf_op jit(solution)/shard_map/ppermute | solution.py:546
  14.8 10.6 %collective-permute-start.2 = (f32[200,128]{1,0:T(8,128)S(1)}, f32[200,128]{1,0:T(8,128)S(1)}, u32[]{:S(2)}, u32[]{:S(2)}) collective-permute-start(f32[200,128]{1,0:T(8,128)S(1)} %get-tuple-element.45), channel_id=1, source_target_pairs={{0,8},{1,9},{2,10},{3,11},{4,12},{5,13},{6,14},{7,15},{8,0},{9,1},... | collective-permute-start | bytes 307208 | tf_op jit(solution)/shard_map/ppermute | solution.py:549
  15.8 9.6 %collective-permute-start.3 = (f32[200,128]{1,0:T(8,128)S(1)}, f32[200,128]{1,0:T(8,128)S(1)}, u32[]{:S(2)}, u32[]{:S(2)}) collective-permute-start(f32[200,128]{1,0:T(8,128)S(1)} %get-tuple-element.46), channel_id=1, source_target_pairs={{0,248},{1,249},{2,250},{3,251},{4,252},{5,253},{6,254},{7,255},{8... | collective-permute-start | bytes 307208 | tf_op jit(solution)/shard_map/ppermute | solution.py:550

commit v2 on v1

--- a/solution.py
+++ b/solution.py
@@ -8,16 +8,16 @@
 from jax.sharding import PartitionSpec as P
 
 F32 = jnp.float32
+BF16 = jnp.bfloat16
 LEVELS = 8
 LANES = 128
 FIELDS = 5
 PLANES = FIELDS * LEVELS + 1
 ROW_MSG = 2 * FIELDS * LEVELS + 8
 BASE = 16
-CHUNKS = 4
-PACK_ROWS = 48
+PACK_ROWS = 96
 MAIN_ROWS = 96
-EDGE_CHUNKS = 1
+LAST_CHUNKS = 2
 
 time_step = 0.2
 viscosity = 0.5
@@ -49,6 +49,33 @@
 
 def gather(x, index):
     return jnp.take_along_axis(x, index, axis=1)
+
+
+def strip_layout(rows):
+    lane = lanes(rows)
+    return lane, lane // 16, lane % 16
+
+
+def own_strips(packed, rows):
+    _, level, slot = strip_layout(rows)
+    own = jnp.where(slot < 4, slot, jnp.where((slot >= 8) & (slot < 12), slot - 4, 0))
+    out = [gather(packed[f // 2], 8 * level + own + 64 * (f % 2)) for f in range(FIELDS)]
+    return out + [gather(packed[2], own + 64)]
+
+
+def split(x):
+    high = x.astype(BF16)
+    rest = x - high.astype(F32)
+    middle = rest.astype(BF16)
+    return high, middle, (rest - middle.astype(F32)).astype(BF16)
+
+
+def face_matrix():
+    row = lax.broadcasted_iota(jnp.int32, (LANES, LANES), 0)
+    step = lax.rem(row - lax.broadcasted_iota(jnp.int32, (LANES, LANES), 1) + LANES, LANES)
+    face = jnp.where(step < 2, 7.0, jnp.where((step == 2) | (step == LANES - 1), -1.0, 0.0))
+    slope = jnp.where(step == 1, 1.0, jnp.where(step == 0, -1.0, 0.0))
+    return jnp.concatenate([face, slope], axis=1).astype(BF16)
 
 
 def is_even(axis):
@@ -120,42 +147,42 @@
     return messages
 
 
-def column_pack_kernel(t_in, s_in, u_in, v_in, w_in, e_in, t, s, u, v, w, e, p, c_ref, m0_ref, m1_ref, wi, sems):
+def column_pack_kernel(t_in, s_in, u_in, v_in, w_in, e_in, t, s, u, v, w, e, p, c_ref, m0_ref, m1_ref, face, slope):
     rows = e_in.shape[0]
-    block = rows // CHUNKS
     even = is_even("lon")
-    fields = (t, s, u, v, w)
-    copies = []
-    for c in range(CHUNKS):
-        src, dst = pl.ds(c * block, block), pl.ds(BASE + c * block, block)
-        pairs = [(x.at[:, src, :], y.at[:, dst, :]) for x, y in ((t_in, t), (s_in, s), (u_in, u), (v_in, v))]
-        pairs += [(w_in.at[:, src, :], wi.at[:, src, :]), (e_in.at[src, :], e.at[dst, :])]
-        copies.append([pltpu.make_async_copy(x, y, sems.at[6 * c + n]) for n, (x, y) in enumerate(pairs)])
-        for x in copies[-1]:
-            x.start()
-    for c in range(CHUNKS):
-        for x in copies[c]:
-            x.wait()
-
-        def step(i, _):
-            out = pl.ds(pl.multiple_of(c * block + i * PACK_ROWS, 8), PACK_ROWS)
-            here = pl.ds(pl.multiple_of(BASE + c * block + i * PACK_ROWS, 8), PACK_ROWS)
+    matrix = face_matrix()
+
+    def step(i, _):
+        out = pl.ds(pl.multiple_of(i * PACK_ROWS, 8), PACK_ROWS)
+        here = pl.ds(pl.multiple_of(BASE + i * PACK_ROWS, 8), PACK_ROWS)
+        for x, y in ((t_in, t), (s_in, s), (u_in, u), (v_in, v), (w_in, w)):
             for k in range(LEVELS):
-                w[k, here, :] = wi[k, out, :].astype(F32)
-
-            def plane(q):
-                if q == PLANES - 1:
-                    return e[here, :]
-                return fields[q // LEVELS][q % LEVELS, here, :]
-
-            packed = pack_columns(plane, PACK_ROWS)
-            for n, x in enumerate(packed):
-                c_ref[out, n * LANES : (n + 1) * LANES] = x
-            m0_ref[out, :], m1_ref[out, :] = column_messages(packed, even, PACK_ROWS)
-            pressure(here, t, s, e, p)
-            return 0
-
-        lax.fori_loop(0, block // PACK_ROWS, step, 0)
+                y[k, here, :] = x[k, out, :].astype(F32)
+        e[here, :] = e_in[out, :]
+
+        def plane(q):
+            if q == PLANES - 1:
+                return e_in[out, :]
+            return (t_in, s_in, u_in, v_in, w_in)[q // LEVELS][q % LEVELS, out, :].astype(F32)
+
+        packed = pack_columns(plane, PACK_ROWS)
+        for n, x in enumerate(own_strips(packed, PACK_ROWS)):
+            c_ref[n, out, :] = x
+        m0_ref[out, :], m1_ref[out, :] = column_messages(packed, even, PACK_ROWS)
+        total = (gravity * 0.5 * time_step) * e_in[out, :]
+        for k in range(LEVELS):
+            h = density_half(t_in[k, out, :], s_in[k, out, :])
+            at = total + h
+            p[k, here, :] = at
+            total = at + h
+        for n, x in enumerate((t_in, s_in)):
+            for k in range(LEVELS):
+                both = sum(jnp.dot(part, matrix, preferred_element_type=F32) for part in split(x[k, out, :])[::-1])
+                face[n * LEVELS + k, out, :] = both[:, :LANES]
+                slope[n * LEVELS + k, out, :] = both[:, LANES:]
+        return 0
+
+    lax.fori_loop(0, rows // PACK_ROWS, step, 0)
 
 
 def column_pack(fields, surface):
@@ -164,14 +191,14 @@
     big = pltpu.VMEM((LEVELS, tall, LANES), F32)
     return pl.pallas_call(
         column_pack_kernel,
-        in_specs=[HBM] * 6,
-        out_specs=[VMEM] * 10,
+        in_specs=[VMEM] * 6,
+        out_specs=[VMEM] * 12,
         out_shape=[big] * 5
         + [pltpu.VMEM((tall, LANES), F32), big]
-        + [pltpu.VMEM((rows + 8, 3 * LANES), F32)]
-        + [pltpu.VMEM((rows + 8, LANES), F32)] * 2,
-        scratch_shapes=[pltpu.VMEM((LEVELS, rows, LANES), jnp.int32), pltpu.SemaphoreType.DMA((6 * CHUNKS,))],
-        compiler_params=params(57.5),
+        + [pltpu.VMEM((FIELDS + 1, rows + 8, LANES), F32)]
+        + [pltpu.VMEM((rows + 8, LANES), F32)] * 2
+        + [pltpu.VMEM((2 * LEVELS, rows, LANES), F32)] * 2,
+        compiler_params=params(16),
         cost_estimate=pl.CostEstimate(flops=10_000_000, bytes_accessed=6_000_000, transcendentals=0),
         name="column_pack",
     )(*fields, surface)
@@ -205,8 +232,8 @@
     g_ref[PLANES - 1] = jnp.where(row < 2, jnp.where(fold, folded, north), jnp.where(row >= 6, south, 0.0))
     packed = pack_columns(lambda q: g_ref[q], 8)
     last = pl.ds(rows, 8)
-    for n, c in enumerate(packed):
-        c_ref[last, n * LANES : (n + 1) * LANES] = c
+    for n, x in enumerate(own_strips(packed, 8)):
+        c_ref[n, last, :] = x
     m0_ref[last, :], m1_ref[last, :] = column_messages(packed, is_even("lon"), 8)
     for side in (pl.ds(BASE - 8, 8), pl.ds(BASE + rows, 8)):
         for f, x in enumerate((t, s, u, v, w)):
@@ -307,116 +334,70 @@
     return tr, out
 
 
-def main_kernel(t, s, u, v, w, e, p, t_out, s_out, u_out, v_out, h_out, me, mn, vel, gt, gs, hy):
-    rows = h_out.shape[0]
-
-    def loop(start, count, body):
-        if count == 1:
-            body(start)
-            return
-
-        def step(i, _):
-            body(pl.multiple_of(start + i * MAIN_ROWS, 8))
-            return 0
-
-        lax.fori_loop(0, count, step, 0)
-
-    def velocities(n, store):
-        def body(r):
-            here = pl.ds(r, n)
-            spin = coriolis_rows(r, n, rows)
-            trial = [velocity_trial(k, r, n, spin, u, v, w, p, me, mn) for k in range(LEVELS)]
-            at_floor = [trial[k][0] > (trial[k + 1][0] if k + 1 < LEVELS else 0.0) for k in range(LEVELS)]
-            u_floor, v_floor = trial[0][1], trial[0][2]
-            for k in range(1, LEVELS):
-                u_floor = jnp.where(at_floor[k], trial[k][1], u_floor)
-                v_floor = jnp.where(at_floor[k], trial[k][2], v_floor)
-            damp = damping(u_floor, v_floor)
-            for k in range(LEVELS):
-                factor = jnp.where(at_floor[k], damp, trial[k][0])
-                v_next = factor * trial[k][2]
-                vel[k, here, :] = v_next
-                if store:
-                    out = pl.ds(pl.multiple_of(r - BASE, 8), n)
-                    u_out[k, out, :] = factor * trial[k][1]
-                    v_out[k, out, :] = v_next
-
-        return body
-
-    def south_edge(r):
-        total = 0.0
+def velocity_kernel(u, v, w, p, un, vel, me, mn):
+    rows = un.shape[1]
+
+    def velocities(r, n, store):
+        here = pl.ds(r, n)
+        spin = coriolis_rows(r, n, rows)
+        trial = [velocity_trial(k, r, n, spin, u, v, w, p, me, mn) for k in range(LEVELS)]
+        at_floor = [trial[k][0] > (trial[k + 1][0] if k + 1 < LEVELS else 0.0) for k in range(LEVELS)]
+        u_floor, v_floor = trial[0][1], trial[0][2]
+        for k in range(1, LEVELS):
+            u_floor = jnp.where(at_floor[k], trial[k][1], u_floor)
+            v_floor = jnp.where(at_floor[k], trial[k][2], v_floor)
+        damp = damping(u_floor, v_floor)
         for k in range(LEVELS):
-            total = total + north_flux(k, r, 8, vel, mn, (t, s), (gt, gs))[0]
-        hy[pl.ds(r, 8), :] = total
-
-    def tracer(r):
-        n = MAIN_ROWS
-        here, down = pl.ds(r, n), pl.ds(r - 1, n)
-        out = pl.ds(pl.multiple_of(r - BASE, 8), n)
-        total_x = total_y = 0.0
-        for k in range(LEVELS):
-            tr_y, (gy_t, gy_s) = north_flux(k, r, n, vel, mn, (t, s), (gt, gs))
-            tr_x, ((tc, gx_t), (sc, gx_s)) = east_flux(k, r, n, u_out[k, out, :], me, (t, s))
-            total_x, total_y = total_x + tr_x, total_y + tr_y
-            wet = w[k, here, :]
-            t_out[k, out, :] = wet * (tc - (gx_t - west(gx_t) + (gy_t - gt[k, down, :])))
-            s_out[k, out, :] = wet * (sc - (gx_s - west(gx_s) + (gy_s - gs[k, down, :])))
-        hy[here, :] = total_y
-        h_out[out, :] = e[here, :] - HEIGHT * (total_x - west(total_x) + (total_y - hy[down, :]))
-
-    count = rows // MAIN_ROWS
-    loop(BASE - 8, 1, velocities(8, False))
-    loop(BASE + rows, 1, velocities(8, False))
-    loop(BASE, count, velocities(MAIN_ROWS, True))
-    south_edge(BASE - 8)
-    loop(BASE, count, tracer)
-
-
-def main(arrays, rows):
-    big = pltpu.VMEM(arrays[0].shape, F32)
-    out3 = pltpu.VMEM((LEVELS, rows, LANES), F32)
+            factor = jnp.where(at_floor[k], damp, trial[k][0])
+            vel[k, here, :] = factor * trial[k][2]
+            if store:
+                un[k, pl.ds(r - BASE, n), :] = factor * trial[k][1]
+
+    velocities(BASE - 8, 8, False)
+    velocities(BASE + rows, 8, False)
+
+    def step(i, _):
+        velocities(pl.multiple_of(BASE + i * MAIN_ROWS, 8), MAIN_ROWS, True)
+        return 0
+
+    lax.fori_loop(0, rows // MAIN_ROWS, step, 0)
+
+
+def new_velocities(u, v, w, p, rows):
+    big = pltpu.VMEM(u.shape, F32)
     return pl.pallas_call(
-        main_kernel,
-        in_specs=[VMEM] * 7,
-        out_specs=[VMEM] * 5,
-        out_shape=[out3] * 4 + [pltpu.VMEM((rows, LANES), F32)],
-        scratch_shapes=[big] * 5 + [pltpu.VMEM(arrays[5].shape, F32)],
+        velocity_kernel,
+        in_specs=[VMEM] * 4,
+        out_specs=[VMEM] * 4,
+        out_shape=[pltpu.VMEM((LEVELS, rows, LANES), F32), big, big, big],
         compiler_params=params(16),
-        cost_estimate=pl.CostEstimate(flops=40_000_000, bytes_accessed=8_000_000, transcendentals=100_000),
-        name="main",
-    )(*arrays)
-
-
-def edge_kernel(c_ref, m0_ref, m1_ref, t_in, s_in, u_in, v_in, h_in, t_hbm, s_hbm, u_hbm, v_hbm, h_hbm,
-                t, s, u, v, w, e, p, me, mn, un, vel, gt, gs, hy, ot, os, ou, ov, oh, sems):
-    rows = h_in.shape[0]
+        cost_estimate=pl.CostEstimate(flops=20_000_000, bytes_accessed=6_000_000, transcendentals=100_000),
+        name="velocities",
+    )(u, v, w, p)
+
+
+def last_kernel(c_ref, m0_ref, m1_ref, mt, ms, mw, mh, mu, mv, mme, mmn, mface, mslope, t_hbm, s_hbm, u_hbm, v_hbm, h_hbm,
+                t, s, u, v, w, e, p, me, mn, un, vel, gt, gs, hy, mgt, mgs, mhy, st, ss, sh, ot, os, ou, ov, oh, sems):
+    rows = oh.shape[0]
     even = is_even("lon")
 
-    def layout(n):
-        lane = lanes(n)
-        return lane, lane // 16, lane % 16
-
-    def spread(source, place, n):
-        lane, level, slot = layout(n)
-        own = jnp.where(slot < 4, slot, jnp.where((slot >= 8) & (slot < 12), slot - 4, 0))
-        other = jnp.where((slot == 5) | (slot == 7), 1, 0)
-        from_east = (slot == 4) | (slot == 5)
-        from_west = (slot == 6) | (slot == 7)
+    def complete(source, place, n):
+        lane, level, slot = strip_layout(n)
+        ghost = (slot >= 4) & (slot < 8)
         src, here = pl.ds(source, n), pl.ds(place, n)
         m0, m1 = m0_ref[src, :], m1_ref[src, :]
         m_east, m_west = jnp.where(even, m0, m1), jnp.where(even, m1, m0)
-
-        def strip(packed, own_lane, ghost_lane):
-            return jnp.where(
-                from_east,
-                gather(m_east, ghost_lane),
-                jnp.where(from_west, gather(m_west, ghost_lane), gather(packed, own_lane)),
-            )
-
-        for f, x in enumerate((t, s, u, v, w)):
-            packed = c_ref[src, (f // 2) * LANES : (f // 2 + 1) * LANES]
-            x[0, here, :] = strip(packed, 8 * level + own + 64 * (f % 2), 2 * level + other + 2 * LEVELS * f)
-        e[here, :] = strip(c_ref[src, 2 * LANES : 3 * LANES], own + 64, other + 2 * (PLANES - 1))
+        four = jnp.where(lane < 64, m_east, pltpu.roll(m_west, 64, 1))
+        rest = jnp.where(lane < 96, m_east, pltpu.roll(m_west, 32, 1))
+        at = jnp.where(slot % 2 == 1, 1, 0)
+        west_side = slot >= 6
+        for f, x in enumerate((t, s, u, v)):
+            other = gather(four, 2 * LEVELS * f + 2 * level + at + jnp.where(west_side, 64, 0))
+            x[0, here, :] = jnp.where(ghost, other, c_ref[f, src, :])
+        other = gather(rest, 64 + 2 * level + at + jnp.where(west_side, 32, 0))
+        w[0, here, :] = jnp.where(ghost, other, c_ref[FIELDS - 1, src, :])
+        other = gather(rest, 80 + at + jnp.where(west_side, 32, 0))
+        e[here, :] = jnp.where(ghost, other, c_ref[FIELDS, src, :])
 
     def strip_pressure(r, n):
         here = pl.ds(r, n)
@@ -427,7 +408,7 @@
             total = total + jnp.where(lane >= step, pltpu.roll(total, step, 1), 0.0)
         p[0, here, :] = (gravity * 0.5 * time_step) * e[here, :] + (2.0 * total - h)
 
-    def velocities(r, n):
+    def strip_velocities(r, n):
         here = pl.ds(r, n)
         lane = lanes(n)
         wet, u_trial, v_trial = velocity_trial(0, r, n, coriolis_rows(r, n, rows), u, v, w, p, me, mn)
@@ -436,78 +417,118 @@
         un[0, here, :] = factor * u_trial
         vel[0, here, :] = factor * v_trial
 
-    def joined(strip, slot):
+    def joined(strip):
+        slot = strip_layout(strip.shape[0])[2]
         return jnp.where(slot < 4, strip, pltpu.roll(strip, LANES - 4, 1))
 
-    def tracer(r, n):
-        lane, level, slot = layout(n)
-        edge = (lane < 2) | (lane >= LANES - 2)
+    def on_edge(n):
+        lane = lanes(n)
+        return (lane < 2) | (lane >= LANES - 2)
+
+    def placed(wide, k):
+        return pltpu.roll(wide, (-(16 * k + 4)) % LANES, 1)
+
+    def strip_tracers(r, n):
         here, down = pl.ds(r, n), pl.ds(r - 1, n)
         out = pl.ds(r - BASE, n)
-        u_next = un[0, here, :]
         tr_y, (gy_t, gy_s) = north_flux(0, r, n, vel, mn, (t, s), (gt, gs))
-        tr_x, ((tc, gx_t), (sc, gx_s)) = east_flux(0, r, n, u_next, me, (t, s))
+        tr_x, ((tc, gx_t), (sc, gx_s)) = east_flux(0, r, n, un[0, here, :], me, (t, s))
         wet = w[0, here, :]
         hy[here, :] = tr_y
-        strips = (
-            wet * (tc - (gx_t - west(gx_t) + (gy_t - gt[0, down, :]))),
-            wet * (sc - (gx_s - west(gx_s) + (gy_s - gs[0, down, :]))),
-            u_next,
-            vel[0, here, :],
-        )
-        for strip, main_in, out_ref in zip(strips, (t_in, s_in, u_in, v_in), (ot, os, ou, ov)):
-            wide = joined(strip, slot)
-            for k in range(LEVELS):
-                placed = pltpu.roll(wide, (-(16 * k + 4)) % LANES, 1)
-                out_ref[k, out, :] = jnp.where(edge, placed, main_in[k, out, :])
+        st[out, :] = joined(wet * (tc - (gx_t - west(gx_t) + (gy_t - gt[0, down, :]))))
+        ss[out, :] = joined(wet * (sc - (gx_s - west(gx_s) + (gy_s - gs[0, down, :]))))
         inflow = tr_x - west(tr_x) + (tr_y - hy[down, :])
         for step in (16, 32, 64):
             inflow = inflow + pltpu.roll(inflow, step, 1)
-        wide = joined(e[here, :] - HEIGHT * inflow, slot)
-        oh[out, :] = jnp.where(edge, pltpu.roll(wide, LANES - 4, 1), h_in[out, :])
-
-    spread(0, BASE, rows + 8)
+        sh[out, :] = joined(e[here, :] - HEIGHT * inflow)
+
+    def tracers(r, n):
+        here, down = pl.ds(r, n), pl.ds(r - 1, n)
+        out = pl.ds(r - BASE, n)
+        edge = on_edge(n)
+        wide_t, wide_s = st[out, :], ss[out, :]
+        total_x = total_y = 0.0
+        for k in range(LEVELS):
+            tr_y, (gy_t, gy_s) = north_flux(k, r, n, mv, mmn, (mt, ms), (mgt, mgs))
+            u_next = mu[k, out, :]
+            mask = mme[k, here, :]
+            tr_x = (FLUX * mask) * (u_next + east(u_next))
+            md = (time_step * diffusivity) * mask
+            gx_t = tr_x * mface[k, out, :] - md * mslope[k, out, :]
+            gx_s = tr_x * mface[LEVELS + k, out, :] - md * mslope[LEVELS + k, out, :]
+            tc, sc = mt[k, here, :], ms[k, here, :]
+            total_x, total_y = total_x + tr_x, total_y + tr_y
+            wet = mw[k, here, :]
+            t_next = wet * (tc - (gx_t - west(gx_t) + (gy_t - mgt[k, down, :])))
+            s_next = wet * (sc - (gx_s - west(gx_s) + (gy_s - mgs[k, down, :])))
+            ot[k, out, :] = jnp.where(edge, placed(wide_t, k), t_next)
+            os[k, out, :] = jnp.where(edge, placed(wide_s, k), s_next)
+        mhy[here, :] = total_y
+        height = mh[here, :] - HEIGHT * (total_x - west(total_x) + (total_y - mhy[down, :]))
+        oh[out, :] = jnp.where(edge, placed(sh[out, :], 0), height)
+
+    copies = []
+
+    def send(x, y):
+        copies.append(pltpu.make_async_copy(x, y, sems.at[len(copies)]))
+        copies[-1].start()
+
+    complete(0, BASE, rows + 8)
     strip_pressure(BASE, rows + 8)
     for x in (t, s, u, v, w, p):
         x[0, pl.ds(BASE - 8, 8), :] = x[0, pl.ds(BASE + rows, 8), :]
     e[pl.ds(BASE - 8, 8), :] = e[pl.ds(BASE + rows, 8), :]
-    velocities(BASE - 8, rows + 16)
-    hy[pl.ds(BASE - 8, 8), :] = north_flux(0, BASE - 8, 8, vel, mn, (t, s), (gt, gs))[0]
-    copies = []
-    block = rows // EDGE_CHUNKS
-    for c in range(EDGE_CHUNKS):
-        tracer(BASE + c * block, block)
+    strip_velocities(BASE - 8, rows + 16)
+    south = pl.ds(BASE - 8, 8)
+    hy[south, :] = north_flux(0, BASE - 8, 8, vel, mn, (t, s), (gt, gs))[0]
+    total = 0.0
+    for k in range(LEVELS):
+        total = total + north_flux(k, BASE - 8, 8, mv, mmn, (mt, ms), (mgt, mgs))[0]
+    mhy[south, :] = total
+    whole = pl.ds(BASE, rows)
+    edge = on_edge(rows)
+    wide_u, wide_v = joined(un[0, whole, :]), joined(vel[0, whole, :])
+    for k in range(LEVELS):
+        ou[k] = jnp.where(edge, placed(wide_u, k), mu[k])
+        ov[k] = jnp.where(edge, placed(wide_v, k), mv[k, whole, :])
+    send(ou, u_hbm)
+    send(ov, v_hbm)
+    strip_tracers(BASE, rows)
+    block = rows // LAST_CHUNKS
+    for c in range(LAST_CHUNKS):
+        tracers(BASE + c * block, block)
         at = pl.ds(c * block, block)
-        for n, (x, y) in enumerate(((ot, t_hbm), (os, s_hbm), (ou, u_hbm), (ov, v_hbm))):
-            copies.append(pltpu.make_async_copy(x.at[:, at, :], y.at[:, at, :], sems.at[c * 5 + n]))
-        copies.append(pltpu.make_async_copy(oh.at[at, :], h_hbm.at[at, :], sems.at[c * 5 + 4]))
-        for x in copies[-5:]:
-            x.start()
+        send(ot.at[:, at, :], t_hbm.at[:, at, :])
+        send(os.at[:, at, :], s_hbm.at[:, at, :])
+    send(oh, h_hbm)
     for x in copies:
         x.wait()
 
 
-def edges(c, m0, m1, outs):
-    rows = outs[4].shape[0]
-    tall = rows + BASE + 16
+def last(c, m0, m1, t, s, w, e, un, vel, me, mn, face, slope):
+    rows, tall = un.shape[1], t.shape[1]
     big = pltpu.VMEM((1, tall, LANES), F32)
     flat = pltpu.VMEM((tall, LANES), F32)
+    high = pltpu.VMEM((LEVELS, tall, LANES), F32)
+    short = pltpu.VMEM((rows, LANES), F32)
     out3 = jax.ShapeDtypeStruct((LEVELS, rows, LANES), F32)
     wide = pltpu.VMEM((LEVELS, rows, LANES), F32)
     return pl.pallas_call(
-        edge_kernel,
-        in_specs=[VMEM] * 8,
+        last_kernel,
+        in_specs=[VMEM] * 13,
         out_specs=[HBM] * 5,
         out_shape=[out3] * 4 + [jax.ShapeDtypeStruct((rows, LANES), F32)],
         scratch_shapes=[big] * 5
         + [flat]
         + [big] * 7
         + [flat]
+        + [high, high, flat]
+        + [short] * 3
         + [wide] * 4
-        + [pltpu.VMEM((rows, LANES), F32), pltpu.SemaphoreType.DMA((5 * EDGE_CHUNKS,))],
-        compiler_params=params(16),
-        name="edges",
-    )(c, m0, m1, *outs)
+        + [short, pltpu.SemaphoreType.DMA((3 + 2 * LAST_CHUNKS,))],
+        compiler_params=params(24),
+        name="last",
+    )(c, m0, m1, t, s, w, e, un, vel, me, mn, face, slope)
 
 
 def swaps():
@@ -544,12 +565,12 @@
     a, b = row_pack(fields, free_elevation)
     a = send(a, perm=lat_first)
     b = send(b, perm=lat_second)
-    arrays = column_pack(fields, free_elevation)
-    *arrays, c, m0, m1 = ghosts(a, b, arrays)
+    *arrays, face, slope = column_pack(fields, free_elevation)
+    t, s, u, v, w, e, p, c, m0, m1 = ghosts(a, b, arrays)
     m0 = send(m0, perm=lon_first)
     m1 = send(m1, perm=lon_second)
-    outs = main(arrays, free_elevation.shape[0])
-    return tuple(edges(c, m0, m1, outs))
+    un, vel, me, mn = new_velocities(u, v, w, p, free_elevation.shape[0])
+    return tuple(last(c, m0, m1, t, s, w, e, un, vel, me, mn, face, slope))
 
 
 def solution(mesh):

time: 29.8 us -> 28.3 us (0.950)
  Pallas kernels: 14.6 us -> 11.8 us
  starting transfers between devices: 14.4 us -> 15.5 us
    pallas_call x3, Pallas kernels: 13.2 us -> 10.3 us  [the longest x1 5.31 us: last(): pl.pallas_call(last_kernel, in_specs=[VMEM] * 13, out_specs=[HBM] * 5, ou...]
    ppermute x1, starting transfers between devices: 3.93 us -> 5.02 us  [on_device(): m1 = send(m1, perm=lon_second)]
  transfers between devices with their start and end apart: 4 -> 4, of which waited for: 0 -> 0; matrix products, arithmetic and copies ran while one was open for 0% -> 0% of each run, Pallas kernels for 30% -> 18%
where the time goes in v2:
time: 28.3 us; the launch traced here: 28.1 us
  starting transfers between devices  15.5 us (55%)
  Pallas kernels  11.8 us (42%)
  between operations  0.8 us (3%)
    ppermute x1, starting transfers between devices, on_device(): b = send(b, perm=lat_second)  8.94 us
    pallas_call x1, Pallas kernels, last(): pl.pallas_call(last_kernel, in_specs=[VMEM] * 13, out_specs=[HBM] * 5, ou...  5.31 us
    ppermute x1, starting transfers between devices, on_device(): m1 = send(m1, perm=lon_second)  5.02 us
    pallas_call x1, Pallas kernels, new_velocities(): pl.pallas_call(velocity_kernel, in_specs=[VMEM] * 4, out_specs=[VMEM] * 4...  2.8 us
    pallas_call x1, Pallas kernels, column_pack(): pl.pallas_call(column_pack_kernel, in_specs=[VMEM] * 6, out_specs=[VMEM]...  2.16 us
    pallas_call x1, Pallas kernels, row_pack(): pl.pallas_call(row_pack_kernel, in_specs=[HBM] * 6, out_specs=[VMEM] * 2,...  1.18 us
    ppermute x1, starting transfers between devices, on_device(): m0 = send(m0, perm=lon_first)  1.04 us
  transfers between devices with their start and end apart: 4, of which 0 were waited for; matrix products, arithmetic and copies ran while one was open for 0% of the time, Pallas kernels for 18%

profile of v2, /device:TPU:14, one launch (start us, length us, event | category | flops | bytes accessed | tf_op | source)
XLA Modules:
  0.0 28.1 jit_solution(6311913062194444135)
XLA Ops:
  0.6 0.0 copy-start.4
  0.6 0.0 copy-start.5
  0.7 0.0 copy-start.3
  0.7 0.0 copy-start.2
  0.7 0.0 copy-start.1
  0.7 0.0 copy-start
  0.7 1.2 %row_pack.1 = (f32[88,128]{1,0:T(8,128)S(1)}, f32[88,128]{1,0:T(8,128)S(1)}) custom-call(f32[8,192,128]{2,1,0:T(8,128)} %t_in.1, f32[8,192,128]{2,1,0:T(8,128)} %s_in.1, f32[8,192,128]{2,1,0:T(8,128)} %u_in.1, f32[8,192,128]{2,1,0:T(8,128)} %v_in.1, s32[8,192,128]{2,1,0:T(8,128)} %w_in.1, f32[192,128]{1,0:T(8,128)} %e_in.1), custom_call_target="tpu_custom_call" | custom-call | tf_op jit(solution)/shard_map/row_pack/pallas_call | solution.py:114
  1.9 0.5 %collective-permute-start = (f32[88,128]{1,0:T(8,128)S(1)}, f32[88,128]{1,0:T(8,128)S(1)}, u32[]{:S(2)}, u32[]{:S(2)}) collective-permute-start(f32[88,128]{1,0:T(8,128)S(1)} %get-tuple-element.33), channel_id=1, source_target_pairs={{0,1},{1,0},{2,3},{3,2},{4,5},{5,4},{6,7},{7,6},{8,9},{9,8},{10,11... | collective-permute-start | bytes 135176 | tf_op jit(solution)/shard_map/ppermute | solution.py:566
  2.4 8.9 %collective-permute-start.1 = (f32[88,128]{1,0:T(8,128)S(1)}, f32[88,128]{1,0:T(8,128)S(1)}, u32[]{:S(2)}, u32[]{:S(2)}) collective-permute-start(f32[88,128]{1,0:T(8,128)S(1)} %get-tuple-element.34), channel_id=1, source_target_pairs={{1,2},{2,1},{3,4},{4,3},{5,6},{6,5},{7,255},{9,10},{10,9},{11,12},... | collective-permute-start | bytes 135176 | tf_op jit(solution)/shard_map/ppermute | solution.py:567
  11.4 0.0 copy-done.4
  11.4 0.0 copy-done.5
  11.4 0.0 copy-done.3
  11.4 0.0 copy-done.2
  11.4 0.0 copy-done.1
  11.4 0.0 copy-done
  11.4 2.2 %column_pack.1 = (f32[8,224,128]{2,1,0:T(8,128)S(1)}, f32[8,224,128]{2,1,0:T(8,128)S(1)}, f32[8,224,128]{2,1,0:T(8,128)S(1)}, f32[8,224,128]{2,1,0:T(8,128)S(1)}...) custom-call(f32[8,192,128]{2,1,0:T(8,128)S(1)} %copy-done, ...), custom_call_target="tpu_custom_call" | custom-call | flops 10000000 | bytes 6000000 | tf_op jit(solution)/shard_map/column_pack/pallas_call | solution.py:192
  13.6 0.0 collective-permute-done.a_ref
  13.6 0.0 collective-permute-done.1.b_ref
  13.6 0.3 %ghosts.1 = (f32[8,224,128]{2,1,0:T(8,128)S(1)}, f32[8,224,128]{2,1,0:T(8,128)S(1)}, f32[8,224,128]{2,1,0:T(8,128)S(1)}, f32[8,224,128]{2,1,0:T(8,128)S(1)}, f32...) custom-call(f32[88,128]{1,0:T(8,128)S(1)} %collective-permute-done.a, ...), custom_call_target="tpu_custom_call", output_to_operand_aliasing={{0}: (2, {}), {1}: (3, {}), {2}: (4, {}), {3}: (5, {}), {4}... | custom-call | tf_op jit(solution)/shard_map/ghosts/pallas_call | solution.py:247
  13.9 1.0 %collective-permute-start.2 = (f32[200,128]{1,0:T(8,128)S(1)}, f32[200,128]{1,0:T(8,128)S(1)}, u32[]{:S(2)}, u32[]{:S(2)}) collective-permute-start(f32[200,128]{1,0:T(8,128)S(1)} %get-tuple-element.46), channel_id=1, source_target_pairs={{0,8},{1,9},{2,10},{3,11},{4,12},{5,13},{6,14},{7,15},{8,0},{9,1},... | collective-permute-start | bytes 307208 | tf_op jit(solution)/shard_map/ppermute | solution.py:570
  15.0 5.0 %collective-permute-start.3 = (f32[200,128]{1,0:T(8,128)S(1)}, f32[200,128]{1,0:T(8,128)S(1)}, u32[]{:S(2)}, u32[]{:S(2)}) collective-permute-start(f32[200,128]{1,0:T(8,128)S(1)} %get-tuple-element.47), channel_id=1, source_target_pairs={{0,248},{1,249},{2,250},{3,251},{4,252},{5,253},{6,254},{7,255},{8... | collective-permute-start | bytes 307208 | tf_op jit(solution)/shard_map/ppermute | solution.py:571
  20.0 2.8 %velocities.1 = (f32[8,192,128]{2,1,0:T(8,128)S(1)}, f32[8,224,128]{2,1,0:T(8,128)S(1)}, f32[8,224,128]{2,1,0:T(8,128)S(1)}, f32[8,224,128]{2,1,0:T(8,128)S(1)}) custom-call(f32[8,224,128]{2,1,0:T(8,128)S(1)} %get-tuple-element.52.u, f32[8,224,128]{2,1,0:T(8,128)S(1)} %get-tuple-element.53.v, f32[8,224,128]{2,1,0:T(8,128)S(1)} %get-tuple-element.50.w.mw, ...), custom_call_target="tpu_custom_call" | custom-call | flops 20000000 | bytes 6000000 | tf_op jit(solution)/shard_map/velocities/pallas_call | solution.py:368
  22.8 0.0 collective-permute-done.2.m0_ref
  22.8 0.0 collective-permute-done.3.m1_ref
  22.8 5.3 %last.1 = (f32[8,192,128]{2,1,0:T(8,128)}, f32[8,192,128]{2,1,0:T(8,128)}, f32[8,192,128]{2,1,0:T(8,128)}, f32[8,192,128]{2,1,0:T(8,128)}, f32[192,128]{1,0:T(8,128)}) custom-call(f32[6,200,128]{2,1,0:T(8,128)S(1)} %get-tuple-element.45.c_ref, f32[200,128]{1,0:T(8,128)S(1)} %collective-permute-done.2.m0_ref, f32[200,128]{1,0:T(8,128)S(1)} %collective-permute-done.3.m1_ref, ...), custom_call_target="tpu_custom_call" | custom-call | tf_op jit(solution)/shard_map/last/pallas_call | solution.py:516
Async XLA Ops:
  0.6 10.7 %copy-start.4 = (s32[8,192,128]{2,1,0:T(8,128)S(1)}, s32[8,192,128]{2,1,0:T(8,128)}, u32[]{:S(2)}) copy-start(s32[8,192,128]{2,1,0:T(8,128)} %w_in.1) | copy-start | bytes 2359300
  0.6 10.7 %copy-start.5 = (f32[192,128]{1,0:T(8,128)S(1)}, f32[192,128]{1,0:T(8,128)}, u32[]{:S(2)}) copy-start(f32[192,128]{1,0:T(8,128)} %e_in.1) | copy-start | bytes 294916
  0.7 10.7 %copy-start.3 = (f32[8,192,128]{2,1,0:T(8,128)S(1)}, f32[8,192,128]{2,1,0:T(8,128)}, u32[]{:S(2)}) copy-start(f32[8,192,128]{2,1,0:T(8,128)} %v_in.1) | copy-start | bytes 2359300
  0.7 10.7 %copy-start.2 = (f32[8,192,128]{2,1,0:T(8,128)S(1)}, f32[8,192,128]{2,1,0:T(8,128)}, u32[]{:S(2)}) copy-start(f32[8,192,128]{2,1,0:T(8,128)} %u_in.1) | copy-start | bytes 2359300
  0.7 10.7 %copy-start.1 = (f32[8,192,128]{2,1,0:T(8,128)S(1)}, f32[8,192,128]{2,1,0:T(8,128)}, u32[]{:S(2)}) copy-start(f32[8,192,128]{2,1,0:T(8,128)} %s_in.1) | copy-start | bytes 2359300
  0.7 10.7 %copy-start = (f32[8,192,128]{2,1,0:T(8,128)S(1)}, f32[8,192,128]{2,1,0:T(8,128)}, u32[]{:S(2)}) copy-start(f32[8,192,128]{2,1,0:T(8,128)} %t_in.1) | copy-start | bytes 2359300
  1.9 11.7 %collective-permute-start = (f32[88,128]{1,0:T(8,128)S(1)}, f32[88,128]{1,0:T(8,128)S(1)}, u32[]{:S(2)}, u32[]{:S(2)}) collective-permute-start(f32[88,128]{1,0:T(8,128)S(1)} %get-tuple-element.33), channel_id=1, source_target_pairs={{0,1},{1,0},{2,3},{3,2},{4,5},{5,4},{6,7},{7,6},{8,9},{9,8},{10,11... | collective-permute-start | bytes 135176 | tf_op jit(solution)/shard_map/ppermute | solution.py:566
  2.4 11.2 %collective-permute-start.1 = (f32[88,128]{1,0:T(8,128)S(1)}, f32[88,128]{1,0:T(8,128)S(1)}, u32[]{:S(2)}, u32[]{:S(2)}) collective-permute-start(f32[88,128]{1,0:T(8,128)S(1)} %get-tuple-element.34), channel_id=1, source_target_pairs={{1,2},{2,1},{3,4},{4,3},{5,6},{6,5},{7,255},{9,10},{10,9},{11,12},... | collective-permute-start | bytes 135176 | tf_op jit(solution)/shard_map/ppermute | solution.py:567
  13.9 8.9 %collective-permute-start.2 = (f32[200,128]{1,0:T(8,128)S(1)}, f32[200,128]{1,0:T(8,128)S(1)}, u32[]{:S(2)}, u32[]{:S(2)}) collective-permute-start(f32[200,128]{1,0:T(8,128)S(1)} %get-tuple-element.46), channel_id=1, source_target_pairs={{0,8},{1,9},{2,10},{3,11},{4,12},{5,13},{6,14},{7,15},{8,0},{9,1},... | collective-permute-start | bytes 307208 | tf_op jit(solution)/shard_map/ppermute | solution.py:570
  15.0 7.8 %collective-permute-start.3 = (f32[200,128]{1,0:T(8,128)S(1)}, f32[200,128]{1,0:T(8,128)S(1)}, u32[]{:S(2)}, u32[]{:S(2)}) collective-permute-start(f32[200,128]{1,0:T(8,128)S(1)} %get-tuple-element.47), channel_id=1, source_target_pairs={{0,248},{1,249},{2,250},{3,251},{4,252},{5,253},{6,254},{7,255},{8... | collective-permute-start | bytes 307208 | tf_op jit(solution)/shard_map/ppermute | solution.py:571

commit v3 on v2

--- a/solution.py
+++ b/solution.py
@@ -16,7 +16,7 @@
 ROW_MSG = 2 * FIELDS * LEVELS + 8
 BASE = 16
 PACK_ROWS = 96
-MAIN_ROWS = 96
+MAIN_ROWS = 192
 LAST_CHUNKS = 2
 
 time_step = 0.2
@@ -71,11 +71,35 @@
 
 
 def face_matrix():
-    row = lax.broadcasted_iota(jnp.int32, (LANES, LANES), 0)
-    step = lax.rem(row - lax.broadcasted_iota(jnp.int32, (LANES, LANES), 1) + LANES, LANES)
+    step = lane_step()
     face = jnp.where(step < 2, 7.0, jnp.where((step == 2) | (step == LANES - 1), -1.0, 0.0))
     slope = jnp.where(step == 1, 1.0, jnp.where(step == 0, -1.0, 0.0))
     return jnp.concatenate([face, slope], axis=1).astype(BF16)
+
+
+def product(x, matrix):
+    return sum(jnp.dot(part, matrix, preferred_element_type=F32) for part in split(x)[::-1])
+
+
+def lane_step():
+    row = lax.broadcasted_iota(jnp.int32, (LANES, LANES), 0)
+    return lax.rem(row - lax.broadcasted_iota(jnp.int32, (LANES, LANES), 1) + LANES, LANES)
+
+
+def neighbour_matrix():
+    step = lane_step()
+    return jnp.concatenate([jnp.where(step == 1, 1.0, 0.0), jnp.where(step == LANES - 1, 1.0, 0.0)], axis=1).astype(BF16)
+
+
+def difference_matrix():
+    step = lane_step()
+    return jnp.where(step == 1, 1.0, jnp.where(step == LANES - 1, -1.0, 0.0)).astype(BF16)
+
+
+def place_matrix(level):
+    lane, row = (lax.broadcasted_iota(jnp.int32, (LANES, LANES), n) for n in (1, 0))
+    slot = jnp.where(lane < 2, lane + 8, jnp.where(lane >= LANES - 2, lane - (LANES - 4), -LANES))
+    return jnp.where(row == 16 * level + slot, 1.0, 0.0).astype(BF16)
 
 
 def is_even(axis):
@@ -147,10 +171,12 @@
     return messages
 
 
-def column_pack_kernel(t_in, s_in, u_in, v_in, w_in, e_in, t, s, u, v, w, e, p, c_ref, m0_ref, m1_ref, face, slope):
+def column_pack_kernel(t_in, s_in, u_in, v_in, w_in, e_in, t, s, u, v, w, e, p, c_ref, m0_ref, m1_ref, face, slope, place):
     rows = e_in.shape[0]
     even = is_even("lon")
     matrix = face_matrix()
+    for k in range(LEVELS):
+        place[:, k * LANES : (k + 1) * LANES] = place_matrix(k)
 
     def step(i, _):
         out = pl.ds(pl.multiple_of(i * PACK_ROWS, 8), PACK_ROWS)
@@ -177,7 +203,7 @@
             total = at + h
         for n, x in enumerate((t_in, s_in)):
             for k in range(LEVELS):
-                both = sum(jnp.dot(part, matrix, preferred_element_type=F32) for part in split(x[k, out, :])[::-1])
+                both = product(x[k, out, :], matrix)
                 face[n * LEVELS + k, out, :] = both[:, :LANES]
                 slope[n * LEVELS + k, out, :] = both[:, LANES:]
         return 0
@@ -192,12 +218,13 @@
     return pl.pallas_call(
         column_pack_kernel,
         in_specs=[VMEM] * 6,
-        out_specs=[VMEM] * 12,
+        out_specs=[VMEM] * 13,
         out_shape=[big] * 5
         + [pltpu.VMEM((tall, LANES), F32), big]
         + [pltpu.VMEM((FIELDS + 1, rows + 8, LANES), F32)]
         + [pltpu.VMEM((rows + 8, LANES), F32)] * 2
-        + [pltpu.VMEM((2 * LEVELS, rows, LANES), F32)] * 2,
+        + [pltpu.VMEM((2 * LEVELS, rows, LANES), F32)] * 2
+        + [pltpu.VMEM((LANES, LEVELS * LANES), BF16)],
         compiler_params=params(16),
         cost_estimate=pl.CostEstimate(flops=10_000_000, bytes_accessed=6_000_000, transcendentals=0),
         name="column_pack",
@@ -277,11 +304,17 @@
     return (time_step * coriolis_max) * (2.0 * (row + 0.5) / total - 1.0)
 
 
-def velocity_trial(k, r, n, spin, u, v, w, p, m_east, m_north):
+def velocity_trial(k, r, n, spin, u, v, w, p, m_east, m_north, matrices=None):
     here, up, down = pl.ds(r, n), pl.ds(r + 1, n), pl.ds(r - 1, n)
     wet = w[k, here, :]
-    me = wet * east(wet)
-    mw = wet * west(wet)
+    pc = p[k, here, :]
+    if matrices is None:
+        wet_east, wet_west, slope = east(wet), west(wet), east(pc) - west(pc)
+    else:
+        both = jnp.dot(wet.astype(BF16), matrices[0], preferred_element_type=F32)
+        wet_east, wet_west, slope = both[:, :LANES], both[:, LANES:], product(pc, matrices[1])
+    me = wet * wet_east
+    mw = wet * wet_west
     mn = wet * w[k, up, :]
     ms = wet * w[k, down, :]
     m_east[k, here, :] = me
@@ -291,8 +324,7 @@
         return me * (east(q) - q) + mw * (west(q) - q) + (mn * (q_ref[k, up, :] - q) + ms * (q_ref[k, down, :] - q))
 
     un, vn = u[k, here, :], v[k, here, :]
-    pc = p[k, here, :]
-    u_trial = un + (spin * vn - (east(pc) - west(pc)) + (time_step * viscosity) * lap(u, un))
+    u_trial = un + (spin * vn - slope + (time_step * viscosity) * lap(u, un))
     v_trial = vn + ((time_step * viscosity) * lap(v, vn) - spin * un - (p[k, up, :] - p[k, down, :]))
     return wet, u_trial, v_trial
 
@@ -336,11 +368,13 @@
 
 def velocity_kernel(u, v, w, p, un, vel, me, mn):
     rows = un.shape[1]
+    matrices = neighbour_matrix(), difference_matrix()
 
     def velocities(r, n, store):
         here = pl.ds(r, n)
         spin = coriolis_rows(r, n, rows)
-        trial = [velocity_trial(k, r, n, spin, u, v, w, p, me, mn) for k in range(LEVELS)]
+        on_unit = matrices if n % 16 == 0 else None
+        trial = [velocity_trial(k, r, n, spin, u, v, w, p, me, mn, on_unit) for k in range(LEVELS)]
         at_floor = [trial[k][0] > (trial[k + 1][0] if k + 1 < LEVELS else 0.0) for k in range(LEVELS)]
         u_floor, v_floor = trial[0][1], trial[0][2]
         for k in range(1, LEVELS):
@@ -376,7 +410,7 @@
     )(u, v, w, p)
 
 
-def last_kernel(c_ref, m0_ref, m1_ref, mt, ms, mw, mh, mu, mv, mme, mmn, mface, mslope, t_hbm, s_hbm, u_hbm, v_hbm, h_hbm,
+def last_kernel(c_ref, m0_ref, m1_ref, mt, ms, mw, mh, mu, mv, mme, mmn, mface, mslope, place, t_hbm, s_hbm, u_hbm, v_hbm, h_hbm,
                 t, s, u, v, w, e, p, me, mn, un, vel, gt, gs, hy, mgt, mgs, mhy, st, ss, sh, ot, os, ou, ov, oh, sems):
     rows = oh.shape[0]
     even = is_even("lon")
@@ -417,16 +451,16 @@
         un[0, here, :] = factor * u_trial
         vel[0, here, :] = factor * v_trial
 
-    def joined(strip):
-        slot = strip_layout(strip.shape[0])[2]
-        return jnp.where(slot < 4, strip, pltpu.roll(strip, LANES - 4, 1))
-
     def on_edge(n):
         lane = lanes(n)
         return (lane < 2) | (lane >= LANES - 2)
 
-    def placed(wide, k):
-        return pltpu.roll(wide, (-(16 * k + 4)) % LANES, 1)
+    def placed(strip, levels=LEVELS):
+        out = []
+        for k in range(0, levels, 2):
+            both = product(strip, place[:, k * LANES : (k + 2) * LANES])
+            out += [both[:, :LANES], both[:, LANES:]]
+        return out
 
     def strip_tracers(r, n):
         here, down = pl.ds(r, n), pl.ds(r - 1, n)
@@ -435,18 +469,18 @@
         tr_x, ((tc, gx_t), (sc, gx_s)) = east_flux(0, r, n, un[0, here, :], me, (t, s))
         wet = w[0, here, :]
         hy[here, :] = tr_y
-        st[out, :] = joined(wet * (tc - (gx_t - west(gx_t) + (gy_t - gt[0, down, :]))))
-        ss[out, :] = joined(wet * (sc - (gx_s - west(gx_s) + (gy_s - gs[0, down, :]))))
+        st[out, :] = wet * (tc - (gx_t - west(gx_t) + (gy_t - gt[0, down, :])))
+        ss[out, :] = wet * (sc - (gx_s - west(gx_s) + (gy_s - gs[0, down, :])))
         inflow = tr_x - west(tr_x) + (tr_y - hy[down, :])
         for step in (16, 32, 64):
             inflow = inflow + pltpu.roll(inflow, step, 1)
-        sh[out, :] = joined(e[here, :] - HEIGHT * inflow)
+        sh[out, :] = e[here, :] - HEIGHT * inflow
 
     def tracers(r, n):
         here, down = pl.ds(r, n), pl.ds(r - 1, n)
         out = pl.ds(r - BASE, n)
         edge = on_edge(n)
-        wide_t, wide_s = st[out, :], ss[out, :]
+        wide_t, wide_s = placed(st[out, :]), placed(ss[out, :])
         total_x = total_y = 0.0
         for k in range(LEVELS):
             tr_y, (gy_t, gy_s) = north_flux(k, r, n, mv, mmn, (mt, ms), (mgt, mgs))
@@ -461,11 +495,11 @@
             wet = mw[k, here, :]
             t_next = wet * (tc - (gx_t - west(gx_t) + (gy_t - mgt[k, down, :])))
             s_next = wet * (sc - (gx_s - west(gx_s) + (gy_s - mgs[k, down, :])))
-            ot[k, out, :] = jnp.where(edge, placed(wide_t, k), t_next)
-            os[k, out, :] = jnp.where(edge, placed(wide_s, k), s_next)
+            ot[k, out, :] = jnp.where(edge, wide_t[k], t_next)
+            os[k, out, :] = jnp.where(edge, wide_s[k], s_next)
         mhy[here, :] = total_y
         height = mh[here, :] - HEIGHT * (total_x - west(total_x) + (total_y - mhy[down, :]))
-        oh[out, :] = jnp.where(edge, placed(sh[out, :], 0), height)
+        oh[out, :] = jnp.where(edge, placed(sh[out, :], 2)[0], height)
 
     copies = []
 
@@ -487,10 +521,10 @@
     mhy[south, :] = total
     whole = pl.ds(BASE, rows)
     edge = on_edge(rows)
-    wide_u, wide_v = joined(un[0, whole, :]), joined(vel[0, whole, :])
+    wide_u, wide_v = placed(un[0, whole, :]), placed(vel[0, whole, :])
     for k in range(LEVELS):
-        ou[k] = jnp.where(edge, placed(wide_u, k), mu[k])
-        ov[k] = jnp.where(edge, placed(wide_v, k), mv[k, whole, :])
+        ou[k] = jnp.where(edge, wide_u[k], mu[k])
+        ov[k] = jnp.where(edge, wide_v[k], mv[k, whole, :])
     send(ou, u_hbm)
     send(ov, v_hbm)
     strip_tracers(BASE, rows)
@@ -505,7 +539,7 @@
         x.wait()
 
 
-def last(c, m0, m1, t, s, w, e, un, vel, me, mn, face, slope):
+def last(c, m0, m1, t, s, w, e, un, vel, me, mn, face, slope, place):
     rows, tall = un.shape[1], t.shape[1]
     big = pltpu.VMEM((1, tall, LANES), F32)
     flat = pltpu.VMEM((tall, LANES), F32)
@@ -515,7 +549,7 @@
     wide = pltpu.VMEM((LEVELS, rows, LANES), F32)
     return pl.pallas_call(
         last_kernel,
-        in_specs=[VMEM] * 13,
+        in_specs=[VMEM] * 14,
         out_specs=[HBM] * 5,
         out_shape=[out3] * 4 + [jax.ShapeDtypeStruct((rows, LANES), F32)],
         scratch_shapes=[big] * 5
@@ -528,7 +562,7 @@
         + [short, pltpu.SemaphoreType.DMA((3 + 2 * LAST_CHUNKS,))],
         compiler_params=params(24),
         name="last",
-    )(c, m0, m1, t, s, w, e, un, vel, me, mn, face, slope)
+    )(c, m0, m1, t, s, w, e, un, vel, me, mn, face, slope, place)
 
 
 def swaps():
@@ -565,12 +599,12 @@
     a, b = row_pack(fields, free_elevation)
     a = send(a, perm=lat_first)
     b = send(b, perm=lat_second)
-    *arrays, face, slope = column_pack(fields, free_elevation)
+    *arrays, face, slope, place = column_pack(fields, free_elevation)
     t, s, u, v, w, e, p, c, m0, m1 = ghosts(a, b, arrays)
     m0 = send(m0, perm=lon_first)
     m1 = send(m1, perm=lon_second)
     un, vel, me, mn = new_velocities(u, v, w, p, free_elevation.shape[0])
-    return tuple(last(c, m0, m1, t, s, w, e, un, vel, me, mn, face, slope))
+    return tuple(last(c, m0, m1, t, s, w, e, un, vel, me, mn, face, slope, place))
 
 
 def solution(mesh):

time: 28.3 us -> 27.4 us (0.968)
  Pallas kernels: 11.8 us -> 10.4 us
  waiting for transfers between devices: 0.01 us -> 0.57 us
    pallas_call x1, Pallas kernels: 5.31 us -> 4.59 us  [last(): pl.pallas_call(last_kernel, in_specs=[VMEM] * 14, out_specs=[HBM] * 5, ou...]
    pallas_call x1, Pallas kernels: 2.8 us -> 2.15 us  [new_velocities(): pl.pallas_call(velocity_kernel, in_specs=[VMEM] * 4, out_specs=[VMEM] * 4...]
    ppermute x1, waiting for transfers between devices: 0.01 us -> 0.56 us  [on_device(): m1 = send(m1, perm=lon_second)]
  transfers between devices with their start and end apart: 4 -> 4, of which waited for: 0 -> 1; matrix products, arithmetic and copies ran while one was open for 0% -> 0% of each run, Pallas kernels for 18% -> 16%
where the time goes in v3:
time: 27.4 us; the launch traced here: 27.3 us
  starting transfers between devices  15.5 us (57%)
  Pallas kernels  10.4 us (38%)
  between operations  0.79 us (3%)
  waiting for transfers between devices  0.57 us (2%)
    ppermute x1, starting transfers between devices, on_device(): b = send(b, perm=lat_second)  8.94 us
    ppermute x1, starting transfers between devices, on_device(): m1 = send(m1, perm=lon_second)  4.98 us
    pallas_call x1, Pallas kernels, last(): pl.pallas_call(last_kernel, in_specs=[VMEM] * 14, out_specs=[HBM] * 5, ou...  4.59 us
    pallas_call x1, Pallas kernels, column_pack(): pl.pallas_call(column_pack_kernel, in_specs=[VMEM] * 6, out_specs=[VMEM]...  2.22 us
    pallas_call x1, Pallas kernels, new_velocities(): pl.pallas_call(velocity_kernel, in_specs=[VMEM] * 4, out_specs=[VMEM] * 4...  2.15 us
    pallas_call x1, Pallas kernels, row_pack(): pl.pallas_call(row_pack_kernel, in_specs=[HBM] * 6, out_specs=[VMEM] * 2,...  1.18 us
    ppermute x1, starting transfers between devices, on_device(): m0 = send(m0, perm=lon_first)  1.03 us
    ppermute x1, waiting for transfers between devices, on_device(): m1 = send(m1, perm=lon_second)  0.56 us
  transfers between devices with their start and end apart: 4, of which 1 were waited for; matrix products, arithmetic and copies ran while one was open for 0% of the time, Pallas kernels for 16%

profile of v3, /device:TPU:14, one launch (start us, length us, event | category | flops | bytes accessed | tf_op | source)
XLA Modules:
  0.0 27.3 jit_solution(2923351697237748837)
XLA Ops:
  0.6 0.0 copy-start.4
  0.6 0.0 copy-start.5
  0.7 0.0 copy-start.3
  0.7 0.0 copy-start.2
  0.7 0.0 copy-start.1
  0.7 0.0 copy-start
  0.7 1.2 %row_pack.1 = (f32[88,128]{1,0:T(8,128)S(1)}, f32[88,128]{1,0:T(8,128)S(1)}) custom-call(f32[8,192,128]{2,1,0:T(8,128)} %t_in.1, f32[8,192,128]{2,1,0:T(8,128)} %s_in.1, f32[8,192,128]{2,1,0:T(8,128)} %u_in.1, f32[8,192,128]{2,1,0:T(8,128)} %v_in.1, s32[8,192,128]{2,1,0:T(8,128)} %w_in.1, f32[192,128]{1,0:T(8,128)} %e_in.1), custom_call_target="tpu_custom_call" | custom-call | tf_op jit(solution)/shard_map/row_pack/pallas_call | solution.py:138
  1.9 0.5 %collective-permute-start = (f32[88,128]{1,0:T(8,128)S(1)}, f32[88,128]{1,0:T(8,128)S(1)}, u32[]{:S(2)}, u32[]{:S(2)}) collective-permute-start(f32[88,128]{1,0:T(8,128)S(1)} %get-tuple-element.34), channel_id=1, source_target_pairs={{0,1},{1,0},{2,3},{3,2},{4,5},{5,4},{6,7},{7,6},{8,9},{9,8},{10,11... | collective-permute-start | bytes 135176 | tf_op jit(solution)/shard_map/ppermute | solution.py:600
  2.4 8.9 %collective-permute-start.1 = (f32[88,128]{1,0:T(8,128)S(1)}, f32[88,128]{1,0:T(8,128)S(1)}, u32[]{:S(2)}, u32[]{:S(2)}) collective-permute-start(f32[88,128]{1,0:T(8,128)S(1)} %get-tuple-element.35), channel_id=1, source_target_pairs={{1,2},{2,1},{3,4},{4,3},{5,6},{6,5},{7,255},{9,10},{10,9},{11,12},... | collective-permute-start | bytes 135176 | tf_op jit(solution)/shard_map/ppermute | solution.py:601
  11.4 0.0 copy-done.4
  11.4 0.0 copy-done.5
  11.4 0.0 copy-done.3
  11.4 0.0 copy-done.2
  11.4 0.0 copy-done.1
  11.4 0.0 copy-done
  11.4 2.2 %column_pack.1 = (f32[8,224,128]{2,1,0:T(8,128)S(1)}, f32[8,224,128]{2,1,0:T(8,128)S(1)}, f32[8,224,128]{2,1,0:T(8,128)S(1)}, f32[8,224,128]{2,1,0:T(8,128)S(1)}...) custom-call(f32[8,192,128]{2,1,0:T(8,128)S(1)} %copy-done, ...), custom_call_target="tpu_custom_call" | custom-call | flops 10000000 | bytes 6000000 | tf_op jit(solution)/shard_map/column_pack/pallas_call | solution.py:218
  13.6 0.0 collective-permute-done.a_ref
  13.7 0.0 collective-permute-done.1.b_ref
  13.7 0.3 %ghosts.1 = (f32[8,224,128]{2,1,0:T(8,128)S(1)}, f32[8,224,128]{2,1,0:T(8,128)S(1)}, f32[8,224,128]{2,1,0:T(8,128)S(1)}, f32[8,224,128]{2,1,0:T(8,128)S(1)}, f32...) custom-call(f32[88,128]{1,0:T(8,128)S(1)} %collective-permute-done.a, ...), custom_call_target="tpu_custom_call", output_to_operand_aliasing={{0}: (2, {}), {1}: (3, {}), {2}: (4, {}), {3}: (5, {}), {4}... | custom-call | tf_op jit(solution)/shard_map/ghosts/pallas_call | solution.py:274
  14.0 1.0 %collective-permute-start.2 = (f32[200,128]{1,0:T(8,128)S(1)}, f32[200,128]{1,0:T(8,128)S(1)}, u32[]{:S(2)}, u32[]{:S(2)}) collective-permute-start(f32[200,128]{1,0:T(8,128)S(1)} %get-tuple-element.47), channel_id=1, source_target_pairs={{0,8},{1,9},{2,10},{3,11},{4,12},{5,13},{6,14},{7,15},{8,0},{9,1},... | collective-permute-start | bytes 307208 | tf_op jit(solution)/shard_map/ppermute | solution.py:604
  15.0 5.0 %collective-permute-start.3 = (f32[200,128]{1,0:T(8,128)S(1)}, f32[200,128]{1,0:T(8,128)S(1)}, u32[]{:S(2)}, u32[]{:S(2)}) collective-permute-start(f32[200,128]{1,0:T(8,128)S(1)} %get-tuple-element.48), channel_id=1, source_target_pairs={{0,248},{1,249},{2,250},{3,251},{4,252},{5,253},{6,254},{7,255},{8... | collective-permute-start | bytes 307208 | tf_op jit(solution)/shard_map/ppermute | solution.py:605
  20.0 2.1 %velocities.1 = (f32[8,192,128]{2,1,0:T(8,128)S(1)}, f32[8,224,128]{2,1,0:T(8,128)S(1)}, f32[8,224,128]{2,1,0:T(8,128)S(1)}, f32[8,224,128]{2,1,0:T(8,128)S(1)}) custom-call(f32[8,224,128]{2,1,0:T(8,128)S(1)} %get-tuple-element.53.u, f32[8,224,128]{2,1,0:T(8,128)S(1)} %get-tuple-element.54.v, f32[8,224,128]{2,1,0:T(8,128)S(1)} %get-tuple-element.51.w.mw, ...), custom_call_target="tpu_custom_call" | custom-call | flops 20000000 | bytes 6000000 | tf_op jit(solution)/shard_map/velocities/pallas_call | solution.py:402
  22.1 0.0 collective-permute-done.2.m0_ref
  22.2 0.6 %collective-permute-done.3.m1_ref = f32[200,128]{1,0:T(8,128)S(1)} collective-permute-done((f32[200,128]{1,0:T(8,128)S(1)}, f32[200,128]{1,0:T(8,128)S(1)}, u32[]{:S(2)}, u32[]{:S(2)}) %collective-permute-start.3) | collective-permute-done | bytes 102432 | tf_op jit(solution)/shard_map/ppermute | solution.py:605
  22.7 4.6 %last.1 = (f32[8,192,128]{2,1,0:T(8,128)}, f32[8,192,128]{2,1,0:T(8,128)}, f32[8,192,128]{2,1,0:T(8,128)}, f32[8,192,128]{2,1,0:T(8,128)}, f32[192,128]{1,0:T(8,128)}) custom-call(f32[6,200,128]{2,1,0:T(8,128)S(1)} %get-tuple-element.46.c_ref, f32[200,128]{1,0:T(8,128)S(1)} %collective-permute-done.2.m0_ref, f32[200,128]{1,0:T(8,128)S(1)} %collective-permute-done.3.m1_ref, ...), custom_call_target="tpu_custom_call" | custom-call | tf_op jit(solution)/shard_map/last/pallas_call | solution.py:550
Async XLA Ops:
  0.6 10.7 %copy-start.4 = (s32[8,192,128]{2,1,0:T(8,128)S(1)}, s32[8,192,128]{2,1,0:T(8,128)}, u32[]{:S(2)}) copy-start(s32[8,192,128]{2,1,0:T(8,128)} %w_in.1) | copy-start | bytes 2359300
  0.6 10.7 %copy-start.5 = (f32[192,128]{1,0:T(8,128)S(1)}, f32[192,128]{1,0:T(8,128)}, u32[]{:S(2)}) copy-start(f32[192,128]{1,0:T(8,128)} %e_in.1) | copy-start | bytes 294916
  0.7 10.7 %copy-start.3 = (f32[8,192,128]{2,1,0:T(8,128)S(1)}, f32[8,192,128]{2,1,0:T(8,128)}, u32[]{:S(2)}) copy-start(f32[8,192,128]{2,1,0:T(8,128)} %v_in.1) | copy-start | bytes 2359300
  0.7 10.7 %copy-start.2 = (f32[8,192,128]{2,1,0:T(8,128)S(1)}, f32[8,192,128]{2,1,0:T(8,128)}, u32[]{:S(2)}) copy-start(f32[8,192,128]{2,1,0:T(8,128)} %u_in.1) | copy-start | bytes 2359300
  0.7 10.7 %copy-start.1 = (f32[8,192,128]{2,1,0:T(8,128)S(1)}, f32[8,192,128]{2,1,0:T(8,128)}, u32[]{:S(2)}) copy-start(f32[8,192,128]{2,1,0:T(8,128)} %s_in.1) | copy-start | bytes 2359300
  0.7 10.7 %copy-start = (f32[8,192,128]{2,1,0:T(8,128)S(1)}, f32[8,192,128]{2,1,0:T(8,128)}, u32[]{:S(2)}) copy-start(f32[8,192,128]{2,1,0:T(8,128)} %t_in.1) | copy-start | bytes 2359300
  1.9 11.8 %collective-permute-start = (f32[88,128]{1,0:T(8,128)S(1)}, f32[88,128]{1,0:T(8,128)S(1)}, u32[]{:S(2)}, u32[]{:S(2)}) collective-permute-start(f32[88,128]{1,0:T(8,128)S(1)} %get-tuple-element.34), channel_id=1, source_target_pairs={{0,1},{1,0},{2,3},{3,2},{4,5},{5,4},{6,7},{7,6},{8,9},{9,8},{10,11... | collective-permute-start | bytes 135176 | tf_op jit(solution)/shard_map/ppermute | solution.py:600
  2.4 11.2 %collective-permute-start.1 = (f32[88,128]{1,0:T(8,128)S(1)}, f32[88,128]{1,0:T(8,128)S(1)}, u32[]{:S(2)}, u32[]{:S(2)}) collective-permute-start(f32[88,128]{1,0:T(8,128)S(1)} %get-tuple-element.35), channel_id=1, source_target_pairs={{1,2},{2,1},{3,4},{4,3},{5,6},{6,5},{7,255},{9,10},{10,9},{11,12},... | collective-permute-start | bytes 135176 | tf_op jit(solution)/shard_map/ppermute | solution.py:601
  14.0 8.2 %collective-permute-start.2 = (f32[200,128]{1,0:T(8,128)S(1)}, f32[200,128]{1,0:T(8,128)S(1)}, u32[]{:S(2)}, u32[]{:S(2)}) collective-permute-start(f32[200,128]{1,0:T(8,128)S(1)} %get-tuple-element.47), channel_id=1, source_target_pairs={{0,8},{1,9},{2,10},{3,11},{4,12},{5,13},{6,14},{7,15},{8,0},{9,1},... | collective-permute-start | bytes 307208 | tf_op jit(solution)/shard_map/ppermute | solution.py:604
  15.0 7.7 %collective-permute-start.3 = (f32[200,128]{1,0:T(8,128)S(1)}, f32[200,128]{1,0:T(8,128)S(1)}, u32[]{:S(2)}, u32[]{:S(2)}) collective-permute-start(f32[200,128]{1,0:T(8,128)S(1)} %get-tuple-element.48), channel_id=1, source_target_pairs={{0,248},{1,249},{2,250},{3,251},{4,252},{5,253},{6,254},{7,255},{8... | collective-permute-start | bytes 307208 | tf_op jit(solution)/shard_map/ppermute | solution.py:605

commit v4 on v3

--- a/solution.py
+++ b/solution.py
@@ -16,6 +16,8 @@
 ROW_MSG = 2 * FIELDS * LEVELS + 8
 BASE = 16
 PACK_ROWS = 96
+REST_ROWS = 32
+REST_LANES = 2 * LEVELS + 2
 MAIN_ROWS = 192
 LAST_CHUNKS = 2
 
@@ -171,7 +173,25 @@
     return messages
 
 
-def column_pack_kernel(t_in, s_in, u_in, v_in, w_in, e_in, t, s, u, v, w, e, p, c_ref, m0_ref, m1_ref, face, slope, place):
+def message_rows(rows):
+    half = (rows + 8 + 15) // 16 * 8
+    return half, half + REST_ROWS
+
+
+def compact(message, rows):
+    half, _ = message_rows(rows)
+    lane = lanes(half)
+    second = jnp.concatenate([message[half:rows, :], jnp.zeros((2 * half - rows, LANES), F32)], axis=0)
+    main = jnp.where(lane < 64, message[:half, :], pltpu.roll(second, 64, 1))
+    lane = lanes(REST_ROWS)
+    rest = jnp.zeros((REST_ROWS, LANES), F32)
+    for g in range(rows // REST_ROWS):
+        part = pltpu.roll(message[g * REST_ROWS : (g + 1) * REST_ROWS, :], (REST_LANES * g - 64) % LANES, 1)
+        rest = jnp.where((lane >= REST_LANES * g) & (lane < REST_LANES * (g + 1)), part, rest)
+    return main, rest
+
+
+def column_pack_kernel(t_in, s_in, u_in, v_in, w_in, e_in, t, s, u, v, w, e, p, c_ref, m0_ref, m1_ref, face, slope, place, m0_wide, m1_wide):
     rows = e_in.shape[0]
     even = is_even("lon")
     matrix = face_matrix()
@@ -194,7 +214,7 @@
         packed = pack_columns(plane, PACK_ROWS)
         for n, x in enumerate(own_strips(packed, PACK_ROWS)):
             c_ref[n, out, :] = x
-        m0_ref[out, :], m1_ref[out, :] = column_messages(packed, even, PACK_ROWS)
+        m0_wide[out, :], m1_wide[out, :] = column_messages(packed, even, PACK_ROWS)
         total = (gravity * 0.5 * time_step) * e_in[out, :]
         for k in range(LEVELS):
             h = density_half(t_in[k, out, :], s_in[k, out, :])
@@ -209,6 +229,11 @@
         return 0
 
     lax.fori_loop(0, rows // PACK_ROWS, step, 0)
+    half, _ = message_rows(rows)
+    for wide, out in ((m0_wide, m0_ref), (m1_wide, m1_ref)):
+        main, rest = compact(wide[...], rows)
+        out[:half, :] = main
+        out[half:, :] = rest
 
 
 def column_pack(fields, surface):
@@ -222,9 +247,10 @@
         out_shape=[big] * 5
         + [pltpu.VMEM((tall, LANES), F32), big]
         + [pltpu.VMEM((FIELDS + 1, rows + 8, LANES), F32)]
-        + [pltpu.VMEM((rows + 8, LANES), F32)] * 2
+        + [pltpu.VMEM((message_rows(rows)[1], LANES), F32)] * 2
         + [pltpu.VMEM((2 * LEVELS, rows, LANES), F32)] * 2
         + [pltpu.VMEM((LANES, LEVELS * LANES), BF16)],
+        scratch_shapes=[pltpu.VMEM((rows, LANES), F32)] * 2,
         compiler_params=params(16),
         cost_estimate=pl.CostEstimate(flops=10_000_000, bytes_accessed=6_000_000, transcendentals=0),
         name="column_pack",
@@ -233,16 +259,18 @@
 
 def ghost_kernel(a_ref, b_ref, *refs):
     t, s, u, v, w, e, p, c_ref, m0_ref, m1_ref, g_ref = refs[10:]
-    rows = m0_ref.shape[0] - 8
+    rows = c_ref.shape[1] - 8
     even = is_even("lat")
     fold = lax.axis_index("lat") == lax.axis_size("lat") - 1
     mirror = LANES - 1 - lanes()
     flat = g_ref.reshape(PLANES * 8, LANES)
     g_ref[...] = jnp.zeros_like(g_ref)
 
+    southmost = lax.axis_index("lat") == 0
+
     def both(start):
         a, b = a_ref[pl.ds(start, 8), :], b_ref[pl.ds(start, 8), :]
-        return jnp.where(even, a, b), jnp.where(even, b, a)
+        return jnp.where(even, a, b), jnp.where(southmost, 0.0, jnp.where(even, b, a))
 
     for f in range(FIELDS):
         sign = -1.0 if f in (2, 3) else 1.0
@@ -261,7 +289,15 @@
     last = pl.ds(rows, 8)
     for n, x in enumerate(own_strips(packed, 8)):
         c_ref[n, last, :] = x
-    m0_ref[last, :], m1_ref[last, :] = column_messages(packed, is_even("lon"), 8)
+    half, _ = message_rows(rows)
+    lane = lanes()
+    first = REST_LANES * (rows // REST_ROWS)
+    for out, message in zip((m0_ref, m1_ref), column_messages(packed, is_even("lon"), 8)):
+        place = pl.ds(rows - half, 8)
+        out[place, :] = jnp.where(lane < 64, out[place, :], pltpu.roll(message, 64, 1))
+        place = pl.ds(half, 8)
+        moved = pltpu.roll(message, (first - 64) % LANES, 1)
+        out[place, :] = jnp.where((lane >= first) & (lane < first + REST_LANES), moved, out[place, :])
     for side in (pl.ds(BASE - 8, 8), pl.ds(BASE + rows, 8)):
         for f, x in enumerate((t, s, u, v, w)):
             for k in range(LEVELS):
@@ -415,23 +451,36 @@
     rows = oh.shape[0]
     even = is_even("lon")
 
-    def complete(source, place, n):
-        lane, level, slot = strip_layout(n)
-        ghost = (slot >= 4) & (slot < 8)
-        src, here = pl.ds(source, n), pl.ds(place, n)
-        m0, m1 = m0_ref[src, :], m1_ref[src, :]
+    def complete():
+        n = rows + 8
+        half, _ = message_rows(rows)
+        m0, m1 = m0_ref[...], m1_ref[...]
         m_east, m_west = jnp.where(even, m0, m1), jnp.where(even, m1, m0)
-        four = jnp.where(lane < 64, m_east, pltpu.roll(m_west, 64, 1))
-        rest = jnp.where(lane < 96, m_east, pltpu.roll(m_west, 32, 1))
-        at = jnp.where(slot % 2 == 1, 1, 0)
-        west_side = slot >= 6
+        low = jnp.where(lanes(half) < 64, m_east[:half, :], pltpu.roll(m_west[:half, :], 64, 1))
+        high = jnp.where(lanes(n - half) < 64, pltpu.roll(m_east[: n - half, :], 64, 1), m_west[: n - half, :])
+        four = jnp.concatenate([low, high], axis=0)
+        rest_east, rest_west = m_east[half:, :], pltpu.roll(m_west[half:, :], 64, 1)
+
+        def slots(count):
+            _, level, slot = strip_layout(count)
+            west_side = jnp.where(slot >= 6, 64, 0)
+            return level, (slot >= 4) & (slot < 8), west_side + jnp.where(slot % 2 == 1, 1, 0)
+
+        level, ghost, at = slots(n)
+        here = pl.ds(BASE, n)
         for f, x in enumerate((t, s, u, v)):
-            other = gather(four, 2 * LEVELS * f + 2 * level + at + jnp.where(west_side, 64, 0))
-            x[0, here, :] = jnp.where(ghost, other, c_ref[f, src, :])
-        other = gather(rest, 64 + 2 * level + at + jnp.where(west_side, 32, 0))
-        w[0, here, :] = jnp.where(ghost, other, c_ref[FIELDS - 1, src, :])
-        other = gather(rest, 80 + at + jnp.where(west_side, 32, 0))
-        e[here, :] = jnp.where(ghost, other, c_ref[FIELDS, src, :])
+            x[0, here, :] = jnp.where(ghost, gather(four, 2 * LEVELS * f + 2 * level + at), c_ref[f])
+        for g in range(-(-n // REST_ROWS)):
+            count = min(REST_ROWS, n - g * REST_ROWS)
+            level, ghost, at = slots(count)
+            lane = lanes(count)
+            mine = (lane >= REST_LANES * g) & (lane < REST_LANES * (g + 1))
+            rest = jnp.where(mine, rest_east[:count, :], rest_west[:count, :])
+            src, dst = pl.ds(g * REST_ROWS, count), pl.ds(BASE + g * REST_ROWS, count)
+            index = (REST_LANES * g + 2 * level + at) % LANES
+            w[0, dst, :] = jnp.where(ghost, gather(rest, index), c_ref[FIELDS - 1, src, :])
+            index = (REST_LANES * g + 2 * LEVELS + at) % LANES
+            e[dst, :] = jnp.where(ghost, gather(rest, index), c_ref[FIELDS, src, :])
 
     def strip_pressure(r, n):
         here = pl.ds(r, n)
@@ -507,7 +556,7 @@
         copies.append(pltpu.make_async_copy(x, y, sems.at[len(copies)]))
         copies[-1].start()
 
-    complete(0, BASE, rows + 8)
+    complete()
     strip_pressure(BASE, rows + 8)
     for x in (t, s, u, v, w, p):
         x[0, pl.ds(BASE - 8, 8), :] = x[0, pl.ds(BASE + rows, 8), :]
@@ -579,6 +628,8 @@
                 lat_second.append((device(o, a), device(lon - 1 - o, a)))
             elif a > 0:
                 lat_second.append((device(o, a), device(o, a + 1 if a % 2 else a - 1)))
+            else:
+                lat_second.append((device(o, a), device(o ^ 1, a)))
             lon_first.append((device(o, a), device(o ^ 1, a)))
             lon_second.append((device(o, a), device(o + 1 if o % 2 else o - 1, a)))
     return lat_first, lat_second, lon_first, lon_second

time: 27.4 us -> 25.2 us (0.920)
  starting transfers between devices: 15.5 us -> 13.5 us
  waiting for transfers between devices: 0.57 us -> 0.29 us
    ppermute x1, starting transfers between devices: 8.94 us -> 7.04 us  [on_device(): b = send(b, perm=lat_second)]
  transfers between devices with their start and end apart: 4 -> 4, of which waited for: 1 -> 1; matrix products, arithmetic and copies ran while one was open for 0% -> 0% of each run, Pallas kernels for 16% -> 18%
where the time goes in v4:
time: 25.2 us; the launch traced here: 25.1 us
  starting transfers between devices  13.5 us (54%)
  Pallas kernels  10.6 us (42%)
  between operations  0.75 us (3%)
  waiting for transfers between devices  0.29 us (1%)
    ppermute x1, starting transfers between devices, on_device(): b = send(b, perm=lat_second)  7.04 us
    ppermute x1, starting transfers between devices, on_device(): m1 = send(m1, perm=lon_second)  4.9 us
    pallas_call x1, Pallas kernels, last(): pl.pallas_call(last_kernel, in_specs=[VMEM] * 14, out_specs=[HBM] * 5, ou...  4.57 us
    pallas_call x1, Pallas kernels, column_pack(): pl.pallas_call(column_pack_kernel, in_specs=[VMEM] * 6, out_specs=[VMEM]...  2.33 us
    pallas_call x1, Pallas kernels, new_velocities(): pl.pallas_call(velocity_kernel, in_specs=[VMEM] * 4, out_specs=[VMEM] * 4...  2.15 us
    pallas_call x1, Pallas kernels, row_pack(): pl.pallas_call(row_pack_kernel, in_specs=[HBM] * 6, out_specs=[VMEM] * 2,...  1.18 us
    ppermute x1, starting transfers between devices, on_device(): m0 = send(m0, perm=lon_first)  1 us
    ppermute x1, starting transfers between devices, on_device(): a = send(a, perm=lat_first)  0.54 us
  transfers between devices with their start and end apart: 4, of which 1 were waited for; matrix products, arithmetic and copies ran while one was open for 0% of the time, Pallas kernels for 18%

profile of v4, /device:TPU:14, one launch (start us, length us, event | category | flops | bytes accessed | tf_op | source)
XLA Modules:
  0.0 25.1 jit_solution(2829635035603480958)
XLA Ops:
  0.6 0.0 copy-start.4
  0.6 0.0 copy-start.5
  0.7 0.0 copy-start.3
  0.7 0.0 copy-start.2
  0.7 0.0 copy-start.1
  0.7 0.0 copy-start
  0.7 1.2 %row_pack.1 = (f32[88,128]{1,0:T(8,128)S(1)}, f32[88,128]{1,0:T(8,128)S(1)}) custom-call(f32[8,192,128]{2,1,0:T(8,128)} %t_in.1, f32[8,192,128]{2,1,0:T(8,128)} %s_in.1, f32[8,192,128]{2,1,0:T(8,128)} %u_in.1, f32[8,192,128]{2,1,0:T(8,128)} %v_in.1, s32[8,192,128]{2,1,0:T(8,128)} %w_in.1, f32[192,128]{1,0:T(8,128)} %e_in.1), custom_call_target="tpu_custom_call" | custom-call | tf_op jit(solution)/shard_map/row_pack/pallas_call | solution.py:140
  1.9 0.5 %collective-permute-start = (f32[88,128]{1,0:T(8,128)S(1)}, f32[88,128]{1,0:T(8,128)S(1)}, u32[]{:S(2)}, u32[]{:S(2)}) collective-permute-start(f32[88,128]{1,0:T(8,128)S(1)} %get-tuple-element.34), channel_id=1, source_target_pairs={{0,1},{1,0},{2,3},{3,2},{4,5},{5,4},{6,7},{7,6},{8,9},{9,8},{10,11... | collective-permute-start | bytes 135176 | tf_op jit(solution)/shard_map/ppermute | solution.py:651
  2.4 7.0 %collective-permute-start.1 = (f32[88,128]{1,0:T(8,128)S(1)}, f32[88,128]{1,0:T(8,128)S(1)}, u32[]{:S(2)}, u32[]{:S(2)}) collective-permute-start(f32[88,128]{1,0:T(8,128)S(1)} %get-tuple-element.35), channel_id=1, source_target_pairs={{0,8},{1,2},{2,1},{3,4},{4,3},{5,6},{6,5},{7,255},{8,0},{9,10},{10... | collective-permute-start | bytes 135176 | tf_op jit(solution)/shard_map/ppermute | solution.py:652
  9.5 0.0 copy-done.4
  9.5 0.0 copy-done.5
  9.5 0.0 copy-done.3
  9.5 0.0 copy-done.2
  9.5 0.0 copy-done.1
  9.5 0.0 copy-done
  9.5 2.3 %column_pack.1 = (f32[8,224,128]{2,1,0:T(8,128)S(1)}, f32[8,224,128]{2,1,0:T(8,128)S(1)}, f32[8,224,128]{2,1,0:T(8,128)S(1)}, f32[8,224,128]{2,1,0:T(8,128)S(1)}...) custom-call(f32[8,192,128]{2,1,0:T(8,128)S(1)} %copy-done, ...), custom_call_target="tpu_custom_call" | custom-call | flops 10000000 | bytes 6000000 | tf_op jit(solution)/shard_map/column_pack/pallas_call | solution.py:243
  11.8 0.0 collective-permute-done.a_ref
  11.8 0.0 collective-permute-done.1.b_ref
  11.9 0.4 %ghosts.1 = (f32[8,224,128]{2,1,0:T(8,128)S(1)}, f32[8,224,128]{2,1,0:T(8,128)S(1)}, f32[8,224,128]{2,1,0:T(8,128)S(1)}, f32[8,224,128]{2,1,0:T(8,128)S(1)}, f32...) custom-call(f32[88,128]{1,0:T(8,128)S(1)} %collective-permute-done.a, ...), custom_call_target="tpu_custom_call", output_to_operand_aliasing={{0}: (2, {}), {1}: (3, {}), {2}: (4, {}), {3}: (5, {}), {4}... | custom-call | tf_op jit(solution)/shard_map/ghosts/pallas_call | solution.py:310
  12.2 1.0 %collective-permute-start.2 = (f32[136,128]{1,0:T(8,128)S(1)}, f32[136,128]{1,0:T(8,128)S(1)}, u32[]{:S(2)}, u32[]{:S(2)}) collective-permute-start(f32[136,128]{1,0:T(8,128)S(1)} %get-tuple-element.47), channel_id=1, source_target_pairs={{0,8},{1,9},{2,10},{3,11},{4,12},{5,13},{6,14},{7,15},{8,0},{9,1},... | collective-permute-start | bytes 208904 | tf_op jit(solution)/shard_map/ppermute | solution.py:655
  13.2 4.9 %collective-permute-start.3 = (f32[136,128]{1,0:T(8,128)S(1)}, f32[136,128]{1,0:T(8,128)S(1)}, u32[]{:S(2)}, u32[]{:S(2)}) collective-permute-start(f32[136,128]{1,0:T(8,128)S(1)} %get-tuple-element.48), channel_id=1, source_target_pairs={{0,248},{1,249},{2,250},{3,251},{4,252},{5,253},{6,254},{7,255},{8... | collective-permute-start | bytes 208904 | tf_op jit(solution)/shard_map/ppermute | solution.py:656
  18.1 2.1 %velocities.1 = (f32[8,192,128]{2,1,0:T(8,128)S(1)}, f32[8,224,128]{2,1,0:T(8,128)S(1)}, f32[8,224,128]{2,1,0:T(8,128)S(1)}, f32[8,224,128]{2,1,0:T(8,128)S(1)}) custom-call(f32[8,224,128]{2,1,0:T(8,128)S(1)} %get-tuple-element.53.u, f32[8,224,128]{2,1,0:T(8,128)S(1)} %get-tuple-element.54.v, f32[8,224,128]{2,1,0:T(8,128)S(1)} %get-tuple-element.51.w.mw, ...), custom_call_target="tpu_custom_call" | custom-call | flops 20000000 | bytes 6000000 | tf_op jit(solution)/shard_map/velocities/pallas_call | solution.py:438
  20.3 0.0 collective-permute-done.2.m0_ref
  20.3 0.3 %collective-permute-done.3.m1_ref = f32[136,128]{1,0:T(8,128)S(1)} collective-permute-done((f32[136,128]{1,0:T(8,128)S(1)}, f32[136,128]{1,0:T(8,128)S(1)}, u32[]{:S(2)}, u32[]{:S(2)}) %collective-permute-start.3) | collective-permute-done | bytes 69664 | tf_op jit(solution)/shard_map/ppermute | solution.py:656
  20.6 4.6 %last.1 = (f32[8,192,128]{2,1,0:T(8,128)}, f32[8,192,128]{2,1,0:T(8,128)}, f32[8,192,128]{2,1,0:T(8,128)}, f32[8,192,128]{2,1,0:T(8,128)}, f32[192,128]{1,0:T(8,128)}) custom-call(f32[6,200,128]{2,1,0:T(8,128)S(1)} %get-tuple-element.46.c_ref, f32[136,128]{1,0:T(8,128)S(1)} %collective-permute-done.2.m0_ref, f32[136,128]{1,0:T(8,128)S(1)} %collective-permute-done.3.m1_ref, ...), custom_call_target="tpu_custom_call" | custom-call | tf_op jit(solution)/shard_map/last/pallas_call | solution.py:599
Async XLA Ops:
  0.6 8.8 %copy-start.4 = (s32[8,192,128]{2,1,0:T(8,128)S(1)}, s32[8,192,128]{2,1,0:T(8,128)}, u32[]{:S(2)}) copy-start(s32[8,192,128]{2,1,0:T(8,128)} %w_in.1) | copy-start | bytes 2359300
  0.6 8.8 %copy-start.5 = (f32[192,128]{1,0:T(8,128)S(1)}, f32[192,128]{1,0:T(8,128)}, u32[]{:S(2)}) copy-start(f32[192,128]{1,0:T(8,128)} %e_in.1) | copy-start | bytes 294916
  0.7 8.8 %copy-start.3 = (f32[8,192,128]{2,1,0:T(8,128)S(1)}, f32[8,192,128]{2,1,0:T(8,128)}, u32[]{:S(2)}) copy-start(f32[8,192,128]{2,1,0:T(8,128)} %v_in.1) | copy-start | bytes 2359300
  0.7 8.8 %copy-start.2 = (f32[8,192,128]{2,1,0:T(8,128)S(1)}, f32[8,192,128]{2,1,0:T(8,128)}, u32[]{:S(2)}) copy-start(f32[8,192,128]{2,1,0:T(8,128)} %u_in.1) | copy-start | bytes 2359300
  0.7 8.8 %copy-start.1 = (f32[8,192,128]{2,1,0:T(8,128)S(1)}, f32[8,192,128]{2,1,0:T(8,128)}, u32[]{:S(2)}) copy-start(f32[8,192,128]{2,1,0:T(8,128)} %s_in.1) | copy-start | bytes 2359300
  0.7 8.8 %copy-start = (f32[8,192,128]{2,1,0:T(8,128)S(1)}, f32[8,192,128]{2,1,0:T(8,128)}, u32[]{:S(2)}) copy-start(f32[8,192,128]{2,1,0:T(8,128)} %t_in.1) | copy-start | bytes 2359300
  1.9 10.0 %collective-permute-start = (f32[88,128]{1,0:T(8,128)S(1)}, f32[88,128]{1,0:T(8,128)S(1)}, u32[]{:S(2)}, u32[]{:S(2)}) collective-permute-start(f32[88,128]{1,0:T(8,128)S(1)} %get-tuple-element.34), channel_id=1, source_target_pairs={{0,1},{1,0},{2,3},{3,2},{4,5},{5,4},{6,7},{7,6},{8,9},{9,8},{10,11... | collective-permute-start | bytes 135176 | tf_op jit(solution)/shard_map/ppermute | solution.py:651
  2.4 9.4 %collective-permute-start.1 = (f32[88,128]{1,0:T(8,128)S(1)}, f32[88,128]{1,0:T(8,128)S(1)}, u32[]{:S(2)}, u32[]{:S(2)}) collective-permute-start(f32[88,128]{1,0:T(8,128)S(1)} %get-tuple-element.35), channel_id=1, source_target_pairs={{0,8},{1,2},{2,1},{3,4},{4,3},{5,6},{6,5},{7,255},{8,0},{9,10},{10... | collective-permute-start | bytes 135176 | tf_op jit(solution)/shard_map/ppermute | solution.py:652
  12.2 8.1 %collective-permute-start.2 = (f32[136,128]{1,0:T(8,128)S(1)}, f32[136,128]{1,0:T(8,128)S(1)}, u32[]{:S(2)}, u32[]{:S(2)}) collective-permute-start(f32[136,128]{1,0:T(8,128)S(1)} %get-tuple-element.47), channel_id=1, source_target_pairs={{0,8},{1,9},{2,10},{3,11},{4,12},{5,13},{6,14},{7,15},{8,0},{9,1},... | collective-permute-start | bytes 208904 | tf_op jit(solution)/shard_map/ppermute | solution.py:655
  13.2 7.3 %collective-permute-start.3 = (f32[136,128]{1,0:T(8,128)S(1)}, f32[136,128]{1,0:T(8,128)S(1)}, u32[]{:S(2)}, u32[]{:S(2)}) collective-permute-start(f32[136,128]{1,0:T(8,128)S(1)} %get-tuple-element.48), channel_id=1, source_target_pairs={{0,248},{1,249},{2,250},{3,251},{4,252},{5,253},{6,254},{7,255},{8... | collective-permute-start | bytes 208904 | tf_op jit(solution)/shard_map/ppermute | solution.py:656

commit v5 on v4

--- a/solution.py
+++ b/solution.py
@@ -18,8 +18,7 @@
 PACK_ROWS = 96
 REST_ROWS = 32
 REST_LANES = 2 * LEVELS + 2
-MAIN_ROWS = 192
-LAST_CHUNKS = 2
+MAIN_BLOCKS = 1
 
 time_step = 0.2
 viscosity = 0.5
@@ -258,7 +257,9 @@
 
 
 def ghost_kernel(a_ref, b_ref, *refs):
-    t, s, u, v, w, e, p, c_ref, m0_ref, m1_ref, g_ref = refs[10:]
+    face, slope = refs[10:12]
+    t, s, u, v, w, e, p, c_ref, m0_ref, m1_ref = refs[12:22]
+    outs, g_ref, scratch = refs[22:27], refs[27], refs[28:]
     rows = c_ref.shape[1] - 8
     even = is_even("lat")
     fold = lax.axis_index("lat") == lax.axis_size("lat") - 1
@@ -305,18 +306,23 @@
         e[side, :] = g_ref[PLANES - 1]
         pressure(side, t, s, e, p)
 
-
-def ghosts(a, b, arrays):
+    @pl.when(waits_for_seam())
+    def _():
+        interior(t, s, u, v, w, e, p, face, slope, *outs, *scratch)
+
+
+def ghosts(a, b, arrays, face, slope):
+    rows, tall = face.shape[1], arrays[0].shape[1]
     return pl.pallas_call(
         ghost_kernel,
-        in_specs=[VMEM] * 12,
-        out_specs=[VMEM] * 10,
-        out_shape=[pltpu.VMEM(x.shape, F32) for x in arrays],
-        scratch_shapes=[pltpu.VMEM((PLANES, 8, LANES), F32)],
+        in_specs=[VMEM] * 14,
+        out_specs=[VMEM] * 15,
+        out_shape=[pltpu.VMEM(x.shape, F32) for x in arrays] + interior_outputs(rows),
+        scratch_shapes=[pltpu.VMEM((PLANES, 8, LANES), F32)] + interior_scratch(tall),
         input_output_aliases={n + 2: n for n in range(10)},
-        compiler_params=params(8),
+        compiler_params=params(16),
         name="ghosts",
-    )(a, b, *arrays)
+    )(a, b, *arrays, face, slope)
 
 
 def density_half(t, s):
@@ -402,8 +408,8 @@
     return tr, out
 
 
-def velocity_kernel(u, v, w, p, un, vel, me, mn):
-    rows = un.shape[1]
+def interior(t, s, u, v, w, e, p, face, slope, t_out, s_out, u_out, v_out, h_out, me, mn, vel, gt, gs, hy):
+    rows = h_out.shape[0]
     matrices = neighbour_matrix(), difference_matrix()
 
     def velocities(r, n, store):
@@ -419,35 +425,81 @@
         damp = damping(u_floor, v_floor)
         for k in range(LEVELS):
             factor = jnp.where(at_floor[k], damp, trial[k][0])
-            vel[k, here, :] = factor * trial[k][2]
+            v_next = factor * trial[k][2]
+            vel[k, here, :] = v_next
             if store:
-                un[k, pl.ds(r - BASE, n), :] = factor * trial[k][1]
+                out = pl.ds(r - BASE, n)
+                u_out[k, out, :] = factor * trial[k][1]
+                v_out[k, out, :] = v_next
+
+    def tracers(r, n):
+        here, down = pl.ds(r, n), pl.ds(r - 1, n)
+        out = pl.ds(r - BASE, n)
+        total_x = total_y = 0.0
+        for k in range(LEVELS):
+            tr_y, (gy_t, gy_s) = north_flux(k, r, n, vel, mn, (t, s), (gt, gs))
+            u_next = u_out[k, out, :]
+            mask = me[k, here, :]
+            tr_x = (FLUX * mask) * (u_next + east(u_next))
+            md = (time_step * diffusivity) * mask
+            gx_t = tr_x * face[k, out, :] - md * slope[k, out, :]
+            gx_s = tr_x * face[LEVELS + k, out, :] - md * slope[LEVELS + k, out, :]
+            total_x, total_y = total_x + tr_x, total_y + tr_y
+            wet = w[k, here, :]
+            t_out[k, out, :] = wet * (t[k, here, :] - (gx_t - west(gx_t) + (gy_t - gt[k, down, :])))
+            s_out[k, out, :] = wet * (s[k, here, :] - (gx_s - west(gx_s) + (gy_s - gs[k, down, :])))
+        hy[here, :] = total_y
+        h_out[out, :] = e[here, :] - HEIGHT * (total_x - west(total_x) + (total_y - hy[down, :]))
 
     velocities(BASE - 8, 8, False)
     velocities(BASE + rows, 8, False)
-
-    def step(i, _):
-        velocities(pl.multiple_of(BASE + i * MAIN_ROWS, 8), MAIN_ROWS, True)
-        return 0
-
-    lax.fori_loop(0, rows // MAIN_ROWS, step, 0)
-
-
-def new_velocities(u, v, w, p, rows):
-    big = pltpu.VMEM(u.shape, F32)
+    velocities(BASE, rows, True)
+    total = 0.0
+    for k in range(LEVELS):
+        total = total + north_flux(k, BASE - 8, 8, vel, mn, (t, s), (gt, gs))[0]
+    hy[pl.ds(BASE - 8, 8), :] = total
+    block = rows // MAIN_BLOCKS
+    for n in range(MAIN_BLOCKS):
+        tracers(BASE + n * block, block)
+
+
+def interior_outputs(rows):
+    return [pltpu.VMEM((LEVELS, rows, LANES), F32)] * 4 + [pltpu.VMEM((rows, LANES), F32)]
+
+
+def interior_scratch(tall):
+    return [pltpu.VMEM((LEVELS, tall, LANES), F32)] * 5 + [pltpu.VMEM((tall, LANES), F32)]
+
+
+def waits_for_seam():
+    return lax.axis_index("lon") == 0
+
+
+def main_kernel(*refs):
+    ins, outs, scratch = refs[:9], refs[14:19], refs[19:]
+
+    @pl.when(jnp.logical_not(waits_for_seam()))
+    def _():
+        interior(*ins, *outs, *scratch)
+
+
+def main(arrays, outs):
+    rows, tall = outs[4].shape[0], arrays[0].shape[1]
     return pl.pallas_call(
-        velocity_kernel,
-        in_specs=[VMEM] * 4,
-        out_specs=[VMEM] * 4,
-        out_shape=[pltpu.VMEM((LEVELS, rows, LANES), F32), big, big, big],
+        main_kernel,
+        in_specs=[VMEM] * 14,
+        out_specs=[VMEM] * 5,
+        out_shape=interior_outputs(rows),
+        scratch_shapes=interior_scratch(tall),
+        input_output_aliases={n + 9: n for n in range(5)},
         compiler_params=params(16),
-        cost_estimate=pl.CostEstimate(flops=20_000_000, bytes_accessed=6_000_000, transcendentals=100_000),
-        name="velocities",
-    )(u, v, w, p)
-
-
-def last_kernel(c_ref, m0_ref, m1_ref, mt, ms, mw, mh, mu, mv, mme, mmn, mface, mslope, place, t_hbm, s_hbm, u_hbm, v_hbm, h_hbm,
-                t, s, u, v, w, e, p, me, mn, un, vel, gt, gs, hy, mgt, mgs, mhy, st, ss, sh, ot, os, ou, ov, oh, sems):
+        cost_estimate=pl.CostEstimate(flops=40_000_000, bytes_accessed=8_000_000, transcendentals=100_000),
+        name="main",
+    )(*arrays, *outs)
+
+
+def last_kernel(c_ref, m0_ref, m1_ref, place, mt, ms, mu, mv, mh, t_hbm, s_hbm, u_hbm, v_hbm, h_hbm,
+                t, s, u, v, w, e, p, me, mn, un, vel, gt, gs, hy, st, ss, sh, ot, os, ou, ov, oh, sems):
     rows = oh.shape[0]
     even = is_even("lon")
 
@@ -525,31 +577,6 @@
             inflow = inflow + pltpu.roll(inflow, step, 1)
         sh[out, :] = e[here, :] - HEIGHT * inflow
 
-    def tracers(r, n):
-        here, down = pl.ds(r, n), pl.ds(r - 1, n)
-        out = pl.ds(r - BASE, n)
-        edge = on_edge(n)
-        wide_t, wide_s = placed(st[out, :]), placed(ss[out, :])
-        total_x = total_y = 0.0
-        for k in range(LEVELS):
-            tr_y, (gy_t, gy_s) = north_flux(k, r, n, mv, mmn, (mt, ms), (mgt, mgs))
-            u_next = mu[k, out, :]
-            mask = mme[k, here, :]
-            tr_x = (FLUX * mask) * (u_next + east(u_next))
-            md = (time_step * diffusivity) * mask
-            gx_t = tr_x * mface[k, out, :] - md * mslope[k, out, :]
-            gx_s = tr_x * mface[LEVELS + k, out, :] - md * mslope[LEVELS + k, out, :]
-            tc, sc = mt[k, here, :], ms[k, here, :]
-            total_x, total_y = total_x + tr_x, total_y + tr_y
-            wet = mw[k, here, :]
-            t_next = wet * (tc - (gx_t - west(gx_t) + (gy_t - mgt[k, down, :])))
-            s_next = wet * (sc - (gx_s - west(gx_s) + (gy_s - mgs[k, down, :])))
-            ot[k, out, :] = jnp.where(edge, wide_t[k], t_next)
-            os[k, out, :] = jnp.where(edge, wide_s[k], s_next)
-        mhy[here, :] = total_y
-        height = mh[here, :] - HEIGHT * (total_x - west(total_x) + (total_y - mhy[down, :]))
-        oh[out, :] = jnp.where(edge, placed(sh[out, :], 2)[0], height)
-
     copies = []
 
     def send(x, y):
@@ -562,56 +589,52 @@
         x[0, pl.ds(BASE - 8, 8), :] = x[0, pl.ds(BASE + rows, 8), :]
     e[pl.ds(BASE - 8, 8), :] = e[pl.ds(BASE + rows, 8), :]
     strip_velocities(BASE - 8, rows + 16)
-    south = pl.ds(BASE - 8, 8)
-    hy[south, :] = north_flux(0, BASE - 8, 8, vel, mn, (t, s), (gt, gs))[0]
-    total = 0.0
-    for k in range(LEVELS):
-        total = total + north_flux(k, BASE - 8, 8, mv, mmn, (mt, ms), (mgt, mgs))[0]
-    mhy[south, :] = total
+    hy[pl.ds(BASE - 8, 8), :] = north_flux(0, BASE - 8, 8, vel, mn, (t, s), (gt, gs))[0]
     whole = pl.ds(BASE, rows)
-    edge = on_edge(rows)
-    wide_u, wide_v = placed(un[0, whole, :]), placed(vel[0, whole, :])
-    for k in range(LEVELS):
-        ou[k] = jnp.where(edge, wide_u[k], mu[k])
-        ov[k] = jnp.where(edge, wide_v[k], mv[k, whole, :])
+
+    def merge(out, strip, inner):
+        edge = on_edge(strip.shape[0])
+        for k, value in enumerate(placed(strip)):
+            out[k] = jnp.where(edge, value, inner[k])
+
+    merge(ou, un[0, whole, :], mu)
+    merge(ov, vel[0, whole, :], mv)
     send(ou, u_hbm)
     send(ov, v_hbm)
     strip_tracers(BASE, rows)
-    block = rows // LAST_CHUNKS
-    for c in range(LAST_CHUNKS):
-        tracers(BASE + c * block, block)
-        at = pl.ds(c * block, block)
-        send(ot.at[:, at, :], t_hbm.at[:, at, :])
-        send(os.at[:, at, :], s_hbm.at[:, at, :])
+    merge(ot, st[...], mt)
+    send(ot, t_hbm)
+    oh[...] = jnp.where(on_edge(rows), placed(sh[...], 2)[0], mh[...])
     send(oh, h_hbm)
+    merge(os, ss[...], ms)
+    send(os, s_hbm)
     for x in copies:
         x.wait()
 
 
-def last(c, m0, m1, t, s, w, e, un, vel, me, mn, face, slope, place):
-    rows, tall = un.shape[1], t.shape[1]
+def last(c, m0, m1, place, outs):
+    rows = outs[4].shape[0]
+    tall = rows + BASE + 16
     big = pltpu.VMEM((1, tall, LANES), F32)
     flat = pltpu.VMEM((tall, LANES), F32)
-    high = pltpu.VMEM((LEVELS, tall, LANES), F32)
     short = pltpu.VMEM((rows, LANES), F32)
     out3 = jax.ShapeDtypeStruct((LEVELS, rows, LANES), F32)
     wide = pltpu.VMEM((LEVELS, rows, LANES), F32)
     return pl.pallas_call(
         last_kernel,
-        in_specs=[VMEM] * 14,
+        in_specs=[VMEM] * 9,
         out_specs=[HBM] * 5,
         out_shape=[out3] * 4 + [jax.ShapeDtypeStruct((rows, LANES), F32)],
         scratch_shapes=[big] * 5
         + [flat]
         + [big] * 7
         + [flat]
-        + [high, high, flat]
         + [short] * 3
         + [wide] * 4
-        + [short, pltpu.SemaphoreType.DMA((3 + 2 * LAST_CHUNKS,))],
+        + [short, pltpu.SemaphoreType.DMA((5,))],
         compiler_params=params(24),
         name="last",
-    )(c, m0, m1, t, s, w, e, un, vel, me, mn, face, slope, place)
+    )(c, m0, m1, place, *outs)
 
 
 def swaps():
@@ -651,11 +674,11 @@
     a = send(a, perm=lat_first)
     b = send(b, perm=lat_second)
     *arrays, face, slope, place = column_pack(fields, free_elevation)
-    t, s, u, v, w, e, p, c, m0, m1 = ghosts(a, b, arrays)
+    *arrays, c, m0, m1, t, s, u, v, h = ghosts(a, b, arrays, face, slope)
     m0 = send(m0, perm=lon_first)
     m1 = send(m1, perm=lon_second)
-    un, vel, me, mn = new_velocities(u, v, w, p, free_elevation.shape[0])
-    return tuple(last(c, m0, m1, t, s, w, e, un, vel, me, mn, face, slope, place))
+    outs = main((*arrays, face, slope), (t, s, u, v, h))
+    return tuple(last(c, m0, m1, place, outs))
 
 
 def solution(mesh):

time: 25.2 us -> 27.5 us (1.091)
  waiting for transfers between devices: 0.29 us -> 5.46 us
  starting transfers between devices: 13.5 us -> 9.64 us
  Pallas kernels: 10.6 us -> 11.5 us
    ppermute x1, waiting for transfers between devices: 0.28 us -> 5.46 us  [on_device(): m1 = send(m1, perm=lon_second)]
    ppermute x1, starting transfers between devices: 4.9 us -> 1.97 us  [on_device(): m1 = send(m1, perm=lon_second)]
    pallas_call x3, Pallas kernels: 7.08 us -> 7.99 us  [the longest x1 4.17 us: ghosts(): pl.pallas_call(ghost_kernel, in_specs=[VMEM] * 14, out_specs=[VMEM] * 15,...]
    ppermute x1, starting transfers between devices: 1 us -> 0.09 us  [on_device(): m0 = send(m0, perm=lon_first)]
  transfers between devices with their start and end apart: 4 -> 4, of which waited for: 1 -> 1; matrix products, arithmetic and copies ran while one was open for 0% -> 0% of each run, Pallas kernels for 18% -> 9%
where the time goes in v5:
time: 27.5 us; the launch traced here: 27.4 us
  Pallas kernels  11.5 us (42%)
  starting transfers between devices  9.64 us (35%)
  waiting for transfers between devices  5.46 us (20%)
  between operations  0.75 us (3%)
    ppermute x1, starting transfers between devices, on_device(): b = send(b, perm=lat_second)  7.04 us
    ppermute x1, waiting for transfers between devices, on_device(): m1 = send(m1, perm=lon_second)  5.46 us
    pallas_call x1, Pallas kernels, ghosts(): pl.pallas_call(ghost_kernel, in_specs=[VMEM] * 14, out_specs=[VMEM] * 15,...  4.17 us
    pallas_call x1, Pallas kernels, last(): pl.pallas_call(last_kernel, in_specs=[VMEM] * 9, out_specs=[HBM] * 5, out...  3.82 us
    pallas_call x1, Pallas kernels, column_pack(): pl.pallas_call(column_pack_kernel, in_specs=[VMEM] * 6, out_specs=[VMEM]...  2.33 us
    ppermute x1, starting transfers between devices, on_device(): m1 = send(m1, perm=lon_second)  1.97 us
    pallas_call x1, Pallas kernels, row_pack(): pl.pallas_call(row_pack_kernel, in_specs=[HBM] * 6, out_specs=[VMEM] * 2,...  1.18 us
  transfers between devices with their start and end apart: 4, of which 1 were waited for; matrix products, arithmetic and copies ran while one was open for 0% of the time, Pallas kernels for 9%

profile of v5, /device:TPU:14, one launch (start us, length us, event | category | flops | bytes accessed | tf_op | source)
XLA Modules:
  0.0 27.4 jit_solution(13627246902597727278)
XLA Ops:
  0.6 0.0 copy-start.4
  0.6 0.0 copy-start.5
  0.7 0.0 copy-start.3
  0.7 0.0 copy-start.2
  0.7 0.0 copy-start.1
  0.7 0.0 copy-start
  0.7 1.2 %row_pack.1 = (f32[88,128]{1,0:T(8,128)S(1)}, f32[88,128]{1,0:T(8,128)S(1)}) custom-call(f32[8,192,128]{2,1,0:T(8,128)} %t_in.1, f32[8,192,128]{2,1,0:T(8,128)} %s_in.1, f32[8,192,128]{2,1,0:T(8,128)} %u_in.1, f32[8,192,128]{2,1,0:T(8,128)} %v_in.1, s32[8,192,128]{2,1,0:T(8,128)} %w_in.1, f32[192,128]{1,0:T(8,128)} %e_in.1), custom_call_target="tpu_custom_call" | custom-call | tf_op jit(solution)/shard_map/row_pack/pallas_call | solution.py:139
  1.9 0.5 %collective-permute-start = (f32[88,128]{1,0:T(8,128)S(1)}, f32[88,128]{1,0:T(8,128)S(1)}, u32[]{:S(2)}, u32[]{:S(2)}) collective-permute-start(f32[88,128]{1,0:T(8,128)S(1)} %get-tuple-element.40), channel_id=1, source_target_pairs={{0,1},{1,0},{2,3},{3,2},{4,5},{5,4},{6,7},{7,6},{8,9},{9,8},{10,11... | collective-permute-start | bytes 135176 | tf_op jit(solution)/shard_map/ppermute | solution.py:674
  2.4 7.0 %collective-permute-start.1 = (f32[88,128]{1,0:T(8,128)S(1)}, f32[88,128]{1,0:T(8,128)S(1)}, u32[]{:S(2)}, u32[]{:S(2)}) collective-permute-start(f32[88,128]{1,0:T(8,128)S(1)} %get-tuple-element.41), channel_id=1, source_target_pairs={{0,8},{1,2},{2,1},{3,4},{4,3},{5,6},{6,5},{7,255},{8,0},{9,10},{10... | collective-permute-start | bytes 135176 | tf_op jit(solution)/shard_map/ppermute | solution.py:675
  9.5 0.0 copy-done.4
  9.5 0.0 copy-done.5
  9.5 0.0 copy-done.3
  9.5 0.0 copy-done.2
  9.5 0.0 copy-done.1
  9.5 0.0 copy-done
  9.5 2.3 %column_pack.1 = (f32[8,224,128]{2,1,0:T(8,128)S(1)}, f32[8,224,128]{2,1,0:T(8,128)S(1)}, f32[8,224,128]{2,1,0:T(8,128)S(1)}, f32[8,224,128]{2,1,0:T(8,128)S(1)}...) custom-call(f32[8,192,128]{2,1,0:T(8,128)S(1)} %copy-done, ...), custom_call_target="tpu_custom_call" | custom-call | flops 10000000 | bytes 6000000 | tf_op jit(solution)/shard_map/column_pack/pallas_call | solution.py:242
  11.8 0.0 collective-permute-done.a_ref
  11.8 0.0 collective-permute-done.1.b_ref
  11.9 4.2 %ghosts.1 = (f32[8,224,128]{2,1,0:T(8,128)S(1)}, f32[8,224,128]{2,1,0:T(8,128)S(1)}, f32[8,224,128]{2,1,0:T(8,128)S(1)}, f32[8,224,128]{2,1,0:T(8,128)S(1)}, f32...) custom-call(f32[88,128]{1,0:T(8,128)S(1)} %collective-permute-done.a, ...), custom_call_target="tpu_custom_call", output_to_operand_aliasing={{0}: (2, {}), {1}: (3, {}), {2}: (4, {}), {3}: (5, {}), {4}... | custom-call | tf_op jit(solution)/shard_map/ghosts/pallas_call | solution.py:316
  16.0 0.1 collective-permute-start.2
  16.1 2.0 %collective-permute-start.3 = (f32[136,128]{1,0:T(8,128)S(1)}, f32[136,128]{1,0:T(8,128)S(1)}, u32[]{:S(2)}, u32[]{:S(2)}) collective-permute-start(f32[136,128]{1,0:T(8,128)S(1)} %get-tuple-element.56), channel_id=1, source_target_pairs={{0,248},{1,249},{2,250},{3,251},{4,252},{5,253},{6,254},{7,255},{8... | collective-permute-start | bytes 208904 | tf_op jit(solution)/shard_map/ppermute | solution.py:679
  18.1 0.0 collective-permute-done.2.m0_ref
  18.1 5.5 %collective-permute-done.3.m1_ref = f32[136,128]{1,0:T(8,128)S(1)} collective-permute-done((f32[136,128]{1,0:T(8,128)S(1)}, f32[136,128]{1,0:T(8,128)S(1)}, u32[]{:S(2)}, u32[]{:S(2)}) %collective-permute-start.3) | collective-permute-done | bytes 69664 | tf_op jit(solution)/shard_map/ppermute | solution.py:679
  23.6 3.8 %last.1 = (f32[8,192,128]{2,1,0:T(8,128)}, f32[8,192,128]{2,1,0:T(8,128)}, f32[8,192,128]{2,1,0:T(8,128)}, f32[8,192,128]{2,1,0:T(8,128)}, f32[192,128]{1,0:T(8,128)}) custom-call(f32[6,200,128]{2,1,0:T(8,128)S(1)} %get-tuple-element.54.c_ref, f32[136,128]{1,0:T(8,128)S(1)} %collective-permute-done.2.m0_ref, f32[136,128]{1,0:T(8,128)S(1)} %collective-permute-done.3.m1_ref, ...), custom_call_target="tpu_custom_call" | custom-call | tf_op jit(solution)/shard_map/last/pallas_call | solution.py:623
  (1 shorter events, 0.0 us)
Async XLA Ops:
  0.6 8.8 %copy-start.4 = (s32[8,192,128]{2,1,0:T(8,128)S(1)}, s32[8,192,128]{2,1,0:T(8,128)}, u32[]{:S(2)}) copy-start(s32[8,192,128]{2,1,0:T(8,128)} %w_in.1) | copy-start | bytes 2359300
  0.6 8.8 %copy-start.5 = (f32[192,128]{1,0:T(8,128)S(1)}, f32[192,128]{1,0:T(8,128)}, u32[]{:S(2)}) copy-start(f32[192,128]{1,0:T(8,128)} %e_in.1) | copy-start | bytes 294916
  0.7 8.8 %copy-start.3 = (f32[8,192,128]{2,1,0:T(8,128)S(1)}, f32[8,192,128]{2,1,0:T(8,128)}, u32[]{:S(2)}) copy-start(f32[8,192,128]{2,1,0:T(8,128)} %v_in.1) | copy-start | bytes 2359300
  0.7 8.8 %copy-start.2 = (f32[8,192,128]{2,1,0:T(8,128)S(1)}, f32[8,192,128]{2,1,0:T(8,128)}, u32[]{:S(2)}) copy-start(f32[8,192,128]{2,1,0:T(8,128)} %u_in.1) | copy-start | bytes 2359300
  0.7 8.8 %copy-start.1 = (f32[8,192,128]{2,1,0:T(8,128)S(1)}, f32[8,192,128]{2,1,0:T(8,128)}, u32[]{:S(2)}) copy-start(f32[8,192,128]{2,1,0:T(8,128)} %s_in.1) | copy-start | bytes 2359300
  0.7 8.8 %copy-start = (f32[8,192,128]{2,1,0:T(8,128)S(1)}, f32[8,192,128]{2,1,0:T(8,128)}, u32[]{:S(2)}) copy-start(f32[8,192,128]{2,1,0:T(8,128)} %t_in.1) | copy-start | bytes 2359300
  1.9 10.0 %collective-permute-start = (f32[88,128]{1,0:T(8,128)S(1)}, f32[88,128]{1,0:T(8,128)S(1)}, u32[]{:S(2)}, u32[]{:S(2)}) collective-permute-start(f32[88,128]{1,0:T(8,128)S(1)} %get-tuple-element.40), channel_id=1, source_target_pairs={{0,1},{1,0},{2,3},{3,2},{4,5},{5,4},{6,7},{7,6},{8,9},{9,8},{10,11... | collective-permute-start | bytes 135176 | tf_op jit(solution)/shard_map/ppermute | solution.py:674
  2.4 9.4 %collective-permute-start.1 = (f32[88,128]{1,0:T(8,128)S(1)}, f32[88,128]{1,0:T(8,128)S(1)}, u32[]{:S(2)}, u32[]{:S(2)}) collective-permute-start(f32[88,128]{1,0:T(8,128)S(1)} %get-tuple-element.41), channel_id=1, source_target_pairs={{0,8},{1,2},{2,1},{3,4},{4,3},{5,6},{6,5},{7,255},{8,0},{9,10},{10... | collective-permute-start | bytes 135176 | tf_op jit(solution)/shard_map/ppermute | solution.py:675
  16.0 2.1 %collective-permute-start.2 = (f32[136,128]{1,0:T(8,128)S(1)}, f32[136,128]{1,0:T(8,128)S(1)}, u32[]{:S(2)}, u32[]{:S(2)}) collective-permute-start(f32[136,128]{1,0:T(8,128)S(1)} %get-tuple-element.55), channel_id=1, source_target_pairs={{0,8},{1,9},{2,10},{3,11},{4,12},{5,13},{6,14},{7,15},{8,0},{9,1},... | collective-permute-start | bytes 208904 | tf_op jit(solution)/shard_map/ppermute | solution.py:678
  16.1 7.4 %collective-permute-start.3 = (f32[136,128]{1,0:T(8,128)S(1)}, f32[136,128]{1,0:T(8,128)S(1)}, u32[]{:S(2)}, u32[]{:S(2)}) collective-permute-start(f32[136,128]{1,0:T(8,128)S(1)} %get-tuple-element.56), channel_id=1, source_target_pairs={{0,248},{1,249},{2,250},{3,251},{4,252},{5,253},{6,254},{7,255},{8... | collective-permute-start | bytes 208904 | tf_op jit(solution)/shard_map/ppermute | solution.py:679

commit v6 on v5

--- a/solution.py
+++ b/solution.py
@@ -195,7 +195,8 @@
     even = is_even("lon")
     matrix = face_matrix()
     for k in range(LEVELS):
-        place[:, k * LANES : (k + 1) * LANES] = place_matrix(k)
+        place[:LANES, k * LANES : (k + 1) * LANES] = place_matrix(k)
+        place[LANES:, k * LANES : (k + 1) * LANES] = place_matrix(k)
 
     def step(i, _):
         out = pl.ds(pl.multiple_of(i * PACK_ROWS, 8), PACK_ROWS)
@@ -248,7 +249,7 @@
         + [pltpu.VMEM((FIELDS + 1, rows + 8, LANES), F32)]
         + [pltpu.VMEM((message_rows(rows)[1], LANES), F32)] * 2
         + [pltpu.VMEM((2 * LEVELS, rows, LANES), F32)] * 2
-        + [pltpu.VMEM((LANES, LEVELS * LANES), BF16)],
+        + [pltpu.VMEM((2 * LANES, LEVELS * LANES), BF16)],
         scratch_shapes=[pltpu.VMEM((rows, LANES), F32)] * 2,
         compiler_params=params(16),
         cost_estimate=pl.CostEstimate(flops=10_000_000, bytes_accessed=6_000_000, transcendentals=0),
@@ -257,9 +258,7 @@
 
 
 def ghost_kernel(a_ref, b_ref, *refs):
-    face, slope = refs[10:12]
-    t, s, u, v, w, e, p, c_ref, m0_ref, m1_ref = refs[12:22]
-    outs, g_ref, scratch = refs[22:27], refs[27], refs[28:]
+    t, s, u, v, w, e, p, c_ref, m0_ref, m1_ref, g_ref = refs[10:]
     rows = c_ref.shape[1] - 8
     even = is_even("lat")
     fold = lax.axis_index("lat") == lax.axis_size("lat") - 1
@@ -306,23 +305,18 @@
         e[side, :] = g_ref[PLANES - 1]
         pressure(side, t, s, e, p)
 
-    @pl.when(waits_for_seam())
-    def _():
-        interior(t, s, u, v, w, e, p, face, slope, *outs, *scratch)
-
-
-def ghosts(a, b, arrays, face, slope):
-    rows, tall = face.shape[1], arrays[0].shape[1]
+
+def ghosts(a, b, arrays):
     return pl.pallas_call(
         ghost_kernel,
-        in_specs=[VMEM] * 14,
-        out_specs=[VMEM] * 15,
-        out_shape=[pltpu.VMEM(x.shape, F32) for x in arrays] + interior_outputs(rows),
-        scratch_shapes=[pltpu.VMEM((PLANES, 8, LANES), F32)] + interior_scratch(tall),
+        in_specs=[VMEM] * 12,
+        out_specs=[VMEM] * 10,
+        out_shape=[pltpu.VMEM(x.shape, F32) for x in arrays],
+        scratch_shapes=[pltpu.VMEM((PLANES, 8, LANES), F32)],
         input_output_aliases={n + 2: n for n in range(10)},
-        compiler_params=params(16),
+        compiler_params=params(8),
         name="ghosts",
-    )(a, b, *arrays, face, slope)
+    )(a, b, *arrays)
 
 
 def density_half(t, s):
@@ -475,6 +469,28 @@
     return lax.axis_index("lon") == 0
 
 
+def early_kernel(*refs):
+    ins, outs, scratch = refs[:9], refs[11:16], refs[16:]
+
+    @pl.when(waits_for_seam())
+    def _():
+        interior(*ins, *outs, *scratch)
+
+
+def early(arrays, message):
+    rows, tall = arrays[-1].shape[1], arrays[0].shape[1]
+    return pl.pallas_call(
+        early_kernel,
+        in_specs=[VMEM] * 10,
+        out_specs=[VMEM] * 6,
+        out_shape=[pltpu.VMEM(message.shape, F32)] + interior_outputs(rows),
+        scratch_shapes=interior_scratch(tall),
+        input_output_aliases={9: 0},
+        compiler_params=params(16),
+        name="early",
+    )(*arrays, message)
+
+
 def main_kernel(*refs):
     ins, outs, scratch = refs[:9], refs[14:19], refs[19:]
 
@@ -484,7 +500,7 @@
 
 
 def main(arrays, outs):
-    rows, tall = outs[4].shape[0], arrays[0].shape[1]
+    rows, tall = arrays[-1].shape[1], arrays[0].shape[1]
     return pl.pallas_call(
         main_kernel,
         in_specs=[VMEM] * 14,
@@ -558,8 +574,12 @@
 
     def placed(strip, levels=LEVELS):
         out = []
+        high, middle, low = split(strip)
+        top = jnp.concatenate([high, middle], axis=1)
         for k in range(0, levels, 2):
-            both = product(strip, place[:, k * LANES : (k + 2) * LANES])
+            at = slice(k * LANES, (k + 2) * LANES)
+            both = jnp.dot(low, place[:LANES, at], preferred_element_type=F32)
+            both = both + jnp.dot(top, place[:, at], preferred_element_type=F32)
             out += [both[:, :LANES], both[:, LANES:]]
         return out
 
@@ -674,10 +694,12 @@
     a = send(a, perm=lat_first)
     b = send(b, perm=lat_second)
     *arrays, face, slope, place = column_pack(fields, free_elevation)
-    *arrays, c, m0, m1, t, s, u, v, h = ghosts(a, b, arrays, face, slope)
+    *arrays, c, m0, m1 = ghosts(a, b, arrays)
+    arrays += [face, slope]
     m0 = send(m0, perm=lon_first)
+    m1, *outs = early(arrays, m1)
     m1 = send(m1, perm=lon_second)
-    outs = main((*arrays, face, slope), (t, s, u, v, h))
+    outs = main(arrays, outs)
     return tuple(last(c, m0, m1, place, outs))
 
 

time: 27.5 us -> 28.2 us (1.025)
  waiting for transfers between devices: 5.46 us -> 6.37 us
    ppermute x1, starting transfers between devices: 1.97 us -> 1.06 us  [on_device(): m1 = send(m1, perm=lon_second)]
    ppermute x1, waiting for transfers between devices: 5.46 us -> 6.37 us  [on_device(): m1 = send(m1, perm=lon_second)]
    ppermute x1, starting transfers between devices: 0.09 us -> 1 us  [on_device(): m0 = send(m0, perm=lon_first)]
    pallas_call x1 -> x2, Pallas kernels: 4.17 us -> 4.14 us  [the longest x1 3.79 us: early(): pl.pallas_call(early_kernel, in_specs=[VMEM] * 10, out_specs=[VMEM] * 6,...]
  transfers between devices with their start and end apart: 4 -> 4, of which waited for: 1 -> 1; matrix products, arithmetic and copies ran while one was open for 0% -> 0% of each run, Pallas kernels for 9% -> 22%
where the time goes in v6:
time: 28.2 us; the launch traced here: 28.1 us
  Pallas kernels  11.3 us (40%)
  starting transfers between devices  9.64 us (34%)
  waiting for transfers between devices  6.37 us (23%)
  between operations  0.74 us (3%)
    ppermute x1, starting transfers between devices, on_device(): b = send(b, perm=lat_second)  7.04 us
    ppermute x1, waiting for transfers between devices, on_device(): m1 = send(m1, perm=lon_second)  6.37 us
    pallas_call x1, Pallas kernels, early(): pl.pallas_call(early_kernel, in_specs=[VMEM] * 10, out_specs=[VMEM] * 6,...  3.79 us
    pallas_call x1, Pallas kernels, last(): pl.pallas_call(last_kernel, in_specs=[VMEM] * 9, out_specs=[HBM] * 5, out...  3.59 us
    pallas_call x1, Pallas kernels, column_pack(): pl.pallas_call(column_pack_kernel, in_specs=[VMEM] * 6, out_specs=[VMEM]...  2.37 us
    pallas_call x1, Pallas kernels, row_pack(): pl.pallas_call(row_pack_kernel, in_specs=[HBM] * 6, out_specs=[VMEM] * 2,...  1.18 us
    ppermute x1, starting transfers between devices, on_device(): m1 = send(m1, perm=lon_second)  1.06 us
    ppermute x1, starting transfers between devices, on_device(): m0 = send(m0, perm=lon_first)  1 us
  transfers between devices with their start and end apart: 4, of which 1 were waited for; matrix products, arithmetic and copies ran while one was open for 0% of the time, Pallas kernels for 22%

profile of v6, /device:TPU:14, one launch (start us, length us, event | category | flops | bytes accessed | tf_op | source)
XLA Modules:
  0.0 28.1 jit_solution(6549412461831587123)
XLA Ops:
  0.6 0.0 copy-start
  0.6 0.0 copy-start.1
  0.7 0.0 copy-start.2
  0.7 0.0 copy-start.3
  0.7 0.0 copy-start.4
  0.7 0.0 copy-start.5
  0.7 1.2 %row_pack.1 = (f32[88,128]{1,0:T(8,128)S(1)}, f32[88,128]{1,0:T(8,128)S(1)}) custom-call(f32[8,192,128]{2,1,0:T(8,128)} %t_in.1, f32[8,192,128]{2,1,0:T(8,128)} %s_in.1, f32[8,192,128]{2,1,0:T(8,128)} %u_in.1, f32[8,192,128]{2,1,0:T(8,128)} %v_in.1, s32[8,192,128]{2,1,0:T(8,128)} %w_in.1, f32[192,128]{1,0:T(8,128)} %e_in.1), custom_call_target="tpu_custom_call" | custom-call | tf_op jit(solution)/shard_map/row_pack/pallas_call | solution.py:139
  1.9 0.5 %collective-permute-start = (f32[88,128]{1,0:T(8,128)S(1)}, f32[88,128]{1,0:T(8,128)S(1)}, u32[]{:S(2)}, u32[]{:S(2)}) collective-permute-start(f32[88,128]{1,0:T(8,128)S(1)} %get-tuple-element.41), channel_id=1, source_target_pairs={{0,1},{1,0},{2,3},{3,2},{4,5},{5,4},{6,7},{7,6},{8,9},{9,8},{10,11... | collective-permute-start | bytes 135176 | tf_op jit(solution)/shard_map/ppermute | solution.py:694
  2.4 7.0 %collective-permute-start.1 = (f32[88,128]{1,0:T(8,128)S(1)}, f32[88,128]{1,0:T(8,128)S(1)}, u32[]{:S(2)}, u32[]{:S(2)}) collective-permute-start(f32[88,128]{1,0:T(8,128)S(1)} %get-tuple-element.42), channel_id=1, source_target_pairs={{0,8},{1,2},{2,1},{3,4},{4,3},{5,6},{6,5},{7,255},{8,0},{9,10},{10... | collective-permute-start | bytes 135176 | tf_op jit(solution)/shard_map/ppermute | solution.py:695
  9.5 0.0 copy-done
  9.5 0.0 copy-done.1
  9.5 0.0 copy-done.2
  9.5 0.0 copy-done.3
  9.5 0.0 copy-done.4
  9.5 0.0 copy-done.5
  9.5 2.4 %column_pack.1 = (f32[8,224,128]{2,1,0:T(8,128)S(1)}, f32[8,224,128]{2,1,0:T(8,128)S(1)}, f32[8,224,128]{2,1,0:T(8,128)S(1)}, f32[8,224,128]{2,1,0:T(8,128)S(1)}...) custom-call(f32[8,192,128]{2,1,0:T(8,128)S(1)} %copy-done, ...), custom_call_target="tpu_custom_call" | custom-call | flops 10000000 | bytes 6000000 | tf_op jit(solution)/shard_map/column_pack/pallas_call | solution.py:243
  11.9 0.0 collective-permute-done.a_ref
  11.9 0.0 collective-permute-done.1.b_ref
  11.9 0.4 %ghosts.1 = (f32[8,224,128]{2,1,0:T(8,128)S(1)}, f32[8,224,128]{2,1,0:T(8,128)S(1)}, f32[8,224,128]{2,1,0:T(8,128)S(1)}, f32[8,224,128]{2,1,0:T(8,128)S(1)}, f32...) custom-call(f32[88,128]{1,0:T(8,128)S(1)} %collective-permute-done.a, ...), custom_call_target="tpu_custom_call", output_to_operand_aliasing={{0}: (2, {}), {1}: (3, {}), {2}: (4, {}), {3}: (5, {}), {4}... | custom-call | tf_op jit(solution)/shard_map/ghosts/pallas_call | solution.py:310
  12.2 1.0 %collective-permute-start.2 = (f32[136,128]{1,0:T(8,128)S(1)}, f32[136,128]{1,0:T(8,128)S(1)}, u32[]{:S(2)}, u32[]{:S(2)}) collective-permute-start(f32[136,128]{1,0:T(8,128)S(1)} %get-tuple-element.54), channel_id=1, source_target_pairs={{0,8},{1,9},{2,10},{3,11},{4,12},{5,13},{6,14},{7,15},{8,0},{9,1},... | collective-permute-start | bytes 208904 | tf_op jit(solution)/shard_map/ppermute | solution.py:699
  13.2 3.8 %early.1 = (f32[136,128]{1,0:T(8,128)S(1)}, f32[8,192,128]{2,1,0:T(8,128)S(1)}, f32[8,192,128]{2,1,0:T(8,128)S(1)}, f32[8,192,128]{2,1,0:T(8,128)S(1)}, f32[8,19...) custom-call(f32[8,224,128]{2,1,0:T(8,128)S(1)} %get-tuple-element.55.refs_0_, ...), custom_call_target="tpu_custom_call", output_to_operand_aliasing={{0}: (9, {})} | custom-call | tf_op jit(solution)/shard_map/early/pallas_call | solution.py:482
  17.0 1.1 %collective-permute-start.3 = (f32[136,128]{1,0:T(8,128)S(1)}, f32[136,128]{1,0:T(8,128)S(1)}, u32[]{:S(2)}, u32[]{:S(2)}) collective-permute-start(f32[136,128]{1,0:T(8,128)S(1)} %get-tuple-element.65), channel_id=1, source_target_pairs={{0,248},{1,249},{2,250},{3,251},{4,252},{5,253},{6,254},{7,255},{8... | collective-permute-start | bytes 208904 | tf_op jit(solution)/shard_map/ppermute | solution.py:701
  18.1 0.0 collective-permute-done.2.m0_ref
  18.1 6.4 %collective-permute-done.3.m1_ref = f32[136,128]{1,0:T(8,128)S(1)} collective-permute-done((f32[136,128]{1,0:T(8,128)S(1)}, f32[136,128]{1,0:T(8,128)S(1)}, u32[]{:S(2)}, u32[]{:S(2)}) %collective-permute-start.3) | collective-permute-done | bytes 69664 | tf_op jit(solution)/shard_map/ppermute | solution.py:701
  24.5 3.6 %last.1 = (f32[8,192,128]{2,1,0:T(8,128)}, f32[8,192,128]{2,1,0:T(8,128)}, f32[8,192,128]{2,1,0:T(8,128)}, f32[8,192,128]{2,1,0:T(8,128)}, f32[192,128]{1,0:T(8,128)}) custom-call(f32[6,200,128]{2,1,0:T(8,128)S(1)} %get-tuple-element.53.c_ref, f32[136,128]{1,0:T(8,128)S(1)} %collective-permute-done.2.m0_ref, f32[136,128]{1,0:T(8,128)S(1)} %collective-permute-done.3.m1_ref, ...), custom_call_target="tpu_custom_call" | custom-call | tf_op jit(solution)/shard_map/last/pallas_call | solution.py:643
  (1 shorter events, 0.0 us)
Async XLA Ops:
  0.6 8.8 %copy-start = (f32[8,192,128]{2,1,0:T(8,128)S(1)}, f32[8,192,128]{2,1,0:T(8,128)}, u32[]{:S(2)}) copy-start(f32[8,192,128]{2,1,0:T(8,128)} %t_in.1) | copy-start | bytes 2359300
  0.6 8.8 %copy-start.1 = (f32[8,192,128]{2,1,0:T(8,128)S(1)}, f32[8,192,128]{2,1,0:T(8,128)}, u32[]{:S(2)}) copy-start(f32[8,192,128]{2,1,0:T(8,128)} %s_in.1) | copy-start | bytes 2359300
  0.7 8.8 %copy-start.2 = (f32[8,192,128]{2,1,0:T(8,128)S(1)}, f32[8,192,128]{2,1,0:T(8,128)}, u32[]{:S(2)}) copy-start(f32[8,192,128]{2,1,0:T(8,128)} %u_in.1) | copy-start | bytes 2359300
  0.7 8.8 %copy-start.3 = (f32[8,192,128]{2,1,0:T(8,128)S(1)}, f32[8,192,128]{2,1,0:T(8,128)}, u32[]{:S(2)}) copy-start(f32[8,192,128]{2,1,0:T(8,128)} %v_in.1) | copy-start | bytes 2359300
  0.7 8.8 %copy-start.4 = (s32[8,192,128]{2,1,0:T(8,128)S(1)}, s32[8,192,128]{2,1,0:T(8,128)}, u32[]{:S(2)}) copy-start(s32[8,192,128]{2,1,0:T(8,128)} %w_in.1) | copy-start | bytes 2359300
  0.7 8.8 %copy-start.5 = (f32[192,128]{1,0:T(8,128)S(1)}, f32[192,128]{1,0:T(8,128)}, u32[]{:S(2)}) copy-start(f32[192,128]{1,0:T(8,128)} %e_in.1) | copy-start | bytes 294916
  1.9 10.0 %collective-permute-start = (f32[88,128]{1,0:T(8,128)S(1)}, f32[88,128]{1,0:T(8,128)S(1)}, u32[]{:S(2)}, u32[]{:S(2)}) collective-permute-start(f32[88,128]{1,0:T(8,128)S(1)} %get-tuple-element.41), channel_id=1, source_target_pairs={{0,1},{1,0},{2,3},{3,2},{4,5},{5,4},{6,7},{7,6},{8,9},{9,8},{10,11... | collective-permute-start | bytes 135176 | tf_op jit(solution)/shard_map/ppermute | solution.py:694
  2.4 9.5 %collective-permute-start.1 = (f32[88,128]{1,0:T(8,128)S(1)}, f32[88,128]{1,0:T(8,128)S(1)}, u32[]{:S(2)}, u32[]{:S(2)}) collective-permute-start(f32[88,128]{1,0:T(8,128)S(1)} %get-tuple-element.42), channel_id=1, source_target_pairs={{0,8},{1,2},{2,1},{3,4},{4,3},{5,6},{6,5},{7,255},{8,0},{9,10},{10... | collective-permute-start | bytes 135176 | tf_op jit(solution)/shard_map/ppermute | solution.py:695
  12.2 5.9 %collective-permute-start.2 = (f32[136,128]{1,0:T(8,128)S(1)}, f32[136,128]{1,0:T(8,128)S(1)}, u32[]{:S(2)}, u32[]{:S(2)}) collective-permute-start(f32[136,128]{1,0:T(8,128)S(1)} %get-tuple-element.54), channel_id=1, source_target_pairs={{0,8},{1,9},{2,10},{3,11},{4,12},{5,13},{6,14},{7,15},{8,0},{9,1},... | collective-permute-start | bytes 208904 | tf_op jit(solution)/shard_map/ppermute | solution.py:699
  17.0 7.4 %collective-permute-start.3 = (f32[136,128]{1,0:T(8,128)S(1)}, f32[136,128]{1,0:T(8,128)S(1)}, u32[]{:S(2)}, u32[]{:S(2)}) collective-permute-start(f32[136,128]{1,0:T(8,128)S(1)} %get-tuple-element.65), channel_id=1, source_target_pairs={{0,248},{1,249},{2,250},{3,251},{4,252},{5,253},{6,254},{7,255},{8... | collective-permute-start | bytes 208904 | tf_op jit(solution)/shard_map/ppermute | solution.py:701

commit v7 on v6

--- a/solution.py
+++ b/solution.py
@@ -190,10 +190,10 @@
     return main, rest
 
 
-def column_pack_kernel(t_in, s_in, u_in, v_in, w_in, e_in, t, s, u, v, w, e, p, c_ref, m0_ref, m1_ref, face, slope, place, m0_wide, m1_wide):
+def column_pack_kernel(t_in, s_in, u_in, v_in, w_in, e_in, t, s, u, v, w, e, p, c_ref, m0_ref, m1_ref, face, slope, xu, xv, me, place, m0_wide, m1_wide):
     rows = e_in.shape[0]
     even = is_even("lon")
-    matrix = face_matrix()
+    matrix, neighbours, difference = face_matrix(), neighbour_matrix(), difference_matrix()
     for k in range(LEVELS):
         place[:LANES, k * LANES : (k + 1) * LANES] = place_matrix(k)
         place[LANES:, k * LANES : (k + 1) * LANES] = place_matrix(k)
@@ -221,6 +221,14 @@
             at = total + h
             p[k, here, :] = at
             total = at + h
+            wet = w_in[k, out, :].astype(F32)
+            both = jnp.dot(wet.astype(BF16), neighbours, preferred_element_type=F32)
+            m_east, m_west = wet * both[:, :LANES], wet * both[:, LANES:]
+            me[k, out, :] = m_east
+            for x, y, gradient in ((u_in, xu, product(at, difference)), (v_in, xv, 0.0)):
+                q = x[k, out, :]
+                spread = m_east * (east(q) - q) + m_west * (west(q) - q)
+                y[k, out, :] = q - gradient + (time_step * viscosity) * spread
         for n, x in enumerate((t_in, s_in)):
             for k in range(LEVELS):
                 both = product(x[k, out, :], matrix)
@@ -243,12 +251,13 @@
     return pl.pallas_call(
         column_pack_kernel,
         in_specs=[VMEM] * 6,
-        out_specs=[VMEM] * 13,
+        out_specs=[VMEM] * 16,
         out_shape=[big] * 5
         + [pltpu.VMEM((tall, LANES), F32), big]
         + [pltpu.VMEM((FIELDS + 1, rows + 8, LANES), F32)]
         + [pltpu.VMEM((message_rows(rows)[1], LANES), F32)] * 2
         + [pltpu.VMEM((2 * LEVELS, rows, LANES), F32)] * 2
+        + [pltpu.VMEM((LEVELS, rows, LANES), F32)] * 3
         + [pltpu.VMEM((2 * LANES, LEVELS * LANES), BF16)],
         scratch_shapes=[pltpu.VMEM((rows, LANES), F32)] * 2,
         compiler_params=params(16),
@@ -340,28 +349,41 @@
     return (time_step * coriolis_max) * (2.0 * (row + 0.5) / total - 1.0)
 
 
-def velocity_trial(k, r, n, spin, u, v, w, p, m_east, m_north, matrices=None):
+def velocity_trial(k, r, n, spin, u, v, w, p, m_east, m_north):
     here, up, down = pl.ds(r, n), pl.ds(r + 1, n), pl.ds(r - 1, n)
     wet = w[k, here, :]
-    pc = p[k, here, :]
-    if matrices is None:
-        wet_east, wet_west, slope = east(wet), west(wet), east(pc) - west(pc)
-    else:
-        both = jnp.dot(wet.astype(BF16), matrices[0], preferred_element_type=F32)
-        wet_east, wet_west, slope = both[:, :LANES], both[:, LANES:], product(pc, matrices[1])
-    me = wet * wet_east
-    mw = wet * wet_west
+    me = wet * east(wet)
+    mw = wet * west(wet)
     mn = wet * w[k, up, :]
     ms = wet * w[k, down, :]
-    m_east[k, here, :] = me
+    if m_east is not None:
+        m_east[k, here, :] = me
     m_north[k, here, :] = mn
 
     def lap(q_ref, q):
         return me * (east(q) - q) + mw * (west(q) - q) + (mn * (q_ref[k, up, :] - q) + ms * (q_ref[k, down, :] - q))
 
     un, vn = u[k, here, :], v[k, here, :]
-    u_trial = un + (spin * vn - slope + (time_step * viscosity) * lap(u, un))
+    pc = p[k, here, :]
+    u_trial = un + (spin * vn - (east(pc) - west(pc)) + (time_step * viscosity) * lap(u, un))
     v_trial = vn + ((time_step * viscosity) * lap(v, vn) - spin * un - (p[k, up, :] - p[k, down, :]))
+    return wet, u_trial, v_trial
+
+
+def velocity_trial_y(k, r, n, spin, u, v, w, p, xu, xv, m_north):
+    here, up, down = pl.ds(r, n), pl.ds(r + 1, n), pl.ds(r - 1, n)
+    out = pl.ds(r - BASE, n)
+    wet = w[k, here, :]
+    mn = wet * w[k, up, :]
+    ms = wet * w[k, down, :]
+    m_north[k, here, :] = mn
+
+    def lap(q_ref, q):
+        return (time_step * viscosity) * (mn * (q_ref[k, up, :] - q) + ms * (q_ref[k, down, :] - q))
+
+    un, vn = u[k, here, :], v[k, here, :]
+    u_trial = xu[k, out, :] + (spin * vn + lap(u, un))
+    v_trial = xv[k, out, :] + (lap(v, vn) - spin * un - (p[k, up, :] - p[k, down, :]))
     return wet, u_trial, v_trial
 
 
@@ -402,15 +424,16 @@
     return tr, out
 
 
-def interior(t, s, u, v, w, e, p, face, slope, t_out, s_out, u_out, v_out, h_out, me, mn, vel, gt, gs, hy):
-    rows = h_out.shape[0]
-    matrices = neighbour_matrix(), difference_matrix()
+def new_velocities(u, v, w, p, xu, xv, u_out, v_out, vel, mn):
+    rows = u_out.shape[1]
 
     def velocities(r, n, store):
         here = pl.ds(r, n)
         spin = coriolis_rows(r, n, rows)
-        on_unit = matrices if n % 16 == 0 else None
-        trial = [velocity_trial(k, r, n, spin, u, v, w, p, me, mn, on_unit) for k in range(LEVELS)]
+        if store:
+            trial = [velocity_trial_y(k, r, n, spin, u, v, w, p, xu, xv, mn) for k in range(LEVELS)]
+        else:
+            trial = [velocity_trial(k, r, n, spin, u, v, w, p, None, mn) for k in range(LEVELS)]
         at_floor = [trial[k][0] > (trial[k + 1][0] if k + 1 < LEVELS else 0.0) for k in range(LEVELS)]
         u_floor, v_floor = trial[0][1], trial[0][2]
         for k in range(1, LEVELS):
@@ -426,92 +449,86 @@
                 u_out[k, out, :] = factor * trial[k][1]
                 v_out[k, out, :] = v_next
 
-    def tracers(r, n):
-        here, down = pl.ds(r, n), pl.ds(r - 1, n)
-        out = pl.ds(r - BASE, n)
-        total_x = total_y = 0.0
-        for k in range(LEVELS):
-            tr_y, (gy_t, gy_s) = north_flux(k, r, n, vel, mn, (t, s), (gt, gs))
-            u_next = u_out[k, out, :]
-            mask = me[k, here, :]
-            tr_x = (FLUX * mask) * (u_next + east(u_next))
-            md = (time_step * diffusivity) * mask
-            gx_t = tr_x * face[k, out, :] - md * slope[k, out, :]
-            gx_s = tr_x * face[LEVELS + k, out, :] - md * slope[LEVELS + k, out, :]
-            total_x, total_y = total_x + tr_x, total_y + tr_y
-            wet = w[k, here, :]
-            t_out[k, out, :] = wet * (t[k, here, :] - (gx_t - west(gx_t) + (gy_t - gt[k, down, :])))
-            s_out[k, out, :] = wet * (s[k, here, :] - (gx_s - west(gx_s) + (gy_s - gs[k, down, :])))
-        hy[here, :] = total_y
-        h_out[out, :] = e[here, :] - HEIGHT * (total_x - west(total_x) + (total_y - hy[down, :]))
-
     velocities(BASE - 8, 8, False)
     velocities(BASE + rows, 8, False)
-    velocities(BASE, rows, True)
+    for n in range(MAIN_BLOCKS):
+        velocities(BASE + n * (rows // MAIN_BLOCKS), rows // MAIN_BLOCKS, True)
+
+
+def new_tracers(t, s, w, e, face, slope, me, u_out, vel, mn, t_out, s_out, h_out, gt, gs, hy):
+    rows = h_out.shape[0]
     total = 0.0
     for k in range(LEVELS):
         total = total + north_flux(k, BASE - 8, 8, vel, mn, (t, s), (gt, gs))[0]
     hy[pl.ds(BASE - 8, 8), :] = total
-    block = rows // MAIN_BLOCKS
-    for n in range(MAIN_BLOCKS):
-        tracers(BASE + n * block, block)
-
-
-def interior_outputs(rows):
-    return [pltpu.VMEM((LEVELS, rows, LANES), F32)] * 4 + [pltpu.VMEM((rows, LANES), F32)]
-
-
-def interior_scratch(tall):
-    return [pltpu.VMEM((LEVELS, tall, LANES), F32)] * 5 + [pltpu.VMEM((tall, LANES), F32)]
+    here, down = pl.ds(BASE, rows), pl.ds(BASE - 1, rows)
+    total_x = total_y = 0.0
+    for k in range(LEVELS):
+        tr_y, (gy_t, gy_s) = north_flux(k, BASE, rows, vel, mn, (t, s), (gt, gs))
+        u_next = u_out[k]
+        mask = me[k]
+        tr_x = (FLUX * mask) * (u_next + east(u_next))
+        md = (time_step * diffusivity) * mask
+        gx_t = tr_x * face[k] - md * slope[k]
+        gx_s = tr_x * face[LEVELS + k] - md * slope[LEVELS + k]
+        total_x, total_y = total_x + tr_x, total_y + tr_y
+        wet = w[k, here, :]
+        t_out[k] = wet * (t[k, here, :] - (gx_t - west(gx_t) + (gy_t - gt[k, down, :])))
+        s_out[k] = wet * (s[k, here, :] - (gx_s - west(gx_s) + (gy_s - gs[k, down, :])))
+    hy[here, :] = total_y
+    h_out[...] = e[here, :] - HEIGHT * (total_x - west(total_x) + (total_y - hy[down, :]))
 
 
 def waits_for_seam():
-    return lax.axis_index("lon") == 0
+    return (lax.axis_index("lon") == 0) & (lax.axis_index("lat") < lax.axis_size("lat") - 1)
 
 
 def early_kernel(*refs):
-    ins, outs, scratch = refs[:9], refs[11:16], refs[16:]
+    ins, outs = refs[:6], refs[8:]
 
     @pl.when(waits_for_seam())
     def _():
-        interior(*ins, *outs, *scratch)
-
-
-def early(arrays, message):
-    rows, tall = arrays[-1].shape[1], arrays[0].shape[1]
+        new_velocities(*ins, *outs)
+
+
+def early(u, v, w, p, xu, xv, message):
+    wide, high = pltpu.VMEM(xu.shape, F32), pltpu.VMEM(u.shape, F32)
     return pl.pallas_call(
         early_kernel,
-        in_specs=[VMEM] * 10,
-        out_specs=[VMEM] * 6,
-        out_shape=[pltpu.VMEM(message.shape, F32)] + interior_outputs(rows),
-        scratch_shapes=interior_scratch(tall),
-        input_output_aliases={9: 0},
+        in_specs=[VMEM] * 7,
+        out_specs=[VMEM] * 5,
+        out_shape=[pltpu.VMEM(message.shape, F32), wide, wide, high, high],
+        input_output_aliases={6: 0},
         compiler_params=params(16),
         name="early",
-    )(*arrays, message)
+    )(u, v, w, p, xu, xv, message)
 
 
 def main_kernel(*refs):
-    ins, outs, scratch = refs[:9], refs[14:19], refs[19:]
+    (t, s, u, v, w, e, p, face, slope, xu, xv, me), outs, scratch = refs[:12], refs[16:23], refs[23:]
+    u_out, v_out, vel, mn, t_out, s_out, h_out = outs
 
     @pl.when(jnp.logical_not(waits_for_seam()))
     def _():
-        interior(*ins, *outs, *scratch)
-
-
-def main(arrays, outs):
+        new_velocities(u, v, w, p, xu, xv, u_out, v_out, vel, mn)
+
+    new_tracers(t, s, w, e, face, slope, me, u_out, vel, mn, t_out, s_out, h_out, *scratch)
+
+
+def main(arrays, velocities):
     rows, tall = arrays[-1].shape[1], arrays[0].shape[1]
+    wide, high = pltpu.VMEM((LEVELS, rows, LANES), F32), pltpu.VMEM((LEVELS, tall, LANES), F32)
     return pl.pallas_call(
         main_kernel,
-        in_specs=[VMEM] * 14,
-        out_specs=[VMEM] * 5,
-        out_shape=interior_outputs(rows),
-        scratch_shapes=interior_scratch(tall),
-        input_output_aliases={n + 9: n for n in range(5)},
+        in_specs=[VMEM] * 16,
+        out_specs=[VMEM] * 7,
+        out_shape=[wide, wide, high, high, wide, wide, pltpu.VMEM((rows, LANES), F32)],
+        scratch_shapes=[high, high, pltpu.VMEM((tall, LANES), F32)],
+        input_output_aliases={n + 12: n for n in range(4)},
         compiler_params=params(16),
         cost_estimate=pl.CostEstimate(flops=40_000_000, bytes_accessed=8_000_000, transcendentals=100_000),
         name="main",
-    )(*arrays, *outs)
+    )(*arrays, *velocities)
 
 
 def last_kernel(c_ref, m0_ref, m1_ref, place, mt, ms, mu, mv, mh, t_hbm, s_hbm, u_hbm, v_hbm, h_hbm,
@@ -693,14 +710,13 @@
     a, b = row_pack(fields, free_elevation)
     a = send(a, perm=lat_first)
     b = send(b, perm=lat_second)
-    *arrays, face, slope, place = column_pack(fields, free_elevation)
-    *arrays, c, m0, m1 = ghosts(a, b, arrays)
-    arrays += [face, slope]
+    *arrays, face, slope, xu, xv, me, place = column_pack(fields, free_elevation)
+    t, s, u, v, w, e, p, c, m0, m1 = ghosts(a, b, arrays)
     m0 = send(m0, perm=lon_first)
-    m1, *outs = early(arrays, m1)
+    m1, *velocities = early(u, v, w, p, xu, xv, m1)
     m1 = send(m1, perm=lon_second)
-    outs = main(arrays, outs)
-    return tuple(last(c, m0, m1, place, outs))
+    u_next, v_next, _, _, *tracers = main((t, s, u, v, w, e, p, face, slope, xu, xv, me), velocities)
+    return tuple(last(c, m0, m1, place, (*tracers[:2], u_next, v_next, tracers[2])))
 
 
 def solution(mesh):

time: 28.2 us -> 25.1 us (0.89)
  waiting for transfers between devices: 6.37 us -> 0.01 us
  starting transfers between devices: 9.64 us -> 12.7 us
  Pallas kernels: 11.3 us -> 11.6 us
    ppermute x1, waiting for transfers between devices: 6.37 us -> 0.01 us  [on_device(): m1 = send(m1, perm=lon_second)]
    ppermute x1, starting transfers between devices: 1.06 us -> 4.11 us  [on_device(): m1 = send(m1, perm=lon_second)]
    pallas_call x1, Pallas kernels: 2.37 us -> 3.12 us  [column_pack(): pl.pallas_call(column_pack_kernel, in_specs=[VMEM] * 6, out_specs=[VMEM]...]
    pallas_call x2, Pallas kernels: 3.79 us -> 3.41 us  [the longest x1 3.41 us: main(): pl.pallas_call(main_kernel, in_specs=[VMEM] * 16, out_specs=[VMEM] * 7, o...]
  transfers between devices with their start and end apart: 4 -> 4, of which waited for: 1 -> 0; matrix products, arithmetic and copies ran while one was open for 0% -> 0% of each run, Pallas kernels for 22% -> 26%
where the time goes in v7:
time: 25.1 us; the launch traced here: 25 us
  starting transfers between devices  12.7 us (51%)
  Pallas kernels  11.6 us (46%)
  between operations  0.76 us (3%)
    ppermute x1, starting transfers between devices, on_device(): b = send(b, perm=lat_second)  7.04 us
    ppermute x1, starting transfers between devices, on_device(): m1 = send(m1, perm=lon_second)  4.11 us
    pallas_call x1, Pallas kernels, last(): pl.pallas_call(last_kernel, in_specs=[VMEM] * 9, out_specs=[HBM] * 5, out...  3.48 us
    pallas_call x1, Pallas kernels, main(): pl.pallas_call(main_kernel, in_specs=[VMEM] * 16, out_specs=[VMEM] * 7, o...  3.41 us
    pallas_call x1, Pallas kernels, column_pack(): pl.pallas_call(column_pack_kernel, in_specs=[VMEM] * 6, out_specs=[VMEM]...  3.12 us
    pallas_call x1, Pallas kernels, row_pack(): pl.pallas_call(row_pack_kernel, in_specs=[HBM] * 6, out_specs=[VMEM] * 2,...  1.18 us
    ppermute x1, starting transfers between devices, on_device(): m0 = send(m0, perm=lon_first)  1 us
    ppermute x1, starting transfers between devices, on_device(): a = send(a, perm=lat_first)  0.54 us
  transfers between devices with their start and end apart: 4, of which 0 were waited for; matrix products, arithmetic and copies ran while one was open for 0% of the time, Pallas kernels for 26%

profile of v7, /device:TPU:14, one launch (start us, length us, event | category | flops | bytes accessed | tf_op | source)
XLA Modules:
  0.0 25.0 jit_solution(9640503895322458537)
XLA Ops:
  0.6 0.0 copy-start
  0.6 0.0 copy-start.1
  0.7 0.0 copy-start.2
  0.7 0.0 copy-start.3
  0.7 0.0 copy-start.4
  0.7 0.0 copy-start.5
  0.7 1.2 %row_pack.1 = (f32[88,128]{1,0:T(8,128)S(1)}, f32[88,128]{1,0:T(8,128)S(1)}) custom-call(f32[8,192,128]{2,1,0:T(8,128)} %t_in.1, f32[8,192,128]{2,1,0:T(8,128)} %s_in.1, f32[8,192,128]{2,1,0:T(8,128)} %u_in.1, f32[8,192,128]{2,1,0:T(8,128)} %v_in.1, s32[8,192,128]{2,1,0:T(8,128)} %w_in.1, f32[192,128]{1,0:T(8,128)} %e_in.1), custom_call_target="tpu_custom_call" | custom-call | tf_op jit(solution)/shard_map/row_pack/pallas_call | solution.py:139
  1.9 0.5 %collective-permute-start = (f32[88,128]{1,0:T(8,128)S(1)}, f32[88,128]{1,0:T(8,128)S(1)}, u32[]{:S(2)}, u32[]{:S(2)}) collective-permute-start(f32[88,128]{1,0:T(8,128)S(1)} %get-tuple-element.43), channel_id=1, source_target_pairs={{0,1},{1,0},{2,3},{3,2},{4,5},{5,4},{6,7},{7,6},{8,9},{9,8},{10,11... | collective-permute-start | bytes 135176 | tf_op jit(solution)/shard_map/ppermute | solution.py:711
  2.4 7.0 %collective-permute-start.1 = (f32[88,128]{1,0:T(8,128)S(1)}, f32[88,128]{1,0:T(8,128)S(1)}, u32[]{:S(2)}, u32[]{:S(2)}) collective-permute-start(f32[88,128]{1,0:T(8,128)S(1)} %get-tuple-element.44), channel_id=1, source_target_pairs={{0,8},{1,2},{2,1},{3,4},{4,3},{5,6},{6,5},{7,255},{8,0},{9,10},{10... | collective-permute-start | bytes 135176 | tf_op jit(solution)/shard_map/ppermute | solution.py:712
  9.5 0.0 copy-done
  9.5 0.0 copy-done.1
  9.5 0.0 copy-done.2
  9.5 0.0 copy-done.3
  9.5 0.0 copy-done.4
  9.5 0.0 copy-done.5
  9.5 3.1 %column_pack.1 = (f32[8,224,128]{2,1,0:T(8,128)S(1)}, f32[8,224,128]{2,1,0:T(8,128)S(1)}, f32[8,224,128]{2,1,0:T(8,128)S(1)}, f32[8,224,128]{2,1,0:T(8,128)S(1)}...) custom-call(f32[8,192,128]{2,1,0:T(8,128)S(1)} %copy-done, ...), custom_call_target="tpu_custom_call" | custom-call | flops 10000000 | bytes 6000000 | tf_op jit(solution)/shard_map/column_pack/pallas_call | solution.py:251
  12.6 0.0 collective-permute-done.a_ref
  12.6 0.0 collective-permute-done.1.b_ref
  12.6 0.4 %ghosts.1 = (f32[8,224,128]{2,1,0:T(8,128)S(1)}, f32[8,224,128]{2,1,0:T(8,128)S(1)}, f32[8,224,128]{2,1,0:T(8,128)S(1)}, f32[8,224,128]{2,1,0:T(8,128)S(1)}, f32...) custom-call(f32[88,128]{1,0:T(8,128)S(1)} %collective-permute-done.a, ...), custom_call_target="tpu_custom_call", output_to_operand_aliasing={{0}: (2, {}), {1}: (3, {}), {2}: (4, {}), {3}: (5, {}), {4}... | custom-call | tf_op jit(solution)/shard_map/ghosts/pallas_call | solution.py:319
  13.0 1.0 %collective-permute-start.2 = (f32[136,128]{1,0:T(8,128)S(1)}, f32[136,128]{1,0:T(8,128)S(1)}, u32[]{:S(2)}, u32[]{:S(2)}) collective-permute-start(f32[136,128]{1,0:T(8,128)S(1)} %get-tuple-element.56), channel_id=1, source_target_pairs={{0,8},{1,9},{2,10},{3,11},{4,12},{5,13},{6,14},{7,15},{8,0},{9,1},... | collective-permute-start | bytes 208904 | tf_op jit(solution)/shard_map/ppermute | solution.py:715
  14.0 4.1 %collective-permute-start.3 = (f32[136,128]{1,0:T(8,128)S(1)}, f32[136,128]{1,0:T(8,128)S(1)}, u32[]{:S(2)}, u32[]{:S(2)}) collective-permute-start(f32[136,128]{1,0:T(8,128)S(1)} %get-tuple-element.64), channel_id=1, source_target_pairs={{0,248},{1,249},{2,250},{3,251},{4,252},{5,253},{6,254},{7,255},{8... | collective-permute-start | bytes 208904 | tf_op jit(solution)/shard_map/ppermute | solution.py:717
  18.1 3.4 %main.1 = (f32[8,192,128]{2,1,0:T(8,128)S(1)}, f32[8,192,128]{2,1,0:T(8,128)S(1)}, f32[8,224,128]{2,1,0:T(8,128)S(1)}, f32[8,224,128]{2,1,0:T(8,128)S(1)}, f32[8...) custom-call(f32[8,224,128]{2,1,0:T(8,128)S(1)} %get-tuple-element.66, ...), custom_call_target="tpu_custom_call", output_to_operand_aliasing={{0}: (12, {}), {1}: (13, {}), {2}: (14, {}), {3}: (15, {})} | custom-call | flops 40000000 | bytes 8000000 | tf_op jit(solution)/shard_map/main/pallas_call | solution.py:521
  21.5 0.0 collective-permute-done.2.m0_ref
  21.5 0.0 collective-permute-done.3.m1_ref
  21.5 3.5 %last.1 = (f32[8,192,128]{2,1,0:T(8,128)}, f32[8,192,128]{2,1,0:T(8,128)}, f32[8,192,128]{2,1,0:T(8,128)}, f32[8,192,128]{2,1,0:T(8,128)}, f32[192,128]{1,0:T(8,128)}) custom-call(f32[6,200,128]{2,1,0:T(8,128)S(1)} %get-tuple-element.55.c_ref, f32[136,128]{1,0:T(8,128)S(1)} %collective-permute-done.2.m0_ref, f32[136,128]{1,0:T(8,128)S(1)} %collective-permute-done.3.m1_ref, ...), custom_call_target="tpu_custom_call" | custom-call | tf_op jit(solution)/shard_map/last/pallas_call | solution.py:660
  (1 shorter events, 0.0 us)
Async XLA Ops:
  0.6 8.8 %copy-start = (f32[8,192,128]{2,1,0:T(8,128)S(1)}, f32[8,192,128]{2,1,0:T(8,128)}, u32[]{:S(2)}) copy-start(f32[8,192,128]{2,1,0:T(8,128)} %t_in.1) | copy-start | bytes 2359300
  0.6 8.8 %copy-start.1 = (f32[8,192,128]{2,1,0:T(8,128)S(1)}, f32[8,192,128]{2,1,0:T(8,128)}, u32[]{:S(2)}) copy-start(f32[8,192,128]{2,1,0:T(8,128)} %s_in.1) | copy-start | bytes 2359300
  0.7 8.8 %copy-start.2 = (f32[8,192,128]{2,1,0:T(8,128)S(1)}, f32[8,192,128]{2,1,0:T(8,128)}, u32[]{:S(2)}) copy-start(f32[8,192,128]{2,1,0:T(8,128)} %u_in.1) | copy-start | bytes 2359300
  0.7 8.8 %copy-start.3 = (f32[8,192,128]{2,1,0:T(8,128)S(1)}, f32[8,192,128]{2,1,0:T(8,128)}, u32[]{:S(2)}) copy-start(f32[8,192,128]{2,1,0:T(8,128)} %v_in.1) | copy-start | bytes 2359300
  0.7 8.8 %copy-start.4 = (s32[8,192,128]{2,1,0:T(8,128)S(1)}, s32[8,192,128]{2,1,0:T(8,128)}, u32[]{:S(2)}) copy-start(s32[8,192,128]{2,1,0:T(8,128)} %w_in.1) | copy-start | bytes 2359300
  0.7 8.8 %copy-start.5 = (f32[192,128]{1,0:T(8,128)S(1)}, f32[192,128]{1,0:T(8,128)}, u32[]{:S(2)}) copy-start(f32[192,128]{1,0:T(8,128)} %e_in.1) | copy-start | bytes 294916
  1.9 10.7 %collective-permute-start = (f32[88,128]{1,0:T(8,128)S(1)}, f32[88,128]{1,0:T(8,128)S(1)}, u32[]{:S(2)}, u32[]{:S(2)}) collective-permute-start(f32[88,128]{1,0:T(8,128)S(1)} %get-tuple-element.43), channel_id=1, source_target_pairs={{0,1},{1,0},{2,3},{3,2},{4,5},{5,4},{6,7},{7,6},{8,9},{9,8},{10,11... | collective-permute-start | bytes 135176 | tf_op jit(solution)/shard_map/ppermute | solution.py:711
  2.4 10.2 %collective-permute-start.1 = (f32[88,128]{1,0:T(8,128)S(1)}, f32[88,128]{1,0:T(8,128)S(1)}, u32[]{:S(2)}, u32[]{:S(2)}) collective-permute-start(f32[88,128]{1,0:T(8,128)S(1)} %get-tuple-element.44), channel_id=1, source_target_pairs={{0,8},{1,2},{2,1},{3,4},{4,3},{5,6},{6,5},{7,255},{8,0},{9,10},{10... | collective-permute-start | bytes 135176 | tf_op jit(solution)/shard_map/ppermute | solution.py:712
  13.0 8.5 %collective-permute-start.2 = (f32[136,128]{1,0:T(8,128)S(1)}, f32[136,128]{1,0:T(8,128)S(1)}, u32[]{:S(2)}, u32[]{:S(2)}) collective-permute-start(f32[136,128]{1,0:T(8,128)S(1)} %get-tuple-element.56), channel_id=1, source_target_pairs={{0,8},{1,9},{2,10},{3,11},{4,12},{5,13},{6,14},{7,15},{8,0},{9,1},... | collective-permute-start | bytes 208904 | tf_op jit(solution)/shard_map/ppermute | solution.py:715
  14.0 7.5 %collective-permute-start.3 = (f32[136,128]{1,0:T(8,128)S(1)}, f32[136,128]{1,0:T(8,128)S(1)}, u32[]{:S(2)}, u32[]{:S(2)}) collective-permute-start(f32[136,128]{1,0:T(8,128)S(1)} %get-tuple-element.64), channel_id=1, source_target_pairs={{0,248},{1,249},{2,250},{3,251},{4,252},{5,253},{6,254},{7,255},{8... | collective-permute-start | bytes 208904 | tf_op jit(solution)/shard_map/ppermute | solution.py:717

commit v8 on v7

--- a/solution.py
+++ b/solution.py
@@ -591,12 +591,10 @@
 
     def placed(strip, levels=LEVELS):
         out = []
-        high, middle, low = split(strip)
+        high, middle, _ = split(strip)
         top = jnp.concatenate([high, middle], axis=1)
         for k in range(0, levels, 2):
-            at = slice(k * LANES, (k + 2) * LANES)
-            both = jnp.dot(low, place[:LANES, at], preferred_element_type=F32)
-            both = both + jnp.dot(top, place[:, at], preferred_element_type=F32)
+            both = jnp.dot(top, place[:, k * LANES : (k + 2) * LANES], preferred_element_type=F32)
             out += [both[:, :LANES], both[:, LANES:]]
         return out
 
@@ -635,8 +633,8 @@
             out[k] = jnp.where(edge, value, inner[k])
 
     merge(ou, un[0, whole, :], mu)
+    send(ou, u_hbm)
     merge(ov, vel[0, whole, :], mv)
-    send(ou, u_hbm)
     send(ov, v_hbm)
     strip_tracers(BASE, rows)
     merge(ot, st[...], mt)

time: 25.1 us -> 24.5 us (0.976)
  Pallas kernels: 11.6 us -> 11 us
    pallas_call x1, Pallas kernels: 3.48 us -> 2.89 us  [last(): pl.pallas_call(last_kernel, in_specs=[VMEM] * 9, out_specs=[HBM] * 5, out...]
  transfers between devices with their start and end apart: 4 -> 4, of which waited for: 0 -> 0; matrix products, arithmetic and copies ran while one was open for 0% -> 0% of each run, Pallas kernels for 26% -> 27%
where the time goes in v8:
time: 24.5 us; the launch traced here: 24.4 us
  starting transfers between devices  12.7 us (52%)
  Pallas kernels  11 us (45%)
  between operations  0.76 us (3%)
    ppermute x1, starting transfers between devices, on_device(): b = send(b, perm=lat_second)  7.04 us
    ppermute x1, starting transfers between devices, on_device(): m1 = send(m1, perm=lon_second)  4.11 us
    pallas_call x1, Pallas kernels, main(): pl.pallas_call(main_kernel, in_specs=[VMEM] * 16, out_specs=[VMEM] * 7, o...  3.41 us
    pallas_call x1, Pallas kernels, column_pack(): pl.pallas_call(column_pack_kernel, in_specs=[VMEM] * 6, out_specs=[VMEM]...  3.12 us
    pallas_call x1, Pallas kernels, last(): pl.pallas_call(last_kernel, in_specs=[VMEM] * 9, out_specs=[HBM] * 5, out...  2.89 us
    pallas_call x1, Pallas kernels, row_pack(): pl.pallas_call(row_pack_kernel, in_specs=[HBM] * 6, out_specs=[VMEM] * 2,...  1.18 us
    ppermute x1, starting transfers between devices, on_device(): m0 = send(m0, perm=lon_first)  1 us
    ppermute x1, starting transfers between devices, on_device(): a = send(a, perm=lat_first)  0.54 us
  transfers between devices with their start and end apart: 4, of which 0 were waited for; matrix products, arithmetic and copies ran while one was open for 0% of the time, Pallas kernels for 27%

profile of v8, /device:TPU:14, one launch (start us, length us, event | category | flops | bytes accessed | tf_op | source)
XLA Modules:
  0.0 24.4 jit_solution(579243618793661245)
XLA Ops:
  0.6 0.0 copy-start
  0.6 0.0 copy-start.1
  0.7 0.0 copy-start.2
  0.7 0.0 copy-start.3
  0.7 0.0 copy-start.4
  0.7 0.0 copy-start.5
  0.7 1.2 %row_pack.1 = (f32[88,128]{1,0:T(8,128)S(1)}, f32[88,128]{1,0:T(8,128)S(1)}) custom-call(f32[8,192,128]{2,1,0:T(8,128)} %t_in.1, f32[8,192,128]{2,1,0:T(8,128)} %s_in.1, f32[8,192,128]{2,1,0:T(8,128)} %u_in.1, f32[8,192,128]{2,1,0:T(8,128)} %v_in.1, s32[8,192,128]{2,1,0:T(8,128)} %w_in.1, f32[192,128]{1,0:T(8,128)} %e_in.1), custom_call_target="tpu_custom_call" | custom-call | tf_op jit(solution)/shard_map/row_pack/pallas_call | solution.py:139
  1.9 0.5 %collective-permute-start = (f32[88,128]{1,0:T(8,128)S(1)}, f32[88,128]{1,0:T(8,128)S(1)}, u32[]{:S(2)}, u32[]{:S(2)}) collective-permute-start(f32[88,128]{1,0:T(8,128)S(1)} %get-tuple-element.43), channel_id=1, source_target_pairs={{0,1},{1,0},{2,3},{3,2},{4,5},{5,4},{6,7},{7,6},{8,9},{9,8},{10,11... | collective-permute-start | bytes 135176 | tf_op jit(solution)/shard_map/ppermute | solution.py:709
  2.4 7.0 %collective-permute-start.1 = (f32[88,128]{1,0:T(8,128)S(1)}, f32[88,128]{1,0:T(8,128)S(1)}, u32[]{:S(2)}, u32[]{:S(2)}) collective-permute-start(f32[88,128]{1,0:T(8,128)S(1)} %get-tuple-element.44), channel_id=1, source_target_pairs={{0,8},{1,2},{2,1},{3,4},{4,3},{5,6},{6,5},{7,255},{8,0},{9,10},{10... | collective-permute-start | bytes 135176 | tf_op jit(solution)/shard_map/ppermute | solution.py:710
  9.5 0.0 copy-done
  9.5 0.0 copy-done.1
  9.5 0.0 copy-done.2
  9.5 0.0 copy-done.3
  9.5 0.0 copy-done.4
  9.5 0.0 copy-done.5
  9.5 3.1 %column_pack.1 = (f32[8,224,128]{2,1,0:T(8,128)S(1)}, f32[8,224,128]{2,1,0:T(8,128)S(1)}, f32[8,224,128]{2,1,0:T(8,128)S(1)}, f32[8,224,128]{2,1,0:T(8,128)S(1)}...) custom-call(f32[8,192,128]{2,1,0:T(8,128)S(1)} %copy-done, ...), custom_call_target="tpu_custom_call" | custom-call | flops 10000000 | bytes 6000000 | tf_op jit(solution)/shard_map/column_pack/pallas_call | solution.py:251
  12.6 0.0 collective-permute-done.a_ref
  12.6 0.0 collective-permute-done.1.b_ref
  12.6 0.4 %ghosts.1 = (f32[8,224,128]{2,1,0:T(8,128)S(1)}, f32[8,224,128]{2,1,0:T(8,128)S(1)}, f32[8,224,128]{2,1,0:T(8,128)S(1)}, f32[8,224,128]{2,1,0:T(8,128)S(1)}, f32...) custom-call(f32[88,128]{1,0:T(8,128)S(1)} %collective-permute-done.a, ...), custom_call_target="tpu_custom_call", output_to_operand_aliasing={{0}: (2, {}), {1}: (3, {}), {2}: (4, {}), {3}: (5, {}), {4}... | custom-call | tf_op jit(solution)/shard_map/ghosts/pallas_call | solution.py:319
  13.0 1.0 %collective-permute-start.2 = (f32[136,128]{1,0:T(8,128)S(1)}, f32[136,128]{1,0:T(8,128)S(1)}, u32[]{:S(2)}, u32[]{:S(2)}) collective-permute-start(f32[136,128]{1,0:T(8,128)S(1)} %get-tuple-element.56), channel_id=1, source_target_pairs={{0,8},{1,9},{2,10},{3,11},{4,12},{5,13},{6,14},{7,15},{8,0},{9,1},... | collective-permute-start | bytes 208904 | tf_op jit(solution)/shard_map/ppermute | solution.py:713
  14.0 4.1 %collective-permute-start.3 = (f32[136,128]{1,0:T(8,128)S(1)}, f32[136,128]{1,0:T(8,128)S(1)}, u32[]{:S(2)}, u32[]{:S(2)}) collective-permute-start(f32[136,128]{1,0:T(8,128)S(1)} %get-tuple-element.64), channel_id=1, source_target_pairs={{0,248},{1,249},{2,250},{3,251},{4,252},{5,253},{6,254},{7,255},{8... | collective-permute-start | bytes 208904 | tf_op jit(solution)/shard_map/ppermute | solution.py:715
  18.1 3.4 %main.1 = (f32[8,192,128]{2,1,0:T(8,128)S(1)}, f32[8,192,128]{2,1,0:T(8,128)S(1)}, f32[8,224,128]{2,1,0:T(8,128)S(1)}, f32[8,224,128]{2,1,0:T(8,128)S(1)}, f32[8...) custom-call(f32[8,224,128]{2,1,0:T(8,128)S(1)} %get-tuple-element.66, ...), custom_call_target="tpu_custom_call", output_to_operand_aliasing={{0}: (12, {}), {1}: (13, {}), {2}: (14, {}), {3}: (15, {})} | custom-call | flops 40000000 | bytes 8000000 | tf_op jit(solution)/shard_map/main/pallas_call | solution.py:521
  21.5 0.0 collective-permute-done.2.m0_ref
  21.5 0.0 collective-permute-done.3.m1_ref
  21.5 2.9 %last.1 = (f32[8,192,128]{2,1,0:T(8,128)}, f32[8,192,128]{2,1,0:T(8,128)}, f32[8,192,128]{2,1,0:T(8,128)}, f32[8,192,128]{2,1,0:T(8,128)}, f32[192,128]{1,0:T(8,128)}) custom-call(f32[6,200,128]{2,1,0:T(8,128)S(1)} %get-tuple-element.55.c_ref, f32[136,128]{1,0:T(8,128)S(1)} %collective-permute-done.2.m0_ref, f32[136,128]{1,0:T(8,128)S(1)} %collective-permute-done.3.m1_ref, ...), custom_call_target="tpu_custom_call" | custom-call | tf_op jit(solution)/shard_map/last/pallas_call | solution.py:658
  (1 shorter events, 0.0 us)
Async XLA Ops:
  0.6 8.8 %copy-start = (f32[8,192,128]{2,1,0:T(8,128)S(1)}, f32[8,192,128]{2,1,0:T(8,128)}, u32[]{:S(2)}) copy-start(f32[8,192,128]{2,1,0:T(8,128)} %t_in.1) | copy-start | bytes 2359300
  0.6 8.8 %copy-start.1 = (f32[8,192,128]{2,1,0:T(8,128)S(1)}, f32[8,192,128]{2,1,0:T(8,128)}, u32[]{:S(2)}) copy-start(f32[8,192,128]{2,1,0:T(8,128)} %s_in.1) | copy-start | bytes 2359300
  0.7 8.8 %copy-start.2 = (f32[8,192,128]{2,1,0:T(8,128)S(1)}, f32[8,192,128]{2,1,0:T(8,128)}, u32[]{:S(2)}) copy-start(f32[8,192,128]{2,1,0:T(8,128)} %u_in.1) | copy-start | bytes 2359300
  0.7 8.8 %copy-start.3 = (f32[8,192,128]{2,1,0:T(8,128)S(1)}, f32[8,192,128]{2,1,0:T(8,128)}, u32[]{:S(2)}) copy-start(f32[8,192,128]{2,1,0:T(8,128)} %v_in.1) | copy-start | bytes 2359300
  0.7 8.8 %copy-start.4 = (s32[8,192,128]{2,1,0:T(8,128)S(1)}, s32[8,192,128]{2,1,0:T(8,128)}, u32[]{:S(2)}) copy-start(s32[8,192,128]{2,1,0:T(8,128)} %w_in.1) | copy-start | bytes 2359300
  0.7 8.8 %copy-start.5 = (f32[192,128]{1,0:T(8,128)S(1)}, f32[192,128]{1,0:T(8,128)}, u32[]{:S(2)}) copy-start(f32[192,128]{1,0:T(8,128)} %e_in.1) | copy-start | bytes 294916
  1.9 10.7 %collective-permute-start = (f32[88,128]{1,0:T(8,128)S(1)}, f32[88,128]{1,0:T(8,128)S(1)}, u32[]{:S(2)}, u32[]{:S(2)}) collective-permute-start(f32[88,128]{1,0:T(8,128)S(1)} %get-tuple-element.43), channel_id=1, source_target_pairs={{0,1},{1,0},{2,3},{3,2},{4,5},{5,4},{6,7},{7,6},{8,9},{9,8},{10,11... | collective-permute-start | bytes 135176 | tf_op jit(solution)/shard_map/ppermute | solution.py:709
  2.4 10.2 %collective-permute-start.1 = (f32[88,128]{1,0:T(8,128)S(1)}, f32[88,128]{1,0:T(8,128)S(1)}, u32[]{:S(2)}, u32[]{:S(2)}) collective-permute-start(f32[88,128]{1,0:T(8,128)S(1)} %get-tuple-element.44), channel_id=1, source_target_pairs={{0,8},{1,2},{2,1},{3,4},{4,3},{5,6},{6,5},{7,255},{8,0},{9,10},{10... | collective-permute-start | bytes 135176 | tf_op jit(solution)/shard_map/ppermute | solution.py:710
  13.0 8.5 %collective-permute-start.2 = (f32[136,128]{1,0:T(8,128)S(1)}, f32[136,128]{1,0:T(8,128)S(1)}, u32[]{:S(2)}, u32[]{:S(2)}) collective-permute-start(f32[136,128]{1,0:T(8,128)S(1)} %get-tuple-element.56), channel_id=1, source_target_pairs={{0,8},{1,9},{2,10},{3,11},{4,12},{5,13},{6,14},{7,15},{8,0},{9,1},... | collective-permute-start | bytes 208904 | tf_op jit(solution)/shard_map/ppermute | solution.py:713
  14.0 7.5 %collective-permute-start.3 = (f32[136,128]{1,0:T(8,128)S(1)}, f32[136,128]{1,0:T(8,128)S(1)}, u32[]{:S(2)}, u32[]{:S(2)}) collective-permute-start(f32[136,128]{1,0:T(8,128)S(1)} %get-tuple-element.64), channel_id=1, source_target_pairs={{0,248},{1,249},{2,250},{3,251},{4,252},{5,253},{6,254},{7,255},{8... | collective-permute-start | bytes 208904 | tf_op jit(solution)/shard_map/ppermute | solution.py:715

commit v9 on v8

--- a/solution.py
+++ b/solution.py
@@ -19,6 +19,7 @@
 REST_ROWS = 32
 REST_LANES = 2 * LEVELS + 2
 MAIN_BLOCKS = 1
+TRACER_BLOCKS = 2
 
 time_step = 0.2
 viscosity = 0.5
@@ -461,22 +462,25 @@
     for k in range(LEVELS):
         total = total + north_flux(k, BASE - 8, 8, vel, mn, (t, s), (gt, gs))[0]
     hy[pl.ds(BASE - 8, 8), :] = total
-    here, down = pl.ds(BASE, rows), pl.ds(BASE - 1, rows)
-    total_x = total_y = 0.0
-    for k in range(LEVELS):
-        tr_y, (gy_t, gy_s) = north_flux(k, BASE, rows, vel, mn, (t, s), (gt, gs))
-        u_next = u_out[k]
-        mask = me[k]
-        tr_x = (FLUX * mask) * (u_next + east(u_next))
-        md = (time_step * diffusivity) * mask
-        gx_t = tr_x * face[k] - md * slope[k]
-        gx_s = tr_x * face[LEVELS + k] - md * slope[LEVELS + k]
-        total_x, total_y = total_x + tr_x, total_y + tr_y
-        wet = w[k, here, :]
-        t_out[k] = wet * (t[k, here, :] - (gx_t - west(gx_t) + (gy_t - gt[k, down, :])))
-        s_out[k] = wet * (s[k, here, :] - (gx_s - west(gx_s) + (gy_s - gs[k, down, :])))
-    hy[here, :] = total_y
-    h_out[...] = e[here, :] - HEIGHT * (total_x - west(total_x) + (total_y - hy[down, :]))
+    n = rows // TRACER_BLOCKS
+    for first in range(0, rows, n):
+        r, out = BASE + first, pl.ds(first, n)
+        here, down = pl.ds(r, n), pl.ds(r - 1, n)
+        total_x = total_y = 0.0
+        for k in range(LEVELS):
+            tr_y, (gy_t, gy_s) = north_flux(k, r, n, vel, mn, (t, s), (gt, gs))
+            u_next = u_out[k, out, :]
+            mask = me[k, out, :]
+            tr_x = (FLUX * mask) * (u_next + east(u_next))
+            md = (time_step * diffusivity) * mask
+            gx_t = tr_x * face[k, out, :] - md * slope[k, out, :]
+            gx_s = tr_x * face[LEVELS + k, out, :] - md * slope[LEVELS + k, out, :]
+            total_x, total_y = total_x + tr_x, total_y + tr_y
+            wet = w[k, here, :]
+            t_out[k, out, :] = wet * (t[k, here, :] - (gx_t - west(gx_t) + (gy_t - gt[k, down, :])))
+            s_out[k, out, :] = wet * (s[k, here, :] - (gx_s - west(gx_s) + (gy_s - gs[k, down, :])))
+        hy[here, :] = total_y
+        h_out[out, :] = e[here, :] - HEIGHT * (total_x - west(total_x) + (total_y - hy[down, :]))
 
 
 def waits_for_seam():

time: 24.5 us -> 24.5 us (level)
  no operation moved by 1% of the time
where the time goes in v9:
time: 24.5 us
  starting transfers between devices  12.7 us (52%)
  Pallas kernels  11 us (45%)
  between operations  0.76 us (3%)
    ppermute x1, starting transfers between devices, on_device(): b = send(b, perm=lat_second)  7.04 us
    ppermute x1, starting transfers between devices, on_device(): m1 = send(m1, perm=lon_second)  4.11 us
    pallas_call x1, Pallas kernels, main(): pl.pallas_call(main_kernel, in_specs=[VMEM] * 16, out_specs=[VMEM] * 7, o...  3.43 us
    pallas_call x1, Pallas kernels, column_pack(): pl.pallas_call(column_pack_kernel, in_specs=[VMEM] * 6, out_specs=[VMEM]...  3.12 us
    pallas_call x1, Pallas kernels, last(): pl.pallas_call(last_kernel, in_specs=[VMEM] * 9, out_specs=[HBM] * 5, out...  2.89 us
    pallas_call x1, Pallas kernels, row_pack(): pl.pallas_call(row_pack_kernel, in_specs=[HBM] * 6, out_specs=[VMEM] * 2,...  1.18 us
    ppermute x1, starting transfers between devices, on_device(): m0 = send(m0, perm=lon_first)  1 us
    ppermute x1, starting transfers between devices, on_device(): a = send(a, perm=lat_first)  0.54 us
  transfers between devices with their start and end apart: 4, of which 0 were waited for; matrix products, arithmetic and copies ran while one was open for 0% of the time, Pallas kernels for 27%

profile of v9, /device:TPU:14, one launch (start us, length us, event | category | flops | bytes accessed | tf_op | source)
XLA Modules:
  0.0 24.5 jit_solution(5490219971450476913)
XLA Ops:
  0.6 0.0 copy-start
  0.6 0.0 copy-start.1
  0.7 0.0 copy-start.2
  0.7 0.0 copy-start.3
  0.7 0.0 copy-start.4
  0.7 0.0 copy-start.5
  0.7 1.2 %row_pack.1 = (f32[88,128]{1,0:T(8,128)S(1)}, f32[88,128]{1,0:T(8,128)S(1)}) custom-call(f32[8,192,128]{2,1,0:T(8,128)} %t_in.1, f32[8,192,128]{2,1,0:T(8,128)} %s_in.1, f32[8,192,128]{2,1,0:T(8,128)} %u_in.1, f32[8,192,128]{2,1,0:T(8,128)} %v_in.1, s32[8,192,128]{2,1,0:T(8,128)} %w_in.1, f32[192,128]{1,0:T(8,128)} %e_in.1), custom_call_target="tpu_custom_call" | custom-call | tf_op jit(solution)/shard_map/row_pack/pallas_call | solution.py:140
  1.9 0.5 %collective-permute-start = (f32[88,128]{1,0:T(8,128)S(1)}, f32[88,128]{1,0:T(8,128)S(1)}, u32[]{:S(2)}, u32[]{:S(2)}) collective-permute-start(f32[88,128]{1,0:T(8,128)S(1)} %get-tuple-element.43), channel_id=1, source_target_pairs={{0,1},{1,0},{2,3},{3,2},{4,5},{5,4},{6,7},{7,6},{8,9},{9,8},{10,11... | collective-permute-start | bytes 135176 | tf_op jit(solution)/shard_map/ppermute | solution.py:713
  2.4 7.0 %collective-permute-start.1 = (f32[88,128]{1,0:T(8,128)S(1)}, f32[88,128]{1,0:T(8,128)S(1)}, u32[]{:S(2)}, u32[]{:S(2)}) collective-permute-start(f32[88,128]{1,0:T(8,128)S(1)} %get-tuple-element.44), channel_id=1, source_target_pairs={{0,8},{1,2},{2,1},{3,4},{4,3},{5,6},{6,5},{7,255},{8,0},{9,10},{10... | collective-permute-start | bytes 135176 | tf_op jit(solution)/shard_map/ppermute | solution.py:714
  9.5 0.0 copy-done
  9.5 0.0 copy-done.1
  9.5 0.0 copy-done.2
  9.5 0.0 copy-done.3
  9.5 0.0 copy-done.4
  9.5 0.0 copy-done.5
  9.5 3.1 %column_pack.1 = (f32[8,224,128]{2,1,0:T(8,128)S(1)}, f32[8,224,128]{2,1,0:T(8,128)S(1)}, f32[8,224,128]{2,1,0:T(8,128)S(1)}, f32[8,224,128]{2,1,0:T(8,128)S(1)}...) custom-call(f32[8,192,128]{2,1,0:T(8,128)S(1)} %copy-done, ...), custom_call_target="tpu_custom_call" | custom-call | flops 10000000 | bytes 6000000 | tf_op jit(solution)/shard_map/column_pack/pallas_call | solution.py:252
  12.6 0.0 collective-permute-done.a_ref
  12.6 0.0 collective-permute-done.1.b_ref
  12.6 0.4 %ghosts.1 = (f32[8,224,128]{2,1,0:T(8,128)S(1)}, f32[8,224,128]{2,1,0:T(8,128)S(1)}, f32[8,224,128]{2,1,0:T(8,128)S(1)}, f32[8,224,128]{2,1,0:T(8,128)S(1)}, f32...) custom-call(f32[88,128]{1,0:T(8,128)S(1)} %collective-permute-done.a, ...), custom_call_target="tpu_custom_call", output_to_operand_aliasing={{0}: (2, {}), {1}: (3, {}), {2}: (4, {}), {3}: (5, {}), {4}... | custom-call | tf_op jit(solution)/shard_map/ghosts/pallas_call | solution.py:320
  13.0 1.0 %collective-permute-start.2 = (f32[136,128]{1,0:T(8,128)S(1)}, f32[136,128]{1,0:T(8,128)S(1)}, u32[]{:S(2)}, u32[]{:S(2)}) collective-permute-start(f32[136,128]{1,0:T(8,128)S(1)} %get-tuple-element.56), channel_id=1, source_target_pairs={{0,8},{1,9},{2,10},{3,11},{4,12},{5,13},{6,14},{7,15},{8,0},{9,1},... | collective-permute-start | bytes 208904 | tf_op jit(solution)/shard_map/ppermute | solution.py:717
  14.0 4.1 %collective-permute-start.3 = (f32[136,128]{1,0:T(8,128)S(1)}, f32[136,128]{1,0:T(8,128)S(1)}, u32[]{:S(2)}, u32[]{:S(2)}) collective-permute-start(f32[136,128]{1,0:T(8,128)S(1)} %get-tuple-element.64), channel_id=1, source_target_pairs={{0,248},{1,249},{2,250},{3,251},{4,252},{5,253},{6,254},{7,255},{8... | collective-permute-start | bytes 208904 | tf_op jit(solution)/shard_map/ppermute | solution.py:719
  18.1 3.4 %main.1 = (f32[8,192,128]{2,1,0:T(8,128)S(1)}, f32[8,192,128]{2,1,0:T(8,128)S(1)}, f32[8,224,128]{2,1,0:T(8,128)S(1)}, f32[8,224,128]{2,1,0:T(8,128)S(1)}, f32[8...) custom-call(f32[8,224,128]{2,1,0:T(8,128)S(1)} %get-tuple-element.66, ...), custom_call_target="tpu_custom_call", output_to_operand_aliasing={{0}: (12, {}), {1}: (13, {}), {2}: (14, {}), {3}: (15, {})} | custom-call | flops 40000000 | bytes 8000000 | tf_op jit(solution)/shard_map/main/pallas_call | solution.py:525
  21.5 0.0 collective-permute-done.2.m0_ref
  21.6 0.0 collective-permute-done.3.m1_ref
  21.6 2.9 %last.1 = (f32[8,192,128]{2,1,0:T(8,128)}, f32[8,192,128]{2,1,0:T(8,128)}, f32[8,192,128]{2,1,0:T(8,128)}, f32[8,192,128]{2,1,0:T(8,128)}, f32[192,128]{1,0:T(8,128)}) custom-call(f32[6,200,128]{2,1,0:T(8,128)S(1)} %get-tuple-element.55.c_ref, f32[136,128]{1,0:T(8,128)S(1)} %collective-permute-done.2.m0_ref, f32[136,128]{1,0:T(8,128)S(1)} %collective-permute-done.3.m1_ref, ...), custom_call_target="tpu_custom_call" | custom-call | tf_op jit(solution)/shard_map/last/pallas_call | solution.py:662
  (1 shorter events, 0.0 us)
Async XLA Ops:
  0.6 8.8 %copy-start = (f32[8,192,128]{2,1,0:T(8,128)S(1)}, f32[8,192,128]{2,1,0:T(8,128)}, u32[]{:S(2)}) copy-start(f32[8,192,128]{2,1,0:T(8,128)} %t_in.1) | copy-start | bytes 2359300
  0.6 8.8 %copy-start.1 = (f32[8,192,128]{2,1,0:T(8,128)S(1)}, f32[8,192,128]{2,1,0:T(8,128)}, u32[]{:S(2)}) copy-start(f32[8,192,128]{2,1,0:T(8,128)} %s_in.1) | copy-start | bytes 2359300
  0.7 8.8 %copy-start.2 = (f32[8,192,128]{2,1,0:T(8,128)S(1)}, f32[8,192,128]{2,1,0:T(8,128)}, u32[]{:S(2)}) copy-start(f32[8,192,128]{2,1,0:T(8,128)} %u_in.1) | copy-start | bytes 2359300
  0.7 8.8 %copy-start.3 = (f32[8,192,128]{2,1,0:T(8,128)S(1)}, f32[8,192,128]{2,1,0:T(8,128)}, u32[]{:S(2)}) copy-start(f32[8,192,128]{2,1,0:T(8,128)} %v_in.1) | copy-start | bytes 2359300
  0.7 8.8 %copy-start.4 = (s32[8,192,128]{2,1,0:T(8,128)S(1)}, s32[8,192,128]{2,1,0:T(8,128)}, u32[]{:S(2)}) copy-start(s32[8,192,128]{2,1,0:T(8,128)} %w_in.1) | copy-start | bytes 2359300
  0.7 8.8 %copy-start.5 = (f32[192,128]{1,0:T(8,128)S(1)}, f32[192,128]{1,0:T(8,128)}, u32[]{:S(2)}) copy-start(f32[192,128]{1,0:T(8,128)} %e_in.1) | copy-start | bytes 294916
  1.9 10.7 %collective-permute-start = (f32[88,128]{1,0:T(8,128)S(1)}, f32[88,128]{1,0:T(8,128)S(1)}, u32[]{:S(2)}, u32[]{:S(2)}) collective-permute-start(f32[88,128]{1,0:T(8,128)S(1)} %get-tuple-element.43), channel_id=1, source_target_pairs={{0,1},{1,0},{2,3},{3,2},{4,5},{5,4},{6,7},{7,6},{8,9},{9,8},{10,11... | collective-permute-start | bytes 135176 | tf_op jit(solution)/shard_map/ppermute | solution.py:713
  2.4 10.2 %collective-permute-start.1 = (f32[88,128]{1,0:T(8,128)S(1)}, f32[88,128]{1,0:T(8,128)S(1)}, u32[]{:S(2)}, u32[]{:S(2)}) collective-permute-start(f32[88,128]{1,0:T(8,128)S(1)} %get-tuple-element.44), channel_id=1, source_target_pairs={{0,8},{1,2},{2,1},{3,4},{4,3},{5,6},{6,5},{7,255},{8,0},{9,10},{10... | collective-permute-start | bytes 135176 | tf_op jit(solution)/shard_map/ppermute | solution.py:714
  13.0 8.5 %collective-permute-start.2 = (f32[136,128]{1,0:T(8,128)S(1)}, f32[136,128]{1,0:T(8,128)S(1)}, u32[]{:S(2)}, u32[]{:S(2)}) collective-permute-start(f32[136,128]{1,0:T(8,128)S(1)} %get-tuple-element.56), channel_id=1, source_target_pairs={{0,8},{1,9},{2,10},{3,11},{4,12},{5,13},{6,14},{7,15},{8,0},{9,1},... | collective-permute-start | bytes 208904 | tf_op jit(solution)/shard_map/ppermute | solution.py:717
  14.0 7.6 %collective-permute-start.3 = (f32[136,128]{1,0:T(8,128)S(1)}, f32[136,128]{1,0:T(8,128)S(1)}, u32[]{:S(2)}, u32[]{:S(2)}) collective-permute-start(f32[136,128]{1,0:T(8,128)S(1)} %get-tuple-element.64), channel_id=1, source_target_pairs={{0,248},{1,249},{2,250},{3,251},{4,252},{5,253},{6,254},{7,255},{8... | collective-permute-start | bytes 208904 | tf_op jit(solution)/shard_map/ppermute | solution.py:719

commit v10 on v8

--- a/solution.py
+++ b/solution.py
@@ -641,8 +641,12 @@
     send(ot, t_hbm)
     oh[...] = jnp.where(on_edge(rows), placed(sh[...], 2)[0], mh[...])
     send(oh, h_hbm)
-    merge(os, ss[...], ms)
-    send(os, s_hbm)
+    edge = on_edge(rows)
+    for k, value in enumerate(placed(ss[...])):
+        os[k] = jnp.where(edge, value, ms[k])
+        if k % (LEVELS // 2) == LEVELS // 2 - 1:
+            half = pl.ds(k + 1 - LEVELS // 2, LEVELS // 2)
+            send(os.at[half], s_hbm.at[half])
     for x in copies:
         x.wait()
 
@@ -666,7 +670,7 @@
         + [flat]
         + [short] * 3
         + [wide] * 4
-        + [short, pltpu.SemaphoreType.DMA((5,))],
+        + [short, pltpu.SemaphoreType.DMA((6,))],
         compiler_params=params(24),
         name="last",
     )(c, m0, m1, place, *outs)

time: 24.5 us -> 24.6 us (level)
  no operation moved by 1% of the time
where the time goes in v10:
time: 24.6 us
  starting transfers between devices  12.7 us (52%)
  Pallas kernels  11.1 us (45%)
  between operations  0.76 us (3%)
    ppermute x1, starting transfers between devices, on_device(): b = send(b, perm=lat_second)  7.04 us
    ppermute x1, starting transfers between devices, on_device(): m1 = send(m1, perm=lon_second)  4.11 us
    pallas_call x1, Pallas kernels, main(): pl.pallas_call(main_kernel, in_specs=[VMEM] * 16, out_specs=[VMEM] * 7, o...  3.41 us
    pallas_call x1, Pallas kernels, column_pack(): pl.pallas_call(column_pack_kernel, in_specs=[VMEM] * 6, out_specs=[VMEM]...  3.12 us
    pallas_call x1, Pallas kernels, last(): pl.pallas_call(last_kernel, in_specs=[VMEM] * 9, out_specs=[HBM] * 5, out...  3.01 us
    pallas_call x1, Pallas kernels, row_pack(): pl.pallas_call(row_pack_kernel, in_specs=[HBM] * 6, out_specs=[VMEM] * 2,...  1.18 us
    ppermute x1, starting transfers between devices, on_device(): m0 = send(m0, perm=lon_first)  1 us
    ppermute x1, starting transfers between devices, on_device(): a = send(a, perm=lat_first)  0.54 us
  transfers between devices with their start and end apart: 4, of which 0 were waited for; matrix products, arithmetic and copies ran while one was open for 0% of the time, Pallas kernels for 27%

profile of v10, /device:TPU:14, one launch (start us, length us, event | category | flops | bytes accessed | tf_op | source)
XLA Modules:
  0.0 24.6 jit_solution(14925733608372230283)
XLA Ops:
  0.6 0.0 copy-start
  0.6 0.0 copy-start.1
  0.7 0.0 copy-start.2
  0.7 0.0 copy-start.3
  0.7 0.0 copy-start.4
  0.7 0.0 copy-start.5
  0.7 1.2 %row_pack.1 = (f32[88,128]{1,0:T(8,128)S(1)}, f32[88,128]{1,0:T(8,128)S(1)}) custom-call(f32[8,192,128]{2,1,0:T(8,128)} %t_in.1, f32[8,192,128]{2,1,0:T(8,128)} %s_in.1, f32[8,192,128]{2,1,0:T(8,128)} %u_in.1, f32[8,192,128]{2,1,0:T(8,128)} %v_in.1, s32[8,192,128]{2,1,0:T(8,128)} %w_in.1, f32[192,128]{1,0:T(8,128)} %e_in.1), custom_call_target="tpu_custom_call" | custom-call | tf_op jit(solution)/shard_map/row_pack/pallas_call | solution.py:139
  1.9 0.5 %collective-permute-start = (f32[88,128]{1,0:T(8,128)S(1)}, f32[88,128]{1,0:T(8,128)S(1)}, u32[]{:S(2)}, u32[]{:S(2)}) collective-permute-start(f32[88,128]{1,0:T(8,128)S(1)} %get-tuple-element.43), channel_id=1, source_target_pairs={{0,1},{1,0},{2,3},{3,2},{4,5},{5,4},{6,7},{7,6},{8,9},{9,8},{10,11... | collective-permute-start | bytes 135176 | tf_op jit(solution)/shard_map/ppermute | solution.py:713
  2.4 7.0 %collective-permute-start.1 = (f32[88,128]{1,0:T(8,128)S(1)}, f32[88,128]{1,0:T(8,128)S(1)}, u32[]{:S(2)}, u32[]{:S(2)}) collective-permute-start(f32[88,128]{1,0:T(8,128)S(1)} %get-tuple-element.44), channel_id=1, source_target_pairs={{0,8},{1,2},{2,1},{3,4},{4,3},{5,6},{6,5},{7,255},{8,0},{9,10},{10... | collective-permute-start | bytes 135176 | tf_op jit(solution)/shard_map/ppermute | solution.py:714
  9.5 0.0 copy-done
  9.5 0.0 copy-done.1
  9.5 0.0 copy-done.2
  9.5 0.0 copy-done.3
  9.5 0.0 copy-done.4
  9.5 0.0 copy-done.5
  9.5 3.1 %column_pack.1 = (f32[8,224,128]{2,1,0:T(8,128)S(1)}, f32[8,224,128]{2,1,0:T(8,128)S(1)}, f32[8,224,128]{2,1,0:T(8,128)S(1)}, f32[8,224,128]{2,1,0:T(8,128)S(1)}...) custom-call(f32[8,192,128]{2,1,0:T(8,128)S(1)} %copy-done, ...), custom_call_target="tpu_custom_call" | custom-call | flops 10000000 | bytes 6000000 | tf_op jit(solution)/shard_map/column_pack/pallas_call | solution.py:251
  12.6 0.0 collective-permute-done.a_ref
  12.6 0.0 collective-permute-done.1.b_ref
  12.6 0.4 %ghosts.1 = (f32[8,224,128]{2,1,0:T(8,128)S(1)}, f32[8,224,128]{2,1,0:T(8,128)S(1)}, f32[8,224,128]{2,1,0:T(8,128)S(1)}, f32[8,224,128]{2,1,0:T(8,128)S(1)}, f32...) custom-call(f32[88,128]{1,0:T(8,128)S(1)} %collective-permute-done.a, ...), custom_call_target="tpu_custom_call", output_to_operand_aliasing={{0}: (2, {}), {1}: (3, {}), {2}: (4, {}), {3}: (5, {}), {4}... | custom-call | tf_op jit(solution)/shard_map/ghosts/pallas_call | solution.py:319
  13.0 1.0 %collective-permute-start.2 = (f32[136,128]{1,0:T(8,128)S(1)}, f32[136,128]{1,0:T(8,128)S(1)}, u32[]{:S(2)}, u32[]{:S(2)}) collective-permute-start(f32[136,128]{1,0:T(8,128)S(1)} %get-tuple-element.56), channel_id=1, source_target_pairs={{0,8},{1,9},{2,10},{3,11},{4,12},{5,13},{6,14},{7,15},{8,0},{9,1},... | collective-permute-start | bytes 208904 | tf_op jit(solution)/shard_map/ppermute | solution.py:717
  14.0 4.1 %collective-permute-start.3 = (f32[136,128]{1,0:T(8,128)S(1)}, f32[136,128]{1,0:T(8,128)S(1)}, u32[]{:S(2)}, u32[]{:S(2)}) collective-permute-start(f32[136,128]{1,0:T(8,128)S(1)} %get-tuple-element.64), channel_id=1, source_target_pairs={{0,248},{1,249},{2,250},{3,251},{4,252},{5,253},{6,254},{7,255},{8... | collective-permute-start | bytes 208904 | tf_op jit(solution)/shard_map/ppermute | solution.py:719
  18.1 3.4 %main.1 = (f32[8,192,128]{2,1,0:T(8,128)S(1)}, f32[8,192,128]{2,1,0:T(8,128)S(1)}, f32[8,224,128]{2,1,0:T(8,128)S(1)}, f32[8,224,128]{2,1,0:T(8,128)S(1)}, f32[8...) custom-call(f32[8,224,128]{2,1,0:T(8,128)S(1)} %get-tuple-element.66, ...), custom_call_target="tpu_custom_call", output_to_operand_aliasing={{0}: (12, {}), {1}: (13, {}), {2}: (14, {}), {3}: (15, {})} | custom-call | flops 40000000 | bytes 8000000 | tf_op jit(solution)/shard_map/main/pallas_call | solution.py:521
  21.5 0.0 collective-permute-done.2.m0_ref
  21.5 0.0 collective-permute-done.3.m1_ref
  21.5 3.0 %last.1 = (f32[8,192,128]{2,1,0:T(8,128)}, f32[8,192,128]{2,1,0:T(8,128)}, f32[8,192,128]{2,1,0:T(8,128)}, f32[8,192,128]{2,1,0:T(8,128)}, f32[192,128]{1,0:T(8,128)}) custom-call(f32[6,200,128]{2,1,0:T(8,128)S(1)} %get-tuple-element.55.c_ref, f32[136,128]{1,0:T(8,128)S(1)} %collective-permute-done.2.m0_ref, f32[136,128]{1,0:T(8,128)S(1)} %collective-permute-done.3.m1_ref, ...), custom_call_target="tpu_custom_call" | custom-call | tf_op jit(solution)/shard_map/last/pallas_call | solution.py:662
  (1 shorter events, 0.0 us)
Async XLA Ops:
  0.6 8.8 %copy-start = (f32[8,192,128]{2,1,0:T(8,128)S(1)}, f32[8,192,128]{2,1,0:T(8,128)}, u32[]{:S(2)}) copy-start(f32[8,192,128]{2,1,0:T(8,128)} %t_in.1) | copy-start | bytes 2359300
  0.6 8.8 %copy-start.1 = (f32[8,192,128]{2,1,0:T(8,128)S(1)}, f32[8,192,128]{2,1,0:T(8,128)}, u32[]{:S(2)}) copy-start(f32[8,192,128]{2,1,0:T(8,128)} %s_in.1) | copy-start | bytes 2359300
  0.7 8.8 %copy-start.2 = (f32[8,192,128]{2,1,0:T(8,128)S(1)}, f32[8,192,128]{2,1,0:T(8,128)}, u32[]{:S(2)}) copy-start(f32[8,192,128]{2,1,0:T(8,128)} %u_in.1) | copy-start | bytes 2359300
  0.7 8.8 %copy-start.3 = (f32[8,192,128]{2,1,0:T(8,128)S(1)}, f32[8,192,128]{2,1,0:T(8,128)}, u32[]{:S(2)}) copy-start(f32[8,192,128]{2,1,0:T(8,128)} %v_in.1) | copy-start | bytes 2359300
  0.7 8.8 %copy-start.4 = (s32[8,192,128]{2,1,0:T(8,128)S(1)}, s32[8,192,128]{2,1,0:T(8,128)}, u32[]{:S(2)}) copy-start(s32[8,192,128]{2,1,0:T(8,128)} %w_in.1) | copy-start | bytes 2359300
  0.7 8.8 %copy-start.5 = (f32[192,128]{1,0:T(8,128)S(1)}, f32[192,128]{1,0:T(8,128)}, u32[]{:S(2)}) copy-start(f32[192,128]{1,0:T(8,128)} %e_in.1) | copy-start | bytes 294916
  1.9 10.7 %collective-permute-start = (f32[88,128]{1,0:T(8,128)S(1)}, f32[88,128]{1,0:T(8,128)S(1)}, u32[]{:S(2)}, u32[]{:S(2)}) collective-permute-start(f32[88,128]{1,0:T(8,128)S(1)} %get-tuple-element.43), channel_id=1, source_target_pairs={{0,1},{1,0},{2,3},{3,2},{4,5},{5,4},{6,7},{7,6},{8,9},{9,8},{10,11... | collective-permute-start | bytes 135176 | tf_op jit(solution)/shard_map/ppermute | solution.py:713
  2.4 10.2 %collective-permute-start.1 = (f32[88,128]{1,0:T(8,128)S(1)}, f32[88,128]{1,0:T(8,128)S(1)}, u32[]{:S(2)}, u32[]{:S(2)}) collective-permute-start(f32[88,128]{1,0:T(8,128)S(1)} %get-tuple-element.44), channel_id=1, source_target_pairs={{0,8},{1,2},{2,1},{3,4},{4,3},{5,6},{6,5},{7,255},{8,0},{9,10},{10... | collective-permute-start | bytes 135176 | tf_op jit(solution)/shard_map/ppermute | solution.py:714
  13.0 8.5 %collective-permute-start.2 = (f32[136,128]{1,0:T(8,128)S(1)}, f32[136,128]{1,0:T(8,128)S(1)}, u32[]{:S(2)}, u32[]{:S(2)}) collective-permute-start(f32[136,128]{1,0:T(8,128)S(1)} %get-tuple-element.56), channel_id=1, source_target_pairs={{0,8},{1,9},{2,10},{3,11},{4,12},{5,13},{6,14},{7,15},{8,0},{9,1},... | collective-permute-start | bytes 208904 | tf_op jit(solution)/shard_map/ppermute | solution.py:717
  14.0 7.5 %collective-permute-start.3 = (f32[136,128]{1,0:T(8,128)S(1)}, f32[136,128]{1,0:T(8,128)S(1)}, u32[]{:S(2)}, u32[]{:S(2)}) collective-permute-start(f32[136,128]{1,0:T(8,128)S(1)} %get-tuple-element.64), channel_id=1, source_target_pairs={{0,248},{1,249},{2,250},{3,251},{4,252},{5,253},{6,254},{7,255},{8... | collective-permute-start | bytes 208904 | tf_op jit(solution)/shard_map/ppermute | solution.py:719
